TPU v7x, 512 devices: a whole 4x8x8 slice. The times are simulated.
512 devices in a mesh: blk: 16 (over z_hi, y), grp: 32 (over x, z_lo, core).
Axes of the slice: x: 4, y: 8, z: 8 (z_hi: 2, z_lo: 4; z = z_hi * 4 + z_lo), core: 2. Of those that a mesh axis runs over, the one named last changes fastest.
Arguments:
- matrix: bfloat16 [8192, 8192], P('blk', 'grp'), as said below
- in_pattern: int32 [64, 64], P('blk', 'grp'), may hold values from 0 to 1, as said below
- out_pattern: int32 [64, 64], P('blk', 'grp'), may hold values from 0 to 1, as said below
Outputs:
- pruned: bfloat16 [8192, 8192], P('blk', 'grp')
Inputs may be any that keep to these rules, and one draw needn't show every extreme that they name: `matrix`: entries are positive. `in_pattern`: every diagonal tile is present. In the 4 x 2 block of tiles of rows [b * 4, (b + 1) * 4) and columns [g * 2, (g + 1) * 2), for every b and g, at most 4 tiles are present, and some such block holds exactly 4. `out_pattern`: every diagonal tile is kept.
All inputs are finite; a program needn't handle non-finite values.
Results may differ from a plain program's by a relative error of at most 0.001.
Values may be sent and summed in bfloat16 or wider, within the bound.
No kernel may reach another device: no remote copies, remote signals or barrier semaphores. Data moves between devices by JAX's collectives and lax.ppermute only.
A program may use at most 64 MiB of HBM per device.

v0:
```python
import jax
import jax.numpy as jnp
from jax import lax
from jax.sharding import PartitionSpec as P

prune_level = 0.5


def shifted(array, axis, by):
    peers = lax.axis_size(axis)
    return lax.ppermute(array, axis, [(i, (i + by) % peers) for i in range(peers)])


def apply_mask(values, pattern, dtype):
    rows_t, cols_t = pattern.shape
    tile = values.shape[0] // rows_t
    shaped = values.reshape(rows_t, tile, cols_t, tile) * pattern[:, None, :, None].astype(dtype)
    return shaped.reshape(values.shape)


def body(matrix, in_pattern, out_pattern):
    local = apply_mask(matrix, in_pattern, jnp.bfloat16)
    band_height = local.shape[0]
    panel_width = local.shape[1]
    blocks = lax.axis_size("blk")
    start_totals = jnp.zeros((band_height, panel_width), jnp.float32)
    gathered = lax.all_gather(local, "grp", axis=1, tiled=True)
    position = lax.axis_index("blk")

    def step_once(step, carry):
        totals, panel = carry
        source = (position - step) % blocks
        operand = lax.dynamic_slice_in_dim(gathered, source * band_height, band_height, 1)
        totals = totals + jnp.dot(operand, panel, preferred_element_type=jnp.float32)
        panel = shifted(panel, "blk", 1)
        return (totals, panel)

    totals, panel = lax.fori_loop(0, blocks - 1, step_once, (start_totals, local))
    source = (position - (blocks - 1)) % blocks
    operand = lax.dynamic_slice_in_dim(gathered, source * band_height, band_height, 1)
    expanded = totals + jnp.dot(operand, panel, preferred_element_type=jnp.float32)
    kept = apply_mask(expanded, out_pattern, jnp.float32)
    inflated = kept * kept
    column_totals = lax.psum(jnp.sum(inflated, axis=0), "blk")
    rows_total = float(band_height * blocks)
    scaled = inflated / column_totals[None, :] * rows_total
    return jnp.maximum(scaled - prune_level, 0.0).astype(jnp.bfloat16)


def solution(mesh):
    in_specs = (P("blk", "grp"), P("blk", "grp"), P("blk", "grp"))
    out_specs = P("blk", "grp")
    return jax.shard_map(body, mesh=mesh, in_specs=in_specs, out_specs=out_specs, check_vma=False)
```

profile of v0, /device:TPU:202, one launch (start us, length us, event | category | flops | bytes accessed | tf_op | source)
XLA Modules:
  0.0 447.5 jit_solution(46112394881607351)
XLA Ops:
  7.5 1.7 bitcast_multiply_fusion
  10.1 90.4 %all-gather.2.cloned.1.call-done = bf16[512,8192]{1,0:T(8,128)(2,1)} async-done(((bf16[512,256]{1,0:T(8,128)(2,1)}), bf16[512,8192]{1,0:T(8,128)(2,1)}) %all-gather.2.cloned.1.call-update) | async-done | bytes 8388624 | tf_op jit(solution)/shard_map/all_gather | solution.py:27
  100.5 280.7 %while.18 = (s32[]{:T(128)}, f32[512,256]{1,0:T(8,128)S(1)}, bf16[512,256]{1,0:T(8,128)(2,1)}, s32[]{:T(128)}, bf16[512,8192]{1,0:T(8,128)(2,1)}, /*index=5*/s32...) while((s32[]{:T(128)}, f32[512,256]{1,0:T(8,128)S(1)}, ...), condition=%wide.region_1.2_spmd.clone, body=%wide.region_0.1_spmd.clone.sunk | while | flops 134479888 | bytes 4456806 | solution.py:38
  100.5 0.9 copy.15
  101.4 3.4 collective-permute-start
  104.8 1.4 convolution_add_fusion.3
  106.3 5.5 %collective-permute-done = bf16[512,256]{1,0:T(8,128)(2,1)S(1)} collective-permute-done((bf16[512,256]{1,0:T(8,128)(2,1)S(1)}, bf16[512,256]{1,0:T(8,128)(2,1)S(1)}, u32[]{:S(2)}, u32[]{:S(2)}) %collective-permute-start) | collective-permute-done | bytes 262176 | tf_op jit(solution)/shard_map/while/body/eval_jaxpr/ppermute | solution.py:11
  112.4 0.9 copy.15
  113.4 3.4 collective-permute-start
  116.8 1.4 convolution_add_fusion.3
  118.3 14.1 %collective-permute-done = bf16[512,256]{1,0:T(8,128)(2,1)S(1)} collective-permute-done((bf16[512,256]{1,0:T(8,128)(2,1)S(1)}, bf16[512,256]{1,0:T(8,128)(2,1)S(1)}, u32[]{:S(2)}, u32[]{:S(2)}) %collective-permute-start) | collective-permute-done | bytes 262176 | tf_op jit(solution)/shard_map/while/body/eval_jaxpr/ppermute | solution.py:11
  133.0 0.9 copy.15
  134.0 1.9 collective-permute-start
  135.9 1.4 convolution_add_fusion.3
  137.3 16.6 %collective-permute-done = bf16[512,256]{1,0:T(8,128)(2,1)S(1)} collective-permute-done((bf16[512,256]{1,0:T(8,128)(2,1)S(1)}, bf16[512,256]{1,0:T(8,128)(2,1)S(1)}, u32[]{:S(2)}, u32[]{:S(2)}) %collective-permute-start) | collective-permute-done | bytes 262176 | tf_op jit(solution)/shard_map/while/body/eval_jaxpr/ppermute | solution.py:11
  154.6 0.9 copy.15
  155.6 1.9 collective-permute-start
  157.5 1.4 convolution_add_fusion.3
  158.9 12.8 %collective-permute-done = bf16[512,256]{1,0:T(8,128)(2,1)S(1)} collective-permute-done((bf16[512,256]{1,0:T(8,128)(2,1)S(1)}, bf16[512,256]{1,0:T(8,128)(2,1)S(1)}, u32[]{:S(2)}, u32[]{:S(2)}) %collective-permute-start) | collective-permute-done | bytes 262176 | tf_op jit(solution)/shard_map/while/body/eval_jaxpr/ppermute | solution.py:11
  172.4 0.9 copy.15
  173.4 1.9 collective-permute-start
  175.3 1.4 convolution_add_fusion.3
  176.7 12.2 %collective-permute-done = bf16[512,256]{1,0:T(8,128)(2,1)S(1)} collective-permute-done((bf16[512,256]{1,0:T(8,128)(2,1)S(1)}, bf16[512,256]{1,0:T(8,128)(2,1)S(1)}, u32[]{:S(2)}, u32[]{:S(2)}) %collective-permute-start) | collective-permute-done | bytes 262176 | tf_op jit(solution)/shard_map/while/body/eval_jaxpr/ppermute | solution.py:11
  189.6 0.9 copy.15
  190.6 1.9 collective-permute-start
  192.5 1.4 convolution_add_fusion.3
  194.0 13.3 %collective-permute-done = bf16[512,256]{1,0:T(8,128)(2,1)S(1)} collective-permute-done((bf16[512,256]{1,0:T(8,128)(2,1)S(1)}, bf16[512,256]{1,0:T(8,128)(2,1)S(1)}, u32[]{:S(2)}, u32[]{:S(2)}) %collective-permute-start) | collective-permute-done | bytes 262176 | tf_op jit(solution)/shard_map/while/body/eval_jaxpr/ppermute | solution.py:11
  207.9 0.9 copy.15
  208.9 1.9 collective-permute-start
  210.8 1.4 convolution_add_fusion.3
  212.3 13.7 %collective-permute-done = bf16[512,256]{1,0:T(8,128)(2,1)S(1)} collective-permute-done((bf16[512,256]{1,0:T(8,128)(2,1)S(1)}, bf16[512,256]{1,0:T(8,128)(2,1)S(1)}, u32[]{:S(2)}, u32[]{:S(2)}) %collective-permute-start) | collective-permute-done | bytes 262176 | tf_op jit(solution)/shard_map/while/body/eval_jaxpr/ppermute | solution.py:11
  226.7 0.9 copy.15
  227.6 1.9 collective-permute-start
  229.6 1.4 convolution_add_fusion.3
  231.0 12.9 %collective-permute-done = bf16[512,256]{1,0:T(8,128)(2,1)S(1)} collective-permute-done((bf16[512,256]{1,0:T(8,128)(2,1)S(1)}, bf16[512,256]{1,0:T(8,128)(2,1)S(1)}, u32[]{:S(2)}, u32[]{:S(2)}) %collective-permute-start) | collective-permute-done | bytes 262176 | tf_op jit(solution)/shard_map/while/body/eval_jaxpr/ppermute | solution.py:11
  244.6 0.9 copy.15
  245.6 1.9 collective-permute-start
  247.5 1.4 convolution_add_fusion.3
  248.9 12.5 %collective-permute-done = bf16[512,256]{1,0:T(8,128)(2,1)S(1)} collective-permute-done((bf16[512,256]{1,0:T(8,128)(2,1)S(1)}, bf16[512,256]{1,0:T(8,128)(2,1)S(1)}, u32[]{:S(2)}, u32[]{:S(2)}) %collective-permute-start) | collective-permute-done | bytes 262176 | tf_op jit(solution)/shard_map/while/body/eval_jaxpr/ppermute | solution.py:11
  262.2 0.9 copy.15
  263.1 1.9 collective-permute-start
  265.1 1.4 convolution_add_fusion.3
  266.5 13.2 %collective-permute-done = bf16[512,256]{1,0:T(8,128)(2,1)S(1)} collective-permute-done((bf16[512,256]{1,0:T(8,128)(2,1)S(1)}, bf16[512,256]{1,0:T(8,128)(2,1)S(1)}, u32[]{:S(2)}, u32[]{:S(2)}) %collective-permute-start) | collective-permute-done | bytes 262176 | tf_op jit(solution)/shard_map/while/body/eval_jaxpr/ppermute | solution.py:11
  280.4 0.9 copy.15
  281.3 1.9 collective-permute-start
  283.2 1.4 convolution_add_fusion.3
  284.7 13.9 %collective-permute-done = bf16[512,256]{1,0:T(8,128)(2,1)S(1)} collective-permute-done((bf16[512,256]{1,0:T(8,128)(2,1)S(1)}, bf16[512,256]{1,0:T(8,128)(2,1)S(1)}, u32[]{:S(2)}, u32[]{:S(2)}) %collective-permute-start) | collective-permute-done | bytes 262176 | tf_op jit(solution)/shard_map/while/body/eval_jaxpr/ppermute | solution.py:11
  299.3 0.9 copy.15
  300.2 1.9 collective-permute-start
  302.2 1.4 convolution_add_fusion.3
  303.6 14.7 %collective-permute-done = bf16[512,256]{1,0:T(8,128)(2,1)S(1)} collective-permute-done((bf16[512,256]{1,0:T(8,128)(2,1)S(1)}, bf16[512,256]{1,0:T(8,128)(2,1)S(1)}, u32[]{:S(2)}, u32[]{:S(2)}) %collective-permute-start) | collective-permute-done | bytes 262176 | tf_op jit(solution)/shard_map/while/body/eval_jaxpr/ppermute | solution.py:11
  319.0 0.9 copy.15
  320.0 1.9 collective-permute-start
  321.9 1.4 convolution_add_fusion.3
  323.4 15.5 %collective-permute-done = bf16[512,256]{1,0:T(8,128)(2,1)S(1)} collective-permute-done((bf16[512,256]{1,0:T(8,128)(2,1)S(1)}, bf16[512,256]{1,0:T(8,128)(2,1)S(1)}, u32[]{:S(2)}, u32[]{:S(2)}) %collective-permute-start) | collective-permute-done | bytes 262176 | tf_op jit(solution)/shard_map/while/body/eval_jaxpr/ppermute | solution.py:11
  339.5 0.9 copy.15
  340.5 1.9 collective-permute-start
  342.4 1.4 convolution_add_fusion.3
  343.9 15.3 %collective-permute-done = bf16[512,256]{1,0:T(8,128)(2,1)S(1)} collective-permute-done((bf16[512,256]{1,0:T(8,128)(2,1)S(1)}, bf16[512,256]{1,0:T(8,128)(2,1)S(1)}, u32[]{:S(2)}, u32[]{:S(2)}) %collective-permute-start) | collective-permute-done | bytes 262176 | tf_op jit(solution)/shard_map/while/body/eval_jaxpr/ppermute | solution.py:11
  360.9 1.9 collective-permute-start
  362.8 1.4 convolution_add_fusion.3
  364.2 16.2 %collective-permute-done = bf16[512,256]{1,0:T(8,128)(2,1)S(1)} collective-permute-done((bf16[512,256]{1,0:T(8,128)(2,1)S(1)}, bf16[512,256]{1,0:T(8,128)(2,1)S(1)}, u32[]{:S(2)}, u32[]{:S(2)}) %collective-permute-start) | collective-permute-done | bytes 262176 | tf_op jit(solution)/shard_map/while/body/eval_jaxpr/ppermute | solution.py:11
  381.4 1.4 fusion.6
  382.8 57.1 %psum.7 = f32[256]{0:T(256)S(1)} all-reduce(f32[256]{0:T(256)S(1)} %get-tuple-element.169), channel_id=1, replica_groups=mesh['blk'=16,'grp'=32] {'blk'}, use_global_device_ids=true, to_apply=%region_3.4 | all-reduce | flops 256 | bytes 2048 | tf_op jit(solution)/shard_map/psum | solution.py:44
  (41 shorter events, 14.3 us)
Async XLA Ops:
  6.5 93.9 %all-gather.2.cloned.1.call-start = ((), (), s32[]{:S(2)}) async-start(), calls=%async_computation | async-start | bytes 8650752 | tf_op jit(solution)/shard_map/all_gather | solution.py:27
  101.4 10.3 %collective-permute-start = (bf16[512,256]{1,0:T(8,128)(2,1)S(1)}, bf16[512,256]{1,0:T(8,128)(2,1)S(1)}, u32[]{:S(2)}, u32[]{:S(2)}) collective-permute-start(bf16[512,256]{1,0:T(8,128)(2,1)S(1)} %copy.15), channel_id=1, source_target_pairs={{0,32},{32,64},{64,96},{96,128},{128,160},{160,192},{192,224},{224... | collective-permute-start | bytes 786440 | tf_op jit(solution)/shard_map/while/body/eval_jaxpr/ppermute | solution.py:11
  111.7 0.7 copy-start
  113.4 18.9 %collective-permute-start = (bf16[512,256]{1,0:T(8,128)(2,1)S(1)}, bf16[512,256]{1,0:T(8,128)(2,1)S(1)}, u32[]{:S(2)}, u32[]{:S(2)}) collective-permute-start(bf16[512,256]{1,0:T(8,128)(2,1)S(1)} %copy.15), channel_id=1, source_target_pairs={{0,32},{32,64},{64,96},{96,128},{128,160},{160,192},{192,224},{224... | collective-permute-start | bytes 786440 | tf_op jit(solution)/shard_map/while/body/eval_jaxpr/ppermute | solution.py:11
  132.3 0.7 copy-start
  134.0 19.9 %collective-permute-start = (bf16[512,256]{1,0:T(8,128)(2,1)S(1)}, bf16[512,256]{1,0:T(8,128)(2,1)S(1)}, u32[]{:S(2)}, u32[]{:S(2)}) collective-permute-start(bf16[512,256]{1,0:T(8,128)(2,1)S(1)} %copy.15), channel_id=1, source_target_pairs={{0,32},{32,64},{64,96},{96,128},{128,160},{160,192},{192,224},{224... | collective-permute-start | bytes 786440 | tf_op jit(solution)/shard_map/while/body/eval_jaxpr/ppermute | solution.py:11
  153.9 0.7 copy-start
  155.6 16.2 %collective-permute-start = (bf16[512,256]{1,0:T(8,128)(2,1)S(1)}, bf16[512,256]{1,0:T(8,128)(2,1)S(1)}, u32[]{:S(2)}, u32[]{:S(2)}) collective-permute-start(bf16[512,256]{1,0:T(8,128)(2,1)S(1)} %copy.15), channel_id=1, source_target_pairs={{0,32},{32,64},{64,96},{96,128},{128,160},{160,192},{192,224},{224... | collective-permute-start | bytes 786440 | tf_op jit(solution)/shard_map/while/body/eval_jaxpr/ppermute | solution.py:11
  171.7 0.7 copy-start
  173.4 15.6 %collective-permute-start = (bf16[512,256]{1,0:T(8,128)(2,1)S(1)}, bf16[512,256]{1,0:T(8,128)(2,1)S(1)}, u32[]{:S(2)}, u32[]{:S(2)}) collective-permute-start(bf16[512,256]{1,0:T(8,128)(2,1)S(1)} %copy.15), channel_id=1, source_target_pairs={{0,32},{32,64},{64,96},{96,128},{128,160},{160,192},{192,224},{224... | collective-permute-start | bytes 786440 | tf_op jit(solution)/shard_map/while/body/eval_jaxpr/ppermute | solution.py:11
  188.9 0.7 copy-start
  190.6 16.7 %collective-permute-start = (bf16[512,256]{1,0:T(8,128)(2,1)S(1)}, bf16[512,256]{1,0:T(8,128)(2,1)S(1)}, u32[]{:S(2)}, u32[]{:S(2)}) collective-permute-start(bf16[512,256]{1,0:T(8,128)(2,1)S(1)} %copy.15), channel_id=1, source_target_pairs={{0,32},{32,64},{64,96},{96,128},{128,160},{160,192},{192,224},{224... | collective-permute-start | bytes 786440 | tf_op jit(solution)/shard_map/while/body/eval_jaxpr/ppermute | solution.py:11
  207.2 0.7 copy-start
  208.9 17.1 %collective-permute-start = (bf16[512,256]{1,0:T(8,128)(2,1)S(1)}, bf16[512,256]{1,0:T(8,128)(2,1)S(1)}, u32[]{:S(2)}, u32[]{:S(2)}) collective-permute-start(bf16[512,256]{1,0:T(8,128)(2,1)S(1)} %copy.15), channel_id=1, source_target_pairs={{0,32},{32,64},{64,96},{96,128},{128,160},{160,192},{192,224},{224... | collective-permute-start | bytes 786440 | tf_op jit(solution)/shard_map/while/body/eval_jaxpr/ppermute | solution.py:11
  226.0 0.7 copy-start
  227.6 16.3 %collective-permute-start = (bf16[512,256]{1,0:T(8,128)(2,1)S(1)}, bf16[512,256]{1,0:T(8,128)(2,1)S(1)}, u32[]{:S(2)}, u32[]{:S(2)}) collective-permute-start(bf16[512,256]{1,0:T(8,128)(2,1)S(1)} %copy.15), channel_id=1, source_target_pairs={{0,32},{32,64},{64,96},{96,128},{128,160},{160,192},{192,224},{224... | collective-permute-start | bytes 786440 | tf_op jit(solution)/shard_map/while/body/eval_jaxpr/ppermute | solution.py:11
  243.9 0.7 copy-start
  245.6 15.9 %collective-permute-start = (bf16[512,256]{1,0:T(8,128)(2,1)S(1)}, bf16[512,256]{1,0:T(8,128)(2,1)S(1)}, u32[]{:S(2)}, u32[]{:S(2)}) collective-permute-start(bf16[512,256]{1,0:T(8,128)(2,1)S(1)} %copy.15), channel_id=1, source_target_pairs={{0,32},{32,64},{64,96},{96,128},{128,160},{160,192},{192,224},{224... | collective-permute-start | bytes 786440 | tf_op jit(solution)/shard_map/while/body/eval_jaxpr/ppermute | solution.py:11
  261.5 0.7 copy-start
  263.1 16.5 %collective-permute-start = (bf16[512,256]{1,0:T(8,128)(2,1)S(1)}, bf16[512,256]{1,0:T(8,128)(2,1)S(1)}, u32[]{:S(2)}, u32[]{:S(2)}) collective-permute-start(bf16[512,256]{1,0:T(8,128)(2,1)S(1)} %copy.15), channel_id=1, source_target_pairs={{0,32},{32,64},{64,96},{96,128},{128,160},{160,192},{192,224},{224... | collective-permute-start | bytes 786440 | tf_op jit(solution)/shard_map/while/body/eval_jaxpr/ppermute | solution.py:11
  279.6 0.7 copy-start
  281.3 17.3 %collective-permute-start = (bf16[512,256]{1,0:T(8,128)(2,1)S(1)}, bf16[512,256]{1,0:T(8,128)(2,1)S(1)}, u32[]{:S(2)}, u32[]{:S(2)}) collective-permute-start(bf16[512,256]{1,0:T(8,128)(2,1)S(1)} %copy.15), channel_id=1, source_target_pairs={{0,32},{32,64},{64,96},{96,128},{128,160},{160,192},{192,224},{224... | collective-permute-start | bytes 786440 | tf_op jit(solution)/shard_map/while/body/eval_jaxpr/ppermute | solution.py:11
  298.6 0.7 copy-start
  300.2 18.1 %collective-permute-start = (bf16[512,256]{1,0:T(8,128)(2,1)S(1)}, bf16[512,256]{1,0:T(8,128)(2,1)S(1)}, u32[]{:S(2)}, u32[]{:S(2)}) collective-permute-start(bf16[512,256]{1,0:T(8,128)(2,1)S(1)} %copy.15), channel_id=1, source_target_pairs={{0,32},{32,64},{64,96},{96,128},{128,160},{160,192},{192,224},{224... | collective-permute-start | bytes 786440 | tf_op jit(solution)/shard_map/while/body/eval_jaxpr/ppermute | solution.py:11
  318.3 0.7 copy-start
  320.0 18.8 %collective-permute-start = (bf16[512,256]{1,0:T(8,128)(2,1)S(1)}, bf16[512,256]{1,0:T(8,128)(2,1)S(1)}, u32[]{:S(2)}, u32[]{:S(2)}) collective-permute-start(bf16[512,256]{1,0:T(8,128)(2,1)S(1)} %copy.15), channel_id=1, source_target_pairs={{0,32},{32,64},{64,96},{96,128},{128,160},{160,192},{192,224},{224... | collective-permute-start | bytes 786440 | tf_op jit(solution)/shard_map/while/body/eval_jaxpr/ppermute | solution.py:11
  338.8 0.7 copy-start
  340.5 18.7 %collective-permute-start = (bf16[512,256]{1,0:T(8,128)(2,1)S(1)}, bf16[512,256]{1,0:T(8,128)(2,1)S(1)}, u32[]{:S(2)}, u32[]{:S(2)}) collective-permute-start(bf16[512,256]{1,0:T(8,128)(2,1)S(1)} %copy.15), channel_id=1, source_target_pairs={{0,32},{32,64},{64,96},{96,128},{128,160},{160,192},{192,224},{224... | collective-permute-start | bytes 786440 | tf_op jit(solution)/shard_map/while/body/eval_jaxpr/ppermute | solution.py:11
  359.2 0.7 copy-start
  360.9 19.6 %collective-permute-start = (bf16[512,256]{1,0:T(8,128)(2,1)S(1)}, bf16[512,256]{1,0:T(8,128)(2,1)S(1)}, u32[]{:S(2)}, u32[]{:S(2)}) collective-permute-start(bf16[512,256]{1,0:T(8,128)(2,1)S(1)} %copy.15), channel_id=1, source_target_pairs={{0,32},{32,64},{64,96},{96,128},{128,160},{160,192},{192,224},{224... | collective-permute-start | bytes 786440 | tf_op jit(solution)/shard_map/while/body/eval_jaxpr/ppermute | solution.py:11
  380.5 0.7 copy-start
Sparse Core Ops, SparseCore 0:
  9.4 90.9 all-gather.1
where the time goes:
time: 449 us; the launch traced here: 448 us
  waiting for transfers between devices  293 us (65%)
  blocking collectives  57.1 us (13%)
  starting transfers between devices  31.6 us (7%)
  local copies, waits for them, and re-layouts  25.4 us (6%)
  matrix products  22.9 us (5%)
  between operations  13.4 us (3%)
    ppermute x15, waiting for transfers between devices, shifted(): lax.ppermute(array, axis, [(i, (i + by) % peers) for i in range(peers)])  202 us
    all_gather x1, waiting for transfers between devices, body(): gathered = lax.all_gather(local, 'grp', axis=1, tiled=True)  90.4 us
    psum x1, blocking collectives, body(): column_totals = lax.psum(jnp.sum(inflated, axis=0), 'blk')  57.1 us
    ppermute x15, starting transfers between devices, shifted(): lax.ppermute(array, axis, [(i, (i + by) % peers) for i in range(peers)])  31.6 us
    while x45, local copies, waits for them, and re-layouts  24.8 us
    dot_general x15, matrix products, step_once(): jnp.dot(operand, panel, preferred_element_type=jnp.float32)  21.5 us
  transfers between devices with their start and end apart: 16, of which 16 were waited for; matrix products, arithmetic and copies ran while one was open for 5% of the time, Pallas kernels for 0%

commit v1 on v0

v1 whole, which is shorter than its diff:
```python
import functools

import jax
import jax.numpy as jnp
from jax import lax
from jax.experimental import pallas as pl
from jax.experimental.pallas import tpu as pltpu
from jax.sharding import Mesh, PartitionSpec as P

prune_level = 0.5
TILE = 128
RB = 4
CB = 2
CAP = 4
META = 16
PACK = CAP * TILE + META
AXES = ("zh", "y", "x", "zl", "core")
SIZES = (2, 8, 4, 4, 2)
BLK = ("zh", "y")
GRP = ("x", "zl", "core")


def pack_kernel(pattern, matrix, out):
    count = jnp.int32(0)
    lane = lax.broadcasted_iota(jnp.int32, (META, TILE), 1)
    slots = jnp.full((META, TILE), CAP, jnp.int32)
    for t in range(RB * CB):
        r, s = divmod(t, CB)
        present = pattern[r, s] != 0
        slot = jnp.minimum(count, CAP - 1)

        @pl.when(present)
        def _():
            place = pl.multiple_of(slot * TILE, TILE)
            out[pl.ds(place, TILE), :] = matrix[r * TILE:(r + 1) * TILE, s * TILE:(s + 1) * TILE]

        slots = jnp.where((lane == t) & present, slot, slots)
        count = count + present.astype(jnp.int32)
    out[CAP * TILE:PACK, :] = slots.astype(jnp.float32).astype(jnp.bfloat16)


def pack(matrix, pattern):
    return pl.pallas_call(
        pack_kernel,
        out_shape=jax.ShapeDtypeStruct((PACK, TILE), jnp.bfloat16),
        in_specs=[pl.BlockSpec(memory_space=pltpu.SMEM), pl.BlockSpec(memory_space=pltpu.VMEM)],
        out_specs=pl.BlockSpec(memory_space=pltpu.VMEM),
        name="pack_tiles",
    )(pattern, matrix)


def product_kernel(steps, place, keep, band, *rest):
    panels = rest[:steps]
    out, totals = rest[steps:steps + 2]
    meta, table, sem, a_dense, b_dense, acc = rest[steps + 2:]
    chips = band.shape[0] // CB
    for g in range(CB * chips):
        row = band[g, CAP * TILE:PACK, :].astype(jnp.float32).astype(jnp.int32)
        meta[g:g + 1, :] = row[0:1]
    for j in range(steps):
        for z in range(2):
            row = panels[j][z, CAP * TILE:PACK, :].astype(jnp.float32).astype(jnp.int32)
            at = CB * chips + 2 * j + z
            meta[at:at + 1, :] = row[0:1]
    copy = pltpu.make_async_copy(meta, table, sem)
    copy.start()
    acc[...] = jnp.zeros_like(acc)
    copy.wait()
    y = place[0]

    def spread(ref, index, row, dense, col):
        for t in range(RB * CB):
            r, s = divmod(t, CB)
            slot = table[row, t]
            start = pl.multiple_of(jnp.minimum(slot, CAP - 1) * TILE, TILE)
            tile = ref[index, pl.ds(start, TILE), :]
            tile = jnp.where(slot < CAP, tile, jnp.zeros_like(tile))
            dense[r * TILE:(r + 1) * TILE, col + s * TILE:col + (s + 1) * TILE] = tile

    for j in range(steps):
        source = lax.rem(y - j + steps, steps)
        for z in range(2):
            chip = z * steps + source
            slot = (2 * j + z) % 2
            for c in range(CB):
                g = chip * CB + c
                spread(band, g, g, a_dense.at[slot], c * CB * TILE)
            spread(panels[j], z, CB * chips + 2 * j + z, b_dense.at[slot], 0)
            acc[...] += jnp.dot(a_dense[slot], b_dense[slot], preferred_element_type=jnp.float32)

    for s in range(CB):
        total = jnp.zeros((1, TILE), jnp.float32)
        for r in range(RB):
            at = (slice(r * TILE, (r + 1) * TILE), slice(s * TILE, (s + 1) * TILE))
            kept = acc[at] * keep[r, s].astype(jnp.float32)
            inflated = kept * kept
            out[at] = inflated
            total = total + jnp.sum(inflated, axis=0, keepdims=True)
        totals[:, s * TILE:(s + 1) * TILE] = total


def product(place, keep, band, panels):
    steps = len(panels)
    smem = pl.BlockSpec(memory_space=pltpu.SMEM)
    vmem = pl.BlockSpec(memory_space=pltpu.VMEM)
    entries = band.shape[0] + 2 * steps
    return pl.pallas_call(
        functools.partial(product_kernel, steps),
        out_shape=(
            jax.ShapeDtypeStruct((RB * TILE, CB * TILE), jnp.float32),
            jax.ShapeDtypeStruct((1, CB * TILE), jnp.float32),
        ),
        in_specs=[smem, smem, vmem] + [vmem] * steps,
        out_specs=(vmem, vmem),
        scratch_shapes=[
            pltpu.VMEM((entries, TILE), jnp.int32),
            pltpu.SMEM((entries, TILE), jnp.int32),
            pltpu.SemaphoreType.DMA,
            pltpu.VMEM((2, RB * TILE, RB * TILE), jnp.bfloat16),
            pltpu.VMEM((2, RB * TILE, CB * TILE), jnp.bfloat16),
            pltpu.VMEM((RB * TILE, CB * TILE), jnp.float32),
        ],
        compiler_params=pltpu.CompilerParams(vmem_limit_bytes=40 * 2**20),
        name="product",
    )(place, keep, band, *panels)


def shifted(array, axis, by):
    n = lax.axis_size(axis)
    return lax.ppermute(array, axis, [(i, (i + by) % n) for i in range(n)])


def body(matrix, in_pattern, out_pattern):
    packed = pack(matrix, in_pattern)
    band = lax.all_gather(packed, GRP)
    other = shifted(packed, "zh", 1)
    hi = lax.axis_index("zh")
    own = jnp.where(hi == 0, jnp.stack([packed, other]), jnp.stack([other, packed]))
    steps = lax.axis_size("y")
    up, down = [own], [own]
    for i in range(steps // 2):
        up.append(shifted(up[-1], "y", 1))
        if i < steps // 2 - 1:
            down.append(shifted(down[-1], "y", -1))
    panels = [own] + up[1:] + down[:0:-1]
    place = lax.axis_index("y").reshape(1)
    inflated, totals = product(place, out_pattern, band, panels)
    column_totals = lax.psum(lax.psum(totals, "zh"), "y")
    scaled = inflated / column_totals * float(SIZES[0] * SIZES[1] * RB * TILE)
    return jnp.maximum(scaled - prune_level, 0.0).astype(jnp.bfloat16)


def solution(mesh):
    fine = Mesh(mesh.devices.reshape(SIZES), AXES)
    spec = P(BLK, GRP)
    return jax.shard_map(body, mesh=fine, in_specs=(spec,) * 3, out_specs=spec, check_vma=False)
```

time: 449 us -> 123 us (0.27)
  the two profiles are of different devices: /device:TPU:202 before, /device:TPU:2 now
where the time goes in v1:
time: 123 us
  waiting for transfers between devices  34.9 us (28%)
  starting transfers between devices  34.2 us (28%)
  blocking collectives  25.8 us (21%)
  between operations  13.5 us (11%)
  Pallas kernels  8.41 us (7%)
  local copies, waits for them, and re-layouts  4.34 us (4%)
  other arithmetic  1.81 us (1%)
    ppermute x8, starting transfers between devices, shifted(): return lax.ppermute(array, axis, [(i, (i + by) % n) for i in range(n)])  34.2 us
    psum x2, blocking collectives, body(): column_totals = lax.psum(lax.psum(totals, 'zh'), 'y')  25.8 us
    ppermute x8, waiting for transfers between devices, shifted(): return lax.ppermute(array, axis, [(i, (i + by) % n) for i in range(n)])  20.1 us
    all_gather x1, waiting for transfers between devices, body(): band = lax.all_gather(packed, GRP)  14.8 us
    pallas_call x1, Pallas kernels, product(): pl.pallas_call(functools.partial(product_kernel, steps), out_shape=(jax.S...  6.71 us
    unnamed x4, local copies, waits for them, and re-layouts  4.34 us
  transfers between devices with their start and end apart: 9, of which 6 were waited for; matrix products, arithmetic and copies ran while one was open for 1% of the time, Pallas kernels for 0%

profile of v1, /device:TPU:2, one launch (start us, length us, event | category | flops | bytes accessed | tf_op | source)
XLA Modules:
  0.0 122.9 jit_solution(1393812675543779664)
XLA Ops:
  6.5 0.0 all-gather.3.cloned.1.call-start
  6.5 1.3 %copy.4.pattern = s32[4,2]{1,0:T(4,128)} copy(s32[4,2]{0,1:T(2,128)} %param.4) | data formatting | bytes 64 | tf_op args[1]
  7.9 1.7 %pack_tiles.1 = bf16[528,128]{1,0:T(8,128)(2,1)} custom-call(s32[4,2]{1,0:T(4,128)} %copy.4.pattern, bf16[512,256]{1,0:T(8,128)(2,1)} %matrix.1), custom_call_target="tpu_custom_call" | custom-call | tf_op jit(solution)/shard_map/pack_tiles/pallas_call | solution.py:43
  9.6 0.0 all-gather.3.cloned.1.call-update
  9.6 10.9 %collective-permute-start = (bf16[528,128]{1,0:T(8,128)(2,1)}, bf16[528,128]{1,0:T(8,128)(2,1)S(1)}, u32[]{:S(2)}, u32[]{:S(2)}) collective-permute-start(bf16[528,128]{1,0:T(8,128)(2,1)} %pack_tiles.1), channel_id=1, source_target_pairs={{0,256},{256,0},{1,257},{257,1},{2,258},{258,2},{3,259},{259,3},{4... | collective-permute-start | bytes 405512 | tf_op jit(solution)/shard_map/ppermute | solution.py:130
  20.5 3.9 %collective-permute-done = bf16[528,128]{1,0:T(8,128)(2,1)S(1)} collective-permute-done((bf16[528,128]{1,0:T(8,128)(2,1)}, bf16[528,128]{1,0:T(8,128)(2,1)S(1)}, u32[]{:S(2)}, u32[]{:S(2)}) %collective-permute-start) | collective-permute-done | bytes 135200 | tf_op jit(solution)/shard_map/ppermute | solution.py:130
  24.4 1.0 maximum_select_fusion.rest_0_
  25.4 3.5 %collective-permute-start.1 = (bf16[2,528,128]{2,1,0:T(8,128)(2,1)S(1)}, bf16[2,528,128]{2,1,0:T(8,128)(2,1)S(1)}, u32[]{:S(2)}, u32[]{:S(2)}) collective-permute-start(bf16[2,528,128]{2,1,0:T(8,128)(2,1)S(1)} %maximum_select_fusion.rest_0_), channel_id=1, source_target_pairs={{0,32},{32,64},{64,96},{96,128},{128,160},{160,192},{192,224},{224... | collective-permute-start | bytes 811016 | tf_op jit(solution)/shard_map/ppermute | solution.py:130
  28.9 3.8 %collective-permute-start.5 = (bf16[2,528,128]{2,1,0:T(8,128)(2,1)S(1)}, bf16[2,528,128]{2,1,0:T(8,128)(2,1)S(1)}, u32[]{:S(2)}, u32[]{:S(2)}) collective-permute-start(bf16[2,528,128]{2,1,0:T(8,128)(2,1)S(1)} %maximum_select_fusion.rest_0_), channel_id=1, source_target_pairs={{0,224},{32,0},{64,32},{96,64},{128,96},{160,128},{192,160},{224,1... | collective-permute-start | bytes 811016 | tf_op jit(solution)/shard_map/ppermute | solution.py:130
  32.7 3.9 %collective-permute-done.1.rest_1_ = bf16[2,528,128]{2,1,0:T(8,128)(2,1)S(1)} collective-permute-done((bf16[2,528,128]{2,1,0:T(8,128)(2,1)S(1)}, bf16[2,528,128]{2,1,0:T(8,128)(2,1)S(1)}, u32[]{:S(2)}, u32[]{:S(2)}) %collective-permute-start.1) | collective-permute-done | bytes 270368 | tf_op jit(solution)/shard_map/ppermute | solution.py:130
  36.6 1.9 %collective-permute-start.2 = (bf16[2,528,128]{2,1,0:T(8,128)(2,1)S(1)}, bf16[2,528,128]{2,1,0:T(8,128)(2,1)S(1)}, u32[]{:S(2)}, u32[]{:S(2)}) collective-permute-start(bf16[2,528,128]{2,1,0:T(8,128)(2,1)S(1)} %collective-permute-done.1.rest_1_), channel_id=1, source_target_pairs={{0,32},{32,64},{64,96},{96,128},{128,160},{160,192},{192,224},{224... | collective-permute-start | bytes 811016 | tf_op jit(solution)/shard_map/ppermute | solution.py:130
  38.5 0.0 collective-permute-done.5.rest_7_
  38.6 5.1 %collective-permute-start.6 = (bf16[2,528,128]{2,1,0:T(8,128)(2,1)S(1)}, bf16[2,528,128]{2,1,0:T(8,128)(2,1)S(1)}, u32[]{:S(2)}, u32[]{:S(2)}) collective-permute-start(bf16[2,528,128]{2,1,0:T(8,128)(2,1)S(1)} %collective-permute-done.5.rest_7_), channel_id=1, source_target_pairs={{0,224},{32,0},{64,32},{96,64},{128,96},{160,128},{192,160},{224,1... | collective-permute-start | bytes 811016 | tf_op jit(solution)/shard_map/ppermute | solution.py:130
  43.7 3.0 %collective-permute-done.2.rest_2_ = bf16[2,528,128]{2,1,0:T(8,128)(2,1)S(1)} collective-permute-done((bf16[2,528,128]{2,1,0:T(8,128)(2,1)S(1)}, bf16[2,528,128]{2,1,0:T(8,128)(2,1)S(1)}, u32[]{:S(2)}, u32[]{:S(2)}) %collective-permute-start.2) | collective-permute-done | bytes 270368 | tf_op jit(solution)/shard_map/ppermute | solution.py:130
  46.6 1.9 %collective-permute-start.3 = (bf16[2,528,128]{2,1,0:T(8,128)(2,1)S(1)}, bf16[2,528,128]{2,1,0:T(8,128)(2,1)S(1)}, u32[]{:S(2)}, u32[]{:S(2)}) collective-permute-start(bf16[2,528,128]{2,1,0:T(8,128)(2,1)S(1)} %collective-permute-done.2.rest_2_), channel_id=1, source_target_pairs={{0,32},{32,64},{64,96},{96,128},{128,160},{160,192},{192,224},{224... | collective-permute-start | bytes 811016 | tf_op jit(solution)/shard_map/ppermute | solution.py:130
  48.6 0.0 collective-permute-done.6.rest_6_
  48.6 5.1 %collective-permute-start.7 = (bf16[2,528,128]{2,1,0:T(8,128)(2,1)S(1)}, bf16[2,528,128]{2,1,0:T(8,128)(2,1)S(1)}, u32[]{:S(2)}, u32[]{:S(2)}) collective-permute-start(bf16[2,528,128]{2,1,0:T(8,128)(2,1)S(1)} %collective-permute-done.6.rest_6_), channel_id=1, source_target_pairs={{0,224},{32,0},{64,32},{96,64},{128,96},{160,128},{192,160},{224,1... | collective-permute-start | bytes 811016 | tf_op jit(solution)/shard_map/ppermute | solution.py:130
  53.7 2.5 %collective-permute-done.3.rest_3_ = bf16[2,528,128]{2,1,0:T(8,128)(2,1)S(1)} collective-permute-done((bf16[2,528,128]{2,1,0:T(8,128)(2,1)S(1)}, bf16[2,528,128]{2,1,0:T(8,128)(2,1)S(1)}, u32[]{:S(2)}, u32[]{:S(2)}) %collective-permute-start.3) | collective-permute-done | bytes 270368 | tf_op jit(solution)/shard_map/ppermute | solution.py:130
  56.2 1.9 %collective-permute-start.4 = (bf16[2,528,128]{2,1,0:T(8,128)(2,1)S(1)}, bf16[2,528,128]{2,1,0:T(8,128)(2,1)S(1)}, u32[]{:S(2)}, u32[]{:S(2)}) collective-permute-start(bf16[2,528,128]{2,1,0:T(8,128)(2,1)S(1)} %collective-permute-done.3.rest_3_), channel_id=1, source_target_pairs={{0,32},{32,64},{64,96},{96,128},{128,160},{160,192},{192,224},{224... | collective-permute-start | bytes 811016 | tf_op jit(solution)/shard_map/ppermute | solution.py:130
  58.1 0.8 copy.5.keep
  58.9 0.0 collective-permute-done.7.rest_5_
  58.9 6.9 %collective-permute-done.4.rest_4_ = bf16[2,528,128]{2,1,0:T(8,128)(2,1)S(1)} collective-permute-done((bf16[2,528,128]{2,1,0:T(8,128)(2,1)S(1)}, bf16[2,528,128]{2,1,0:T(8,128)(2,1)S(1)}, u32[]{:S(2)}, u32[]{:S(2)}) %collective-permute-start.4) | collective-permute-done | bytes 270368 | tf_op jit(solution)/shard_map/ppermute | solution.py:130
  65.8 14.8 %all-gather.3.cloned.1.call-done = bf16[16896,128]{1,0:T(8,128)(2,1)} async-done(((bf16[528,128]{1,0:T(8,128)(2,1)}), bf16[16896,128]{1,0:T(8,128)(2,1)}) %all-gather.3.cloned.1.call-update) | async-done | bytes 4325392 | tf_op jit(solution)/shard_map/all_gather | solution.py:135
  80.6 0.0 copy-start
  80.6 2.2 %copy-done = bf16[16896,128]{1,0:T(8,128)(2,1)S(1)} copy-done((bf16[16896,128]{1,0:T(8,128)(2,1)S(1)}, bf16[16896,128]{1,0:T(8,128)(2,1)}, u32[]{:S(2)}) %copy-start) | copy-done | bytes 4325400
  82.8 6.7 %product.1 = (f32[512,256]{1,0:T(8,128)S(1)}, f32[1,256]{1,0:T(1,128)S(1)}) custom-call(s32[1]{0:T(128)} %bitcast.place, s32[4,2]{1,0:T(4,128)S(1)} %copy.5.keep, bf16[32,528,128]{2,1,0:T(8,128)(2,1)S(1)} %bitcast.5, bf16[2,528,128]{2,1,0:T(8,128)(2,1)S(1)} %maximum_select_fusion.rest_0_, bf16[2,528,128]{2,1,0:T(8,128)(2,1)S(1)} %collective-permute-done.1.rest_1_, ...), custom_call_target="tpu_custom_call" | custom-call | tf_op jit(solution)/shard_map/product/pallas_call | solution.py:107
  89.5 8.8 %psum.14 = f32[1,256]{1,0:T(1,128)S(1)} all-reduce(f32[1,256]{1,0:T(1,128)S(1)} %get-tuple-element.8), channel_id=1, replica_groups=mesh['zh'=2,'y'=8,'x'=4,'zl'=4,'core'=2] {'zh'}, use_global_device_ids=true, to_apply=%region_0.1 | all-reduce | flops 256 | bytes 2048 | tf_op jit(solution)/shard_map/psum | solution.py:148
  98.3 16.9 %psum.15 = f32[256]{0:T(256)S(1)} all-reduce(f32[256]{0:T(256)S(1)} %bitcast.8), channel_id=1, replica_groups=mesh['zh'=2,'y'=8,'x'=4,'zl'=4,'core'=2] {'y'}, use_global_device_ids=true, to_apply=%region_1.2 | all-reduce | flops 256 | bytes 2048 | tf_op jit(solution)/shard_map/psum | solution.py:148
  115.3 0.8 maximum_convert_fusion
Async XLA Ops:
  6.5 74.0 %all-gather.3.cloned.1.call-start = ((), (), s32[]{:S(2)}) async-start(), calls=%async_computation | async-start | bytes 4460544 | tf_op jit(solution)/shard_map/all_gather | solution.py:135
  9.6 14.8 %collective-permute-start = (bf16[528,128]{1,0:T(8,128)(2,1)}, bf16[528,128]{1,0:T(8,128)(2,1)S(1)}, u32[]{:S(2)}, u32[]{:S(2)}) collective-permute-start(bf16[528,128]{1,0:T(8,128)(2,1)} %pack_tiles.1), channel_id=1, source_target_pairs={{0,256},{256,0},{1,257},{257,1},{2,258},{258,2},{3,259},{259,3},{4... | collective-permute-start | bytes 405512 | tf_op jit(solution)/shard_map/ppermute | solution.py:130
  25.4 11.2 %collective-permute-start.1 = (bf16[2,528,128]{2,1,0:T(8,128)(2,1)S(1)}, bf16[2,528,128]{2,1,0:T(8,128)(2,1)S(1)}, u32[]{:S(2)}, u32[]{:S(2)}) collective-permute-start(bf16[2,528,128]{2,1,0:T(8,128)(2,1)S(1)} %maximum_select_fusion.rest_0_), channel_id=1, source_target_pairs={{0,32},{32,64},{64,96},{96,128},{128,160},{160,192},{192,224},{224... | collective-permute-start | bytes 811016 | tf_op jit(solution)/shard_map/ppermute | solution.py:130
  28.9 9.6 %collective-permute-start.5 = (bf16[2,528,128]{2,1,0:T(8,128)(2,1)S(1)}, bf16[2,528,128]{2,1,0:T(8,128)(2,1)S(1)}, u32[]{:S(2)}, u32[]{:S(2)}) collective-permute-start(bf16[2,528,128]{2,1,0:T(8,128)(2,1)S(1)} %maximum_select_fusion.rest_0_), channel_id=1, source_target_pairs={{0,224},{32,0},{64,32},{96,64},{128,96},{160,128},{192,160},{224,1... | collective-permute-start | bytes 811016 | tf_op jit(solution)/shard_map/ppermute | solution.py:130
  36.6 10.0 %collective-permute-start.2 = (bf16[2,528,128]{2,1,0:T(8,128)(2,1)S(1)}, bf16[2,528,128]{2,1,0:T(8,128)(2,1)S(1)}, u32[]{:S(2)}, u32[]{:S(2)}) collective-permute-start(bf16[2,528,128]{2,1,0:T(8,128)(2,1)S(1)} %collective-permute-done.1.rest_1_), channel_id=1, source_target_pairs={{0,32},{32,64},{64,96},{96,128},{128,160},{160,192},{192,224},{224... | collective-permute-start | bytes 811016 | tf_op jit(solution)/shard_map/ppermute | solution.py:130
  38.6 10.0 %collective-permute-start.6 = (bf16[2,528,128]{2,1,0:T(8,128)(2,1)S(1)}, bf16[2,528,128]{2,1,0:T(8,128)(2,1)S(1)}, u32[]{:S(2)}, u32[]{:S(2)}) collective-permute-start(bf16[2,528,128]{2,1,0:T(8,128)(2,1)S(1)} %collective-permute-done.5.rest_7_), channel_id=1, source_target_pairs={{0,224},{32,0},{64,32},{96,64},{128,96},{160,128},{192,160},{224,1... | collective-permute-start | bytes 811016 | tf_op jit(solution)/shard_map/ppermute | solution.py:130
  46.6 9.6 %collective-permute-start.3 = (bf16[2,528,128]{2,1,0:T(8,128)(2,1)S(1)}, bf16[2,528,128]{2,1,0:T(8,128)(2,1)S(1)}, u32[]{:S(2)}, u32[]{:S(2)}) collective-permute-start(bf16[2,528,128]{2,1,0:T(8,128)(2,1)S(1)} %collective-permute-done.2.rest_2_), channel_id=1, source_target_pairs={{0,32},{32,64},{64,96},{96,128},{128,160},{160,192},{192,224},{224... | collective-permute-start | bytes 811016 | tf_op jit(solution)/shard_map/ppermute | solution.py:130
  48.6 10.3 %collective-permute-start.7 = (bf16[2,528,128]{2,1,0:T(8,128)(2,1)S(1)}, bf16[2,528,128]{2,1,0:T(8,128)(2,1)S(1)}, u32[]{:S(2)}, u32[]{:S(2)}) collective-permute-start(bf16[2,528,128]{2,1,0:T(8,128)(2,1)S(1)} %collective-permute-done.6.rest_6_), channel_id=1, source_target_pairs={{0,224},{32,0},{64,32},{96,64},{128,96},{160,128},{192,160},{224,1... | collective-permute-start | bytes 811016 | tf_op jit(solution)/shard_map/ppermute | solution.py:130
  56.2 9.6 %collective-permute-start.4 = (bf16[2,528,128]{2,1,0:T(8,128)(2,1)S(1)}, bf16[2,528,128]{2,1,0:T(8,128)(2,1)S(1)}, u32[]{:S(2)}, u32[]{:S(2)}) collective-permute-start(bf16[2,528,128]{2,1,0:T(8,128)(2,1)S(1)} %collective-permute-done.3.rest_3_), channel_id=1, source_target_pairs={{0,32},{32,64},{64,96},{96,128},{128,160},{160,192},{192,224},{224... | collective-permute-start | bytes 811016 | tf_op jit(solution)/shard_map/ppermute | solution.py:130
  80.6 2.2 %copy-start = (bf16[16896,128]{1,0:T(8,128)(2,1)S(1)}, bf16[16896,128]{1,0:T(8,128)(2,1)}, u32[]{:S(2)}) copy-start(bf16[16896,128]{1,0:T(8,128)(2,1)} %all-gather.3.cloned.1.call-done) | copy-start | bytes 12976132
Sparse Core Ops, SparseCore 0:
  9.7 70.7 all-gather.2

commit v2 on v1

v2 whole, which is shorter than its diff:
```python
import functools

import jax
import jax.numpy as jnp
from jax import lax
from jax.experimental import pallas as pl
from jax.experimental.pallas import tpu as pltpu
from jax.sharding import Mesh, PartitionSpec as P

prune_level = 0.5
TILE = 128
RB = 4
CB = 2
CAP = 4
META = 16
PACK = CAP * TILE + META
AXES = ("zh", "y", "x", "zl", "core")
SIZES = (2, 8, 4, 4, 2)
BLK = ("zh", "y")
GRP = ("x", "zl", "core")


SMEM = pl.BlockSpec(memory_space=pltpu.SMEM)
VMEM = pl.BlockSpec(memory_space=pltpu.VMEM)
BLOCK = (RB * TILE, CB * TILE)


def pack_kernel(pattern, matrix, *outs):
    count = jnp.int32(0)
    lane = lax.broadcasted_iota(jnp.int32, (META, TILE), 1)
    slots = jnp.full((META, TILE), CAP, jnp.int32)
    for t in range(RB * CB):
        r, s = divmod(t, CB)
        present = pattern[s, r] != 0
        slot = jnp.minimum(count, CAP - 1)

        @pl.when(present)
        def _():
            place = pl.multiple_of(slot * TILE, TILE)
            tile = matrix[r * TILE:(r + 1) * TILE, s * TILE:(s + 1) * TILE]
            for out in outs:
                for i in range(out.shape[0]):
                    out[i, pl.ds(place, TILE), :] = tile

        slots = jnp.where((lane == t) & present, slot, slots)
        count = count + present.astype(jnp.int32)
    head = slots.astype(jnp.float32).astype(jnp.bfloat16)
    for out in outs:
        for i in range(out.shape[0]):
            out[i, CAP * TILE:PACK, :] = head


def pack(matrix, pattern, copies):
    return pl.pallas_call(
        pack_kernel,
        out_shape=tuple(jax.ShapeDtypeStruct((n, PACK, TILE), jnp.bfloat16) for n in copies),
        in_specs=[SMEM, VMEM],
        out_specs=(VMEM,) * len(copies),
        name="pack_tiles",
    )(pattern.T, matrix)


def tile_of(ref, lead, table, row, t):
    slot = table[row, t]
    start = pl.multiple_of(jnp.minimum(slot, CAP - 1) * TILE, TILE)
    tile = ref[(*lead, pl.ds(start, TILE), slice(None))]
    return jnp.where(slot < CAP, tile, jnp.zeros_like(tile))


def read_slots(blocks, meta, table, sem):
    for i, (ref, lead) in enumerate(blocks):
        head = ref[(*lead, pl.ds(CAP * TILE, META), slice(None))]
        meta[i:i + 1, :] = head.astype(jnp.float32).astype(jnp.int32)[0:1]
    copy = pltpu.make_async_copy(meta, table, sem)
    copy.start()
    copy.wait()


def spread_band(band, table, chips, dense):
    nl = band.shape[1]
    for i, chip in enumerate(chips):
        for t in range(RB * CB):
            r, s = divmod(t, CB)
            k = (i * CB + s) * TILE
            dense[r * TILE:(r + 1) * TILE, k:k + TILE] = tile_of(band, (lax.div(chip, nl), lax.rem(chip, nl)), table, chip, t)


def spread_panel(panel, table, entry, core, owns):
    for z in range(2):
        for h, dense in enumerate(owns):
            owner = lax.rem(core + h, 2)
            for i in range(CB):
                for s in range(CB):
                    t = (owner * CB + i) * CB + s
                    at = (z * CB + i) * TILE
                    dense[at:at + TILE, s * TILE:(s + 1) * TILE] = tile_of(panel, (z,), table, entry + z, t)


def first_kernel(ny, place, mine, *rest):
    panels = dict(zip([j for j in range(ny) if j != ny // 2], rest[:ny - 1]))
    acc, spare, meta, table, a_dense, b_dense, sem = rest[ny - 1:]
    nx, nl = mine.shape[0], mine.shape[1]
    chips = nx * nl
    blocks = [(mine, (c // nl, c % nl)) for c in range(chips)]
    blocks += [(panel, (z,)) for panel in panels.values() for z in range(2)]
    read_slots(blocks, meta, table, sem)
    y, core = place[0], place[1]
    acc[...] = jnp.zeros_like(acc)
    for n, (j, panel) in enumerate(panels.items()):
        source = lax.rem(y - j + ny, ny)
        a, b = a_dense.at[n % 2], b_dense.at[n % 2]
        spread_panel(panel, table, chips + 2 * n, core, (b, spare.at[n]))
        spread_band(mine, table, (source, ny + source), a)
        acc[...] += jnp.dot(a[...], b[...], preferred_element_type=jnp.float32)


def second_kernel(ny, place, keep, mine, others, last, start, spare, out, totals, meta, table, a_dense, b_dense, acc, sem):
    nx, nl = mine.shape[0], mine.shape[1]
    chips = nx * nl
    y, core = place[0], place[1]
    source = lax.rem(y + ny // 2, ny)
    blocks = [(others, (c // nl, c % nl)) for c in range(chips)]
    blocks += [(last, (z,)) for z in range(2)]
    far = [source, ny + source]
    blocks += [(mine, (lax.div(chip, nl), lax.rem(chip, nl))) for chip in far]
    read_slots(blocks, meta, table, sem)
    own, other = b_dense.at[0], b_dense.at[1]
    spread_panel(last, table, chips, core, (own, other))
    for i, chip in enumerate(far):
        for t in range(RB * CB):
            r, s = divmod(t, CB)
            k = (i * CB + s) * TILE
            tile = tile_of(mine, (lax.div(chip, nl), lax.rem(chip, nl)), table, chips + 2 + i, t)
            a_dense[0, r * TILE:(r + 1) * TILE, k:k + TILE] = tile
    acc[...] = start[...] + jnp.dot(a_dense[0], own[...], preferred_element_type=jnp.float32)
    for n, j in enumerate([j for j in range(ny) if j != ny // 2] + [ny // 2]):
        source = lax.rem(y - j + ny, ny)
        a = a_dense.at[(n + 1) % 2]
        spread_band(others, table, (source, ny + source), a)
        b = spare[n] if n < ny - 1 else other[...]
        acc[...] += jnp.dot(a[...], b, preferred_element_type=jnp.float32)
    for s in range(CB):
        total = jnp.zeros((1, TILE), jnp.float32)
        for r in range(RB):
            at = (slice(r * TILE, (r + 1) * TILE), slice(s * TILE, (s + 1) * TILE))
            kept = acc[at] * keep[s, r].astype(jnp.float32)
            inflated = kept * kept
            out[at] = inflated
            total = total + jnp.sum(inflated, axis=0, keepdims=True)
        totals[:, s * TILE:(s + 1) * TILE] = total


def table_scratch(entries):
    return [pltpu.VMEM((entries, TILE), jnp.int32), pltpu.SMEM((entries, TILE), jnp.int32)]


HALF_COST = pl.CostEstimate(flops=2**30, bytes_accessed=2**23, transcendentals=0)
WIDE = (2, RB * TILE, 2 * CB * TILE)
DEEP = (2 * CB * TILE, CB * TILE)


def first_half(place, mine, panels):
    chips, ny = mine.shape[0] * mine.shape[1], len(panels) + 1
    return pl.pallas_call(
        functools.partial(first_kernel, ny),
        out_shape=(
            jax.ShapeDtypeStruct(BLOCK, jnp.float32),
            jax.ShapeDtypeStruct((ny - 1, *DEEP), jnp.bfloat16),
        ),
        in_specs=[SMEM] + [VMEM] * ny,
        out_specs=(VMEM, VMEM),
        scratch_shapes=table_scratch(chips + 2 * (ny - 1)) + [
            pltpu.VMEM(WIDE, jnp.bfloat16),
            pltpu.VMEM((2, *DEEP), jnp.bfloat16),
            pltpu.SemaphoreType.DMA,
        ],
        compiler_params=pltpu.CompilerParams(vmem_limit_bytes=24 * 2**20),
        cost_estimate=HALF_COST,
        name="first_half",
    )(place, mine, *panels)


def second_half(place, keep, mine, others, last, start, spare):
    chips, ny = mine.shape[0] * mine.shape[1], spare.shape[0] + 1
    return pl.pallas_call(
        functools.partial(second_kernel, ny),
        out_shape=(jax.ShapeDtypeStruct(BLOCK, jnp.float32), jax.ShapeDtypeStruct((1, CB * TILE), jnp.float32)),
        in_specs=[SMEM, SMEM] + [VMEM] * 5,
        out_specs=(VMEM, VMEM),
        scratch_shapes=table_scratch(chips + 4) + [
            pltpu.VMEM(WIDE, jnp.bfloat16),
            pltpu.VMEM((2, *DEEP), jnp.bfloat16),
            pltpu.VMEM(BLOCK, jnp.float32),
            pltpu.SemaphoreType.DMA,
        ],
        compiler_params=pltpu.CompilerParams(vmem_limit_bytes=24 * 2**20),
        cost_estimate=HALF_COST,
        name="second_half",
    )(place, keep.T, mine, others, last, start, spare)


def shifted(array, axis, by):
    n = lax.axis_size(axis)
    return lax.ppermute(array, axis, [(i, (i + by) % n) for i in range(n)])


def body(matrix, in_pattern, out_pattern):
    ny, nx, nl = lax.axis_size("y"), lax.axis_size("x"), lax.axis_size("zl")
    pair, copies = pack(matrix, in_pattern, (2, nl))
    own = lax.all_to_all(pair, "zh", 0, 0)
    line = lax.all_to_all(copies, "zl", 0, 0)
    up, down = [own], [own]
    for i in range(1, ny // 2):
        u, d = shifted(up[-1], "y", 1), shifted(down[-1], "y", -1)
        if i == 1:
            lines = jnp.broadcast_to(line, (nx, *line.shape))
            lines, u, d = lax.optimization_barrier((lines, u, d))
            mine = lax.all_to_all(lines, "x", 0, 0)
        elif i == ny // 2 - 1:
            mine, u, d = lax.optimization_barrier((mine, u, d))
        else:
            u, d = lax.optimization_barrier((u, d))
        up.append(u)
        down.append(d)
    last = shifted(up[-1], "y", 1)
    others = shifted(mine, "core", 1)
    place = jnp.stack([lax.axis_index(a) for a in ("y", "core")])
    start, spare = first_half(place, mine, [own] + up[1:] + down[:0:-1])
    inflated, totals = second_half(place, out_pattern, mine, others, last, start, spare)
    totals = totals + shifted(totals, "zh", 1)
    copies = jnp.broadcast_to(totals, (ny, totals.shape[1]))
    column_totals = jnp.sum(lax.all_to_all(copies, "y", 0, 0, tiled=True), axis=0, keepdims=True)
    scaled = inflated / column_totals * float(SIZES[0] * SIZES[1] * RB * TILE)
    return jnp.maximum(scaled - prune_level, 0.0).astype(jnp.bfloat16)


def solution(mesh):
    fine = Mesh(mesh.devices.reshape(SIZES), AXES)
    spec = P(BLK, GRP)
    return jax.shard_map(body, mesh=fine, in_specs=(spec,) * 3, out_specs=spec, check_vma=False)
```

time: 123 us -> 119 us (0.967)
  the two profiles are of different devices: /device:TPU:2 before, /device:TPU:1 now
where the time goes in v2:
time: 119 us; the launch traced here: 117 us
  starting transfers between devices  42.3 us (36%)
  blocking collectives  31.4 us (26%)
  waiting for transfers between devices  26.2 us (22%)
  Pallas kernels  11.2 us (9%)
  local copies, waits for them, and re-layouts  4.97 us (4%)
    ppermute x9, starting transfers between devices, shifted(): return lax.ppermute(array, axis, [(i, (i + by) % n) for i in range(n)])  30.6 us
    ppermute x9, waiting for transfers between devices, shifted(): return lax.ppermute(array, axis, [(i, (i + by) % n) for i in range(n)])  24.6 us
    all_to_all x1, blocking collectives, body(): own = lax.all_to_all(pair, 'zh', 0, 0)  18.9 us
    all_to_all x1, blocking collectives, body(): lax.all_to_all(copies, 'y', 0, 0, tiled=True)  12.5 us
    all_to_all x1, starting transfers between devices, body(): line = lax.all_to_all(copies, 'zl', 0, 0)  7.71 us
    pallas_call x1, Pallas kernels, second_half(): pl.pallas_call(functools.partial(second_kernel, ny), out_shape=(jax.Shape...  4.9 us
    pallas_call x1, Pallas kernels, first_half(): pl.pallas_call(functools.partial(first_kernel, ny), out_shape=(jax.ShapeD...  4.36 us
    all_to_all x1, starting transfers between devices, body(): mine = lax.all_to_all(lines, 'x', 0, 0)  4.03 us
  transfers between devices with their start and end apart: 11, of which 9 were waited for; matrix products, arithmetic and copies ran while one was open for 0% of the time, Pallas kernels for 4%

profile of v2, /device:TPU:1, one launch (start us, length us, event | category | flops | bytes accessed | tf_op | source)
XLA Modules:
  0.0 117.2 jit_solution(2056163468134949461)
XLA Ops:
  0.0 2.0 %pack_tiles.1 = (bf16[2,528,128]{2,1,0:T(8,128)(2,1)}, bf16[4,528,128]{2,1,0:T(8,128)(2,1)}) custom-call(s32[2,4]{1,0:T(2,128)} %bitcast.7, bf16[512,256]{1,0:T(8,128)(2,1)} %matrix.1), custom_call_target="tpu_custom_call" | custom-call | tf_op jit(solution)/shard_map/pack_tiles/pallas_call | solution.py:54
  2.0 18.9 %all_to_all.21.rest_0_ = bf16[2,528,128]{2,1,0:T(8,128)(2,1)S(1)} all-to-all(bf16[2,528,128]{2,1,0:T(8,128)(2,1)} %get-tuple-element.20), channel_id=1, replica_groups=mesh['zh'=2,'y'=8,'x'=4,'zl'=4,'core'=2] {'zh'}, dimensions={0} | all-to-all | bytes 540672 | tf_op jit(solution)/shard_map/all_to_all | solution.py:210
  20.9 7.7 %all-to-all-start = ((bf16[4,528,128]{2,1,0:T(8,128)(2,1)}), bf16[4,528,128]{2,1,0:T(8,128)(2,1)S(1)}, u32[]{:S(2)}, u32[]{:S(2)}) async-start(bf16[4,528,128]{2,1,0:T(8,128)(2,1)} %get-tuple-element.19), calls=%async_computation | async-start | bytes 1081344 | tf_op jit(solution)/shard_map/all_to_all | solution.py:211
  28.6 5.0 %collective-permute-start.1 = (bf16[2,528,128]{2,1,0:T(8,128)(2,1)S(1)}, bf16[2,528,128]{2,1,0:T(8,128)(2,1)S(1)}, u32[]{:S(2)}, u32[]{:S(2)}) collective-permute-start(bf16[2,528,128]{2,1,0:T(8,128)(2,1)S(1)} %all_to_all.21.rest_0_), channel_id=1, source_target_pairs={{0,224},{32,0},{64,32},{96,64},{128,96},{160,128},{192,160},{224,1... | collective-permute-start | bytes 811016 | tf_op jit(solution)/shard_map/ppermute | solution.py:204
  33.6 1.9 %collective-permute-start = (bf16[2,528,128]{2,1,0:T(8,128)(2,1)S(1)}, bf16[2,528,128]{2,1,0:T(8,128)(2,1)S(1)}, u32[]{:S(2)}, u32[]{:S(2)}) collective-permute-start(bf16[2,528,128]{2,1,0:T(8,128)(2,1)S(1)} %all_to_all.21.rest_0_), channel_id=1, source_target_pairs={{0,32},{32,64},{64,96},{96,128},{128,160},{160,192},{192,224},{224... | collective-permute-start | bytes 811016 | tf_op jit(solution)/shard_map/ppermute | solution.py:204
  35.5 3.1 %collective-permute-done.1.rest_6_ = bf16[2,528,128]{2,1,0:T(8,128)(2,1)S(1)} collective-permute-done((bf16[2,528,128]{2,1,0:T(8,128)(2,1)S(1)}, bf16[2,528,128]{2,1,0:T(8,128)(2,1)S(1)}, u32[]{:S(2)}, u32[]{:S(2)}) %collective-permute-start.1) | collective-permute-done | bytes 270368 | tf_op jit(solution)/shard_map/ppermute | solution.py:204
  38.6 5.0 %collective-permute-done.rest_1_ = bf16[2,528,128]{2,1,0:T(8,128)(2,1)S(1)} collective-permute-done((bf16[2,528,128]{2,1,0:T(8,128)(2,1)S(1)}, bf16[2,528,128]{2,1,0:T(8,128)(2,1)S(1)}, u32[]{:S(2)}, u32[]{:S(2)}) %collective-permute-start) | collective-permute-done | bytes 270368 | tf_op jit(solution)/shard_map/ppermute | solution.py:204
  43.6 0.0 all-to-all-done
  43.6 1.6 %broadcast_in_dim.4 = bf16[4,4,528,128]{3,2,1,0:T(8,128)(2,1)} broadcast(bf16[4,528,128]{2,1,0:T(8,128)(2,1)S(1)} %all-to-all-done), dimensions={1,2,3} | broadcast | bytes 2703360 | tf_op jit(solution)/shard_map/broadcast_in_dim | solution.py:216
  45.2 4.0 %all-to-all-start.2 = ((bf16[4,4,528,128]{3,2,1,0:T(8,128)(2,1)}), bf16[4,4,528,128]{3,2,1,0:T(8,128)(2,1)S(1)}, u32[]{:S(2)}, u32[]{:S(2)}) async-start(bf16[4,4,528,128]{3,2,1,0:T(8,128)(2,1)} %broadcast_in_dim.4), calls=%async_computation.2 | async-start | bytes 4325376 | tf_op jit(solution)/shard_map/all_to_all | solution.py:218
  49.3 0.0 copy-start.4
  49.3 2.5 %collective-permute-start.2 = (bf16[2,528,128]{2,1,0:T(8,128)(2,1)S(1)}, bf16[2,528,128]{2,1,0:T(8,128)(2,1)S(1)}, u32[]{:S(2)}, u32[]{:S(2)}) collective-permute-start(bf16[2,528,128]{2,1,0:T(8,128)(2,1)S(1)} %collective-permute-done.rest_1_), channel_id=1, source_target_pairs={{0,32},{32,64},{64,96},{96,128},{128,160},{160,192},{192,224},{224... | collective-permute-start | bytes 811016 | tf_op jit(solution)/shard_map/ppermute | solution.py:204
  51.8 4.1 %collective-permute-start.3 = (bf16[2,528,128]{2,1,0:T(8,128)(2,1)S(1)}, bf16[2,528,128]{2,1,0:T(8,128)(2,1)S(1)}, u32[]{:S(2)}, u32[]{:S(2)}) collective-permute-start(bf16[2,528,128]{2,1,0:T(8,128)(2,1)S(1)} %collective-permute-done.1.rest_6_), channel_id=1, source_target_pairs={{0,224},{32,0},{64,32},{96,64},{128,96},{160,128},{192,160},{224,1... | collective-permute-start | bytes 811016 | tf_op jit(solution)/shard_map/ppermute | solution.py:204
  55.9 2.3 %collective-permute-done.2.rest_2_ = bf16[2,528,128]{2,1,0:T(8,128)(2,1)S(1)} collective-permute-done((bf16[2,528,128]{2,1,0:T(8,128)(2,1)S(1)}, bf16[2,528,128]{2,1,0:T(8,128)(2,1)S(1)}, u32[]{:S(2)}, u32[]{:S(2)}) %collective-permute-start.2) | collective-permute-done | bytes 270368 | tf_op jit(solution)/shard_map/ppermute | solution.py:204
  58.2 1.5 %collective-permute-done.3.rest_5_ = bf16[2,528,128]{2,1,0:T(8,128)(2,1)S(1)} collective-permute-done((bf16[2,528,128]{2,1,0:T(8,128)(2,1)S(1)}, bf16[2,528,128]{2,1,0:T(8,128)(2,1)S(1)}, u32[]{:S(2)}, u32[]{:S(2)}) %collective-permute-start.3) | collective-permute-done | bytes 270368 | tf_op jit(solution)/shard_map/ppermute | solution.py:204
  59.7 3.3 %collective-permute-start.4 = (bf16[2,528,128]{2,1,0:T(8,128)(2,1)S(1)}, bf16[2,528,128]{2,1,0:T(8,128)(2,1)S(1)}, u32[]{:S(2)}, u32[]{:S(2)}) collective-permute-start(bf16[2,528,128]{2,1,0:T(8,128)(2,1)S(1)} %collective-permute-done.2.rest_2_), channel_id=1, source_target_pairs={{0,32},{32,64},{64,96},{96,128},{128,160},{160,192},{192,224},{224... | collective-permute-start | bytes 811016 | tf_op jit(solution)/shard_map/ppermute | solution.py:204
  63.0 3.5 %collective-permute-start.5 = (bf16[2,528,128]{2,1,0:T(8,128)(2,1)S(1)}, bf16[2,528,128]{2,1,0:T(8,128)(2,1)S(1)}, u32[]{:S(2)}, u32[]{:S(2)}) collective-permute-start(bf16[2,528,128]{2,1,0:T(8,128)(2,1)S(1)} %collective-permute-done.3.rest_5_), channel_id=1, source_target_pairs={{0,224},{32,0},{64,32},{96,64},{128,96},{160,128},{192,160},{224,1... | collective-permute-start | bytes 811016 | tf_op jit(solution)/shard_map/ppermute | solution.py:204
  66.5 2.2 %collective-permute-done.4.rest_3_ = bf16[2,528,128]{2,1,0:T(8,128)(2,1)S(1)} collective-permute-done((bf16[2,528,128]{2,1,0:T(8,128)(2,1)S(1)}, bf16[2,528,128]{2,1,0:T(8,128)(2,1)S(1)}, u32[]{:S(2)}, u32[]{:S(2)}) %collective-permute-start.4) | collective-permute-done | bytes 270368 | tf_op jit(solution)/shard_map/ppermute | solution.py:204
  68.7 0.0 copy-start
  68.7 0.7 copy-done
  69.4 2.2 %collective-permute-done.5.rest_4_ = bf16[2,528,128]{2,1,0:T(8,128)(2,1)S(1)} collective-permute-done((bf16[2,528,128]{2,1,0:T(8,128)(2,1)S(1)}, bf16[2,528,128]{2,1,0:T(8,128)(2,1)S(1)}, u32[]{:S(2)}, u32[]{:S(2)}) %collective-permute-start.5) | collective-permute-done | bytes 270368 | tf_op jit(solution)/shard_map/ppermute | solution.py:204
  71.7 0.0 copy-start.2
  71.7 0.7 copy-done.2
  72.4 1.7 %all-to-all-done.2.mine = bf16[4,4,528,128]{3,2,1,0:T(8,128)(2,1)S(1)} async-done(((bf16[4,4,528,128]{3,2,1,0:T(8,128)(2,1)}), bf16[4,4,528,128]{3,2,1,0:T(8,128)(2,1)S(1)}, u32[]{:S(2)}, u32[]{:S(2)}) %all-to-all-start.2) | async-done | bytes 2162720 | tf_op jit(solution)/shard_map/all_to_all | solution.py:218
  74.1 5.1 %collective-permute-start.6 = (bf16[4,4,528,128]{3,2,1,0:T(8,128)(2,1)S(1)}, bf16[4,4,528,128]{3,2,1,0:T(8,128)(2,1)}, u32[]{:S(2)}, u32[]{:S(2)}) collective-permute-start(bf16[4,4,528,128]{3,2,1,0:T(8,128)(2,1)S(1)} %all-to-all-done.2.mine), channel_id=1, source_target_pairs={{0,1},{1,0},{2,3},{3,2},{4,5},{5,4},{6,7},{7,6},{8,9},{9,8},{10,11... | collective-permute-start | bytes 6488072 | tf_op jit(solution)/shard_map/ppermute | solution.py:204
  79.2 3.2 %collective-permute-start.7 = (bf16[2,528,128]{2,1,0:T(8,128)(2,1)}, bf16[2,528,128]{2,1,0:T(8,128)(2,1)}, u32[]{:S(2)}, u32[]{:S(2)}) collective-permute-start(bf16[2,528,128]{2,1,0:T(8,128)(2,1)} %copy-done), channel_id=1, source_target_pairs={{0,32},{32,64},{64,96},{96,128},{128,160},{160,192},{192,224},{224... | collective-permute-start | bytes 811016 | tf_op jit(solution)/shard_map/ppermute | solution.py:204
  82.4 0.1 pad_add_fusion.place
  82.4 0.0 copy-start.1
  82.5 1.0 copy-done.1
  83.4 0.0 copy-start.3
  83.4 1.0 copy-done.3
  84.4 4.4 %first_half.1 = (f32[512,256]{1,0:T(8,128)S(1)}, bf16[7,512,256]{2,1,0:T(8,128)(2,1)S(1)}) custom-call(s32[2]{0:T(128)S(1)} %pad_add_fusion.place, bf16[4,4,528,128]{3,2,1,0:T(8,128)(2,1)S(1)} %all-to-all-done.2.mine, bf16[2,528,128]{2,1,0:T(8,128)(2,1)S(1)} %all_to_all.21.rest_0_, bf16[2,528,128]{2,1,0:T(8,128)(2,1)S(1)} %collective-permute-done.rest_1_, ...), custom_call_target="tpu_custom_call" | custom-call | flops 1073741824 | bytes 8388608 | tf_op jit(solution)/shard_map/first_half/pallas_call | solution.py:164
  88.7 2.0 %collective-permute-done.7.last = bf16[2,528,128]{2,1,0:T(8,128)(2,1)} collective-permute-done((bf16[2,528,128]{2,1,0:T(8,128)(2,1)}, bf16[2,528,128]{2,1,0:T(8,128)(2,1)}, u32[]{:S(2)}, u32[]{:S(2)}) %collective-permute-start.7) | collective-permute-done | bytes 270368 | tf_op jit(solution)/shard_map/ppermute | solution.py:204
  90.7 0.0 collective-permute-done.6.others
  90.7 0.0 copy-done.4
  90.7 4.9 %second_half.1 = (f32[512,256]{1,0:T(8,128)S(1)}, f32[1,256]{1,0:T(1,128)S(1)}) custom-call(s32[2]{0:T(128)S(1)} %pad_add_fusion.place, s32[2,4]{1,0:T(2,128)S(1)} %bitcast.5, bf16[4,4,528,128]{3,2,1,0:T(8,128)(2,1)S(1)} %all-to-all-done.2.mine, bf16[4,4,528,128]{3,2,1,0:T(8,128)(2,1)} %collective-permute-done.6.others, ...), custom_call_target="tpu_custom_call" | custom-call | flops 1073741824 | bytes 8388608 | tf_op jit(solution)/shard_map/second_half/pallas_call | solution.py:185
  95.6 1.9 %collective-permute-start.8 = (f32[1,256]{1,0:T(1,128)S(1)}, f32[1,256]{1,0:T(1,128)S(1)}, u32[]{:S(2)}, u32[]{:S(2)}) collective-permute-start(f32[1,256]{1,0:T(1,128)S(1)} %get-tuple-element.32), channel_id=1, source_target_pairs={{0,256},{256,0},{1,257},{257,1},{2,258},{258,2},{3,259},{259,3},{4... | collective-permute-start | bytes 3080 | tf_op jit(solution)/shard_map/ppermute | solution.py:204
  97.5 6.3 %collective-permute-done.8 = f32[1,256]{1,0:T(1,128)S(1)} collective-permute-done((f32[1,256]{1,0:T(1,128)S(1)}, f32[1,256]{1,0:T(1,128)S(1)}, u32[]{:S(2)}, u32[]{:S(2)}) %collective-permute-start.8) | collective-permute-done | bytes 1056 | tf_op jit(solution)/shard_map/ppermute | solution.py:204
  103.8 12.5 %all_to_all.22 = f32[8,1,256]{2,1,0:T(1,128)S(1)} all-to-all(f32[8,1,256]{2,1,0:T(1,128)S(1)} %broadcast_in_dim.10), channel_id=1, replica_groups=mesh['zh'=2,'y'=8,'x'=4,'zl'=4,'core'=2] {'y'}, dimensions={0} | all-to-all | bytes 16384 | tf_op jit(solution)/shard_map/all_to_all | solution.py:232
  116.4 0.8 maximum_convert_fusion
  (3 shorter events, 0.0 us)
Async XLA Ops:
  20.9 22.7 %all-to-all-start = ((bf16[4,528,128]{2,1,0:T(8,128)(2,1)}), bf16[4,528,128]{2,1,0:T(8,128)(2,1)S(1)}, u32[]{:S(2)}, u32[]{:S(2)}) async-start(bf16[4,528,128]{2,1,0:T(8,128)(2,1)} %get-tuple-element.19), calls=%async_computation | async-start | bytes 1081344 | tf_op jit(solution)/shard_map/all_to_all | solution.py:211
  28.6 10.0 %collective-permute-start.1 = (bf16[2,528,128]{2,1,0:T(8,128)(2,1)S(1)}, bf16[2,528,128]{2,1,0:T(8,128)(2,1)S(1)}, u32[]{:S(2)}, u32[]{:S(2)}) collective-permute-start(bf16[2,528,128]{2,1,0:T(8,128)(2,1)S(1)} %all_to_all.21.rest_0_), channel_id=1, source_target_pairs={{0,224},{32,0},{64,32},{96,64},{128,96},{160,128},{192,160},{224,1... | collective-permute-start | bytes 811016 | tf_op jit(solution)/shard_map/ppermute | solution.py:204
  33.6 10.0 %collective-permute-start = (bf16[2,528,128]{2,1,0:T(8,128)(2,1)S(1)}, bf16[2,528,128]{2,1,0:T(8,128)(2,1)S(1)}, u32[]{:S(2)}, u32[]{:S(2)}) collective-permute-start(bf16[2,528,128]{2,1,0:T(8,128)(2,1)S(1)} %all_to_all.21.rest_0_), channel_id=1, source_target_pairs={{0,32},{32,64},{64,96},{96,128},{128,160},{160,192},{192,224},{224... | collective-permute-start | bytes 811016 | tf_op jit(solution)/shard_map/ppermute | solution.py:204
  45.2 28.8 %all-to-all-start.2 = ((bf16[4,4,528,128]{3,2,1,0:T(8,128)(2,1)}), bf16[4,4,528,128]{3,2,1,0:T(8,128)(2,1)S(1)}, u32[]{:S(2)}, u32[]{:S(2)}) async-start(bf16[4,4,528,128]{3,2,1,0:T(8,128)(2,1)} %broadcast_in_dim.4), calls=%async_computation.2 | async-start | bytes 4325376 | tf_op jit(solution)/shard_map/all_to_all | solution.py:218
  49.3 41.4 %copy-start.4 = (s32[4,2]{0,1:T(2,128)S(1)}, s32[4,2]{0,1:T(2,128)}, u32[]{:S(2)}) copy-start(s32[4,2]{0,1:T(2,128)} %param.5) | copy-start | bytes 100
  49.3 8.9 %collective-permute-start.2 = (bf16[2,528,128]{2,1,0:T(8,128)(2,1)S(1)}, bf16[2,528,128]{2,1,0:T(8,128)(2,1)S(1)}, u32[]{:S(2)}, u32[]{:S(2)}) collective-permute-start(bf16[2,528,128]{2,1,0:T(8,128)(2,1)S(1)} %collective-permute-done.rest_1_), channel_id=1, source_target_pairs={{0,32},{32,64},{64,96},{96,128},{128,160},{160,192},{192,224},{224... | collective-permute-start | bytes 811016 | tf_op jit(solution)/shard_map/ppermute | solution.py:204
  51.8 7.9 %collective-permute-start.3 = (bf16[2,528,128]{2,1,0:T(8,128)(2,1)S(1)}, bf16[2,528,128]{2,1,0:T(8,128)(2,1)S(1)}, u32[]{:S(2)}, u32[]{:S(2)}) collective-permute-start(bf16[2,528,128]{2,1,0:T(8,128)(2,1)S(1)} %collective-permute-done.1.rest_6_), channel_id=1, source_target_pairs={{0,224},{32,0},{64,32},{96,64},{128,96},{160,128},{192,160},{224,1... | collective-permute-start | bytes 811016 | tf_op jit(solution)/shard_map/ppermute | solution.py:204
  59.7 9.0 %collective-permute-start.4 = (bf16[2,528,128]{2,1,0:T(8,128)(2,1)S(1)}, bf16[2,528,128]{2,1,0:T(8,128)(2,1)S(1)}, u32[]{:S(2)}, u32[]{:S(2)}) collective-permute-start(bf16[2,528,128]{2,1,0:T(8,128)(2,1)S(1)} %collective-permute-done.2.rest_2_), channel_id=1, source_target_pairs={{0,32},{32,64},{64,96},{96,128},{128,160},{160,192},{192,224},{224... | collective-permute-start | bytes 811016 | tf_op jit(solution)/shard_map/ppermute | solution.py:204
  63.0 8.7 %collective-permute-start.5 = (bf16[2,528,128]{2,1,0:T(8,128)(2,1)S(1)}, bf16[2,528,128]{2,1,0:T(8,128)(2,1)S(1)}, u32[]{:S(2)}, u32[]{:S(2)}) collective-permute-start(bf16[2,528,128]{2,1,0:T(8,128)(2,1)S(1)} %collective-permute-done.3.rest_5_), channel_id=1, source_target_pairs={{0,224},{32,0},{64,32},{96,64},{128,96},{160,128},{192,160},{224,1... | collective-permute-start | bytes 811016 | tf_op jit(solution)/shard_map/ppermute | solution.py:204
  68.7 0.7 copy-start
  71.7 0.7 copy-start.2
  74.1 16.6 %collective-permute-start.6 = (bf16[4,4,528,128]{3,2,1,0:T(8,128)(2,1)S(1)}, bf16[4,4,528,128]{3,2,1,0:T(8,128)(2,1)}, u32[]{:S(2)}, u32[]{:S(2)}) collective-permute-start(bf16[4,4,528,128]{3,2,1,0:T(8,128)(2,1)S(1)} %all-to-all-done.2.mine), channel_id=1, source_target_pairs={{0,1},{1,0},{2,3},{3,2},{4,5},{5,4},{6,7},{7,6},{8,9},{9,8},{10,11... | collective-permute-start | bytes 6488072 | tf_op jit(solution)/shard_map/ppermute | solution.py:204
  79.2 11.5 %collective-permute-start.7 = (bf16[2,528,128]{2,1,0:T(8,128)(2,1)}, bf16[2,528,128]{2,1,0:T(8,128)(2,1)}, u32[]{:S(2)}, u32[]{:S(2)}) collective-permute-start(bf16[2,528,128]{2,1,0:T(8,128)(2,1)} %copy-done), channel_id=1, source_target_pairs={{0,32},{32,64},{64,96},{96,128},{128,160},{160,192},{192,224},{224... | collective-permute-start | bytes 811016 | tf_op jit(solution)/shard_map/ppermute | solution.py:204
  82.4 1.0 copy-start.1
  83.4 1.0 copy-start.3
  95.6 8.2 %collective-permute-start.8 = (f32[1,256]{1,0:T(1,128)S(1)}, f32[1,256]{1,0:T(1,128)S(1)}, u32[]{:S(2)}, u32[]{:S(2)}) collective-permute-start(f32[1,256]{1,0:T(1,128)S(1)} %get-tuple-element.32), channel_id=1, source_target_pairs={{0,256},{256,0},{1,257},{257,1},{2,258},{258,2},{3,259},{259,3},{4... | collective-permute-start | bytes 3080 | tf_op jit(solution)/shard_map/ppermute | solution.py:204

commit v3 on v1

v3 whole, which is shorter than its diff:
```python
import functools

import jax
import jax.numpy as jnp
from jax import lax
from jax.experimental import pallas as pl
from jax.experimental.pallas import tpu as pltpu
from jax.sharding import Mesh, PartitionSpec as P

prune_level = 0.5
TILE = 128
RB = 4
CB = 2
CAP = 4
HEAD = 16
SIGNS = 4
LEAST = 2.0**-126
PACK = CAP * TILE
AXES = ("zh", "y", "x", "zl", "core")
SIZES = (2, 8, 4, 4, 2)
BLK = ("zh", "y")
GRP = ("x", "zl", "core")


SMEM = pl.BlockSpec(memory_space=pltpu.SMEM)
VMEM = pl.BlockSpec(memory_space=pltpu.VMEM)
BLOCK = (RB * TILE, CB * TILE)


def pack_kernel(pattern, matrix, out):
    lane = lax.broadcasted_iota(jnp.int32, (HEAD, TILE), 1)
    row = lax.broadcasted_iota(jnp.int32, (HEAD, TILE), 0)
    signs = (row == 0) & (lane < SIGNS)
    for slot in range(CAP):
        out[0, slot * TILE:slot * TILE + HEAD, :] = jnp.ones((HEAD, TILE), jnp.bfloat16)
    count = jnp.int32(0)
    for t in range(RB * CB):
        r, s = divmod(t, CB)
        present = pattern[s, r] != 0
        slot = jnp.minimum(count, CAP - 1)

        @pl.when(present)
        def _():
            place = pl.multiple_of(slot * TILE, TILE)
            tile = matrix[r * TILE:(r + 1) * TILE, s * TILE:(s + 1) * TILE]
            head = tile[:HEAD].astype(jnp.float32)
            size = jnp.maximum(head, LEAST)
            bit = lax.shift_right_logical(jnp.full_like(lane, t + RB * CB), jnp.minimum(lane, SIGNS)) & 1
            head = jnp.where(signs, jnp.where(bit == 1, -size, size), head)
            out[0, pl.ds(place, HEAD), :] = head.astype(jnp.bfloat16)
            out[0, pl.ds(pl.multiple_of(place + HEAD, HEAD), TILE - HEAD), :] = tile[HEAD:]

        count = count + present.astype(jnp.int32)


def pack(matrix, pattern):
    return pl.pallas_call(
        pack_kernel,
        out_shape=jax.ShapeDtypeStruct((1, PACK, TILE), jnp.bfloat16),
        in_specs=[SMEM, VMEM],
        out_specs=VMEM,
        name="pack_tiles",
    )(pattern.T, matrix)


def put_tile(dense, at, ref, lead, table, row, t):
    slot = table[row, t]
    start = pl.multiple_of(jnp.minimum(slot, CAP - 1) * TILE, TILE)
    head = jnp.abs(ref[(*lead, pl.ds(start, HEAD), slice(None))])
    rest = ref[(*lead, pl.ds(pl.multiple_of(start + HEAD, HEAD), TILE - HEAD), slice(None))]
    r, c = at
    dense[r:r + HEAD, c:c + TILE] = jnp.where(slot < CAP, head, jnp.zeros_like(head))
    dense[r + HEAD:r + TILE, c:c + TILE] = jnp.where(slot < CAP, rest, jnp.zeros_like(rest))


def read_slots(blocks, heads, meta, table, sem):
    for i, (ref, lead) in enumerate(blocks):
        for slot in range(CAP):
            head = ref[(*lead, pl.ds(slot * TILE, HEAD), slice(None))].astype(jnp.float32)
            heads[slot, i:i + 1, :] = head[0:1]
    lane = lax.broadcasted_iota(jnp.int32, meta.shape, 1)
    weight = jnp.where(lane < SIGNS, lax.shift_left(jnp.ones_like(lane), jnp.minimum(lane, SIGNS)), 0)
    slots = jnp.full(meta.shape, CAP, jnp.int32)
    for slot in range(CAP):
        code = jnp.sum(jnp.where(heads[slot] < 0, weight, 0), axis=1, keepdims=True)
        slots = jnp.where(code == lane + RB * CB, slot, slots)
    meta[...] = slots
    copy = pltpu.make_async_copy(meta, table, sem)
    copy.start()
    copy.wait()


def spread_band(band, table, entries, places, dense, col):
    for i, (entry, lead) in enumerate(zip(entries, places)):
        for t in range(RB * CB):
            r, s = divmod(t, CB)
            k = col + (i * CB + s) * TILE
            put_tile(dense, (r * TILE, k), band, lead, table, entry, t)


def spread_panel(panel, table, entry, core, owns):
    for z in range(2):
        for h, (dense, row) in enumerate(owns):
            owner = lax.rem(core + h, 2)
            for i in range(CB):
                for s in range(CB):
                    t = (owner * CB + i) * CB + s
                    at = row + (z * CB + i) * TILE
                    put_tile(dense, (at, s * TILE), panel, (z,), table, entry + z, t)


def sources(hi, y, ny, nl, js):
    for j in js:
        source = lax.rem(y - j + ny, ny)
        chips = (hi * ny + source, (1 - hi) * ny + source)
        yield chips, [(lax.div(chip, nl), lax.rem(chip, nl)) for chip in chips]


def all_blocks(band):
    return [(band, (x, k)) for x in range(band.shape[0]) for k in range(band.shape[1])]


def own_kernel(ny, js, far, place, mine, *rest):
    panels, rest = rest[:len(js)], rest[len(js):]
    start, rest = (rest[0], rest[1:]) if far else (None, rest)
    acc, spare, rest = rest[0], rest[1], rest[2:]
    far_dense, rest = (rest[0], rest[1:]) if far else (None, rest)
    heads, meta, table, a_dense, b_dense, sem = rest
    hi, y, core = place[0], place[1], place[2]
    nl = mine.shape[1]
    blocks = all_blocks(mine)
    chips = len(blocks)
    blocks += [(panel, (z,)) for panel in panels for z in range(2)]
    read_slots(blocks, heads, meta, table, sem)
    for n, (entries, places) in enumerate(sources(hi, y, ny, nl, js)):
        spread_panel(panels[n], table, chips + 2 * n, core, ((b_dense, n * DEEP), (spare, n * DEEP)))
        spread_band(mine, table, entries, places, a_dense, n * DEEP)
    total = jnp.dot(a_dense[...], b_dense[...], preferred_element_type=jnp.float32)
    acc[...] = total if start is None else start[...] + total
    if far:
        ((entries, places),) = sources(hi, y, ny, nl, [ny // 2])
        spread_band(mine, table, entries, places, far_dense, 0)


def other_kernel(ny, order, place, others, start, *rest):
    spares, (acc, far_dense, heads, meta, table, a_dense, sem) = rest[:len(order)], rest[len(order):]
    hi, y = place[0], place[1]
    nl = others.shape[1]
    read_slots(all_blocks(others), heads, meta, table, sem)
    total = start[...]
    col = 0
    for js, spare in zip(order, spares):
        depth = len(js) * DEEP
        for n, (entries, places) in enumerate(sources(hi, y, ny, nl, js)):
            spread_band(others, table, entries, places, a_dense, col + n * DEEP)
        total += jnp.dot(a_dense[:, col:col + depth], spare[...], preferred_element_type=jnp.float32)
        col += depth
    acc[...] = total
    ((entries, places),) = sources(hi, y, ny, nl, [ny // 2])
    spread_band(others, table, entries, places, far_dense, 0)


def last_kernel(place, keep, last, start, far_mine, far_others, out, totals, heads, meta, table, b_dense, acc, sem):
    core = place[2]
    read_slots([(last, (z,)) for z in range(2)], heads, meta, table, sem)
    mine_rows, others_rows = b_dense.at[pl.ds(0, DEEP)], b_dense.at[pl.ds(DEEP, DEEP)]
    spread_panel(last, table, 0, core, ((mine_rows, 0), (others_rows, 0)))
    total = start[...] + jnp.dot(far_mine[...], mine_rows[...], preferred_element_type=jnp.float32)
    acc[...] = total + jnp.dot(far_others[...], others_rows[...], preferred_element_type=jnp.float32)
    for s in range(CB):
        total = jnp.zeros((1, TILE), jnp.float32)
        for r in range(RB):
            at = (slice(r * TILE, (r + 1) * TILE), slice(s * TILE, (s + 1) * TILE))
            kept = acc[at] * keep[s, r].astype(jnp.float32)
            inflated = kept * kept
            out[at] = inflated
            total = total + jnp.sum(inflated, axis=0, keepdims=True)
        totals[:, s * TILE:(s + 1) * TILE] = total


def scratch(entries, *more):
    return [
        pltpu.VMEM((CAP, entries, TILE), jnp.float32),
        pltpu.VMEM((entries, TILE), jnp.int32),
        pltpu.SMEM((entries, TILE), jnp.int32),
        *more,
        pltpu.SemaphoreType.DMA,
    ]


def kernel_call(kernel, name, outs, smems, vmems, scratch_shapes):
    return pl.pallas_call(
        kernel,
        out_shape=outs,
        in_specs=[SMEM] * len(smems) + [VMEM] * len(vmems),
        out_specs=jax.tree.map(lambda _: VMEM, outs),
        scratch_shapes=scratch_shapes,
        compiler_params=pltpu.CompilerParams(vmem_limit_bytes=24 * 2**20),
        cost_estimate=pl.CostEstimate(flops=2**35, bytes_accessed=2**23, transcendentals=0),
        name=name,
    )(*smems, *vmems)


DEEP = 2 * CB * TILE
BLOCK_SUM = jax.ShapeDtypeStruct(BLOCK, jnp.float32)
FAR = jax.ShapeDtypeStruct((RB * TILE, DEEP), jnp.bfloat16)


def rows_of(count):
    return (count * DEEP, CB * TILE)


def own_part(ny, js, place, mine, panels, start=None):
    chips = mine.shape[0] * mine.shape[1]
    far = start is not None
    outs = (BLOCK_SUM, jax.ShapeDtypeStruct(rows_of(len(js)), jnp.bfloat16)) + ((FAR,) if far else ())
    shapes = scratch(
        chips + 2 * len(js),
        pltpu.VMEM((RB * TILE, len(js) * DEEP), jnp.bfloat16),
        pltpu.VMEM(rows_of(len(js)), jnp.bfloat16),
    )
    arrays = [mine, *panels] + ([start] if far else [])
    return kernel_call(functools.partial(own_kernel, ny, js, far), "own_part", outs, [place], arrays, shapes)


def other_part(ny, order, place, others, start, spares):
    chips = others.shape[0] * others.shape[1]
    shapes = scratch(chips, pltpu.VMEM((RB * TILE, sum(map(len, order)) * DEEP), jnp.bfloat16))
    arrays = [others, start, *spares]
    return kernel_call(functools.partial(other_kernel, ny, order), "other_part", (BLOCK_SUM, FAR), [place], arrays, shapes)


def last_part(place, keep, last, start, far_mine, far_others):
    outs = (BLOCK_SUM, jax.ShapeDtypeStruct((1, CB * TILE), jnp.float32))
    shapes = scratch(2, pltpu.VMEM(rows_of(2), jnp.bfloat16), pltpu.VMEM(BLOCK, jnp.float32))
    arrays = [last, start, far_mine, far_others]
    return kernel_call(last_kernel, "last_part", outs, [place, keep.T], arrays, shapes)


def shifted(array, axis, by):
    n = lax.axis_size(axis)
    return lax.ppermute(array, axis, [(i, (i + by) % n) for i in range(n)])


def body(matrix, in_pattern, out_pattern):
    ny, nx, nl = lax.axis_size("y"), lax.axis_size("x"), lax.axis_size("zl")
    packed = pack(matrix, in_pattern)
    other = shifted(packed, "zh", 1)
    line = lax.all_gather(packed, "zl", tiled=True)
    line, other = lax.optimization_barrier((line, other))
    own = jnp.concatenate([packed, other])
    mine = lax.all_to_all(jnp.broadcast_to(line, (nx, *line.shape)), "x", 0, 0)
    place = jnp.stack([lax.axis_index(a) for a in ("zh", "y", "core")])
    half = ny // 2
    panels = {0: own}
    for i in range(1, half):
        panels[i] = shifted(panels[i - 1], "y", 1)
        panels[ny - i] = shifted(panels[(ny - i + 1) % ny], "y", -1)
    early = [j for j in range(ny) if min(j, ny - j) < half - 1]
    late = [half - 1, half + 1]
    start, spare = own_part(ny, early, place, mine, [panels[j] for j in early])
    sent, _, _ = lax.optimization_barrier((mine, panels[half - 2], panels[half + 2]))
    others = shifted(sent, "core", 1)
    last = shifted(panels[half - 1], "y", 1)
    start, late_spare, far_mine = own_part(ny, late, place, mine, [panels[j] for j in late], start)
    start, far_others = other_part(ny, [early, late], place, others, start, [spare, late_spare])
    inflated, totals = last_part(place, out_pattern, last, start, far_mine, far_others)
    totals = totals + shifted(totals, "zh", 1)
    copies = jnp.broadcast_to(totals, (ny, totals.shape[1]))
    column_totals = jnp.sum(lax.all_to_all(copies, "y", 0, 0, tiled=True), axis=0, keepdims=True)
    scaled = inflated / column_totals * float(SIZES[0] * SIZES[1] * RB * TILE)
    return jnp.maximum(scaled - prune_level, 0.0).astype(jnp.bfloat16)


def solution(mesh):
    fine = Mesh(mesh.devices.reshape(SIZES), AXES)
    spec = P(BLK, GRP)
    return jax.shard_map(body, mesh=fine, in_specs=(spec,) * 3, out_specs=spec, check_vma=False)
```

time: 123 us -> 109 us (0.89)
  waiting for transfers between devices: 34.9 us -> 14.8 us
  between operations: 13.5 us -> 0.18 us
  starting transfers between devices: 34.2 us -> 43.5 us
  blocking collectives: 25.8 us -> 34 us
  Pallas kernels: 8.41 us -> 13.5 us
  local copies, waits for them, and re-layouts: 4.34 us -> 1.76 us
    psum x2 -> x0, blocking collectives: 25.8 us -> none  [body(): column_totals = lax.psum(lax.psum(totals, 'zh'), 'y')]
    all_gather x0 -> x1, blocking collectives: none -> 18.8 us  [body(): line = lax.all_gather(packed, 'zl', tiled=True)]
    all_to_all x0 -> x1, blocking collectives: none -> 15.2 us  [body(): lax.all_to_all(copies, 'y', 0, 0, tiled=True)]
    all_gather x1 -> x0, waiting for transfers between devices: 14.8 us -> none  [body(): band = lax.all_gather(packed, GRP)]
    ppermute x8 -> x10, waiting for transfers between devices: 20.1 us -> 14.8 us  [shifted(): return lax.ppermute(array, axis, [(i, (i + by) % n) for i in range(n)])]
    pallas_call x2 -> x5, Pallas kernels: 8.41 us -> 13.5 us  [the longest x4 11.8 us: kernel_call(): pl.pallas_call(kernel, out_shape=outs, in_specs=[SMEM] * len(smems) + [VM...]
    all_to_all x0 -> x1, starting transfers between devices: none -> 4.92 us  [body(): mine = lax.all_to_all(jnp.broadcast_to(line, (nx, *line.shape)), 'x', 0, 0)]
    unnamed x4, local copies, waits for them, and re-layouts: 4.34 us -> 0.01 us
  transfers between devices with their start and end apart: 9 -> 11, of which waited for: 6 -> 4; matrix products, arithmetic and copies ran while one was open for 1% -> 0% of each run, Pallas kernels for 0% -> 9%
where the time goes in v3:
time: 109 us
  starting transfers between devices  43.5 us (40%)
  blocking collectives  34 us (31%)
  waiting for transfers between devices  14.8 us (14%)
  Pallas kernels  13.5 us (12%)
  local copies, waits for them, and re-layouts  1.76 us (2%)
    ppermute x10, starting transfers between devices, shifted(): return lax.ppermute(array, axis, [(i, (i + by) % n) for i in range(n)])  38.5 us
    all_gather x1, blocking collectives, body(): line = lax.all_gather(packed, 'zl', tiled=True)  18.8 us
    all_to_all x1, blocking collectives, body(): lax.all_to_all(copies, 'y', 0, 0, tiled=True)  15.2 us
    ppermute x10, waiting for transfers between devices, shifted(): return lax.ppermute(array, axis, [(i, (i + by) % n) for i in range(n)])  14.8 us
    pallas_call x4, Pallas kernels, kernel_call(): pl.pallas_call(kernel, out_shape=outs, in_specs=[SMEM] * len(smems) + [VM...  11.8 us
    all_to_all x1, starting transfers between devices, body(): mine = lax.all_to_all(jnp.broadcast_to(line, (nx, *line.shape)), 'x', 0, 0)  4.92 us
  transfers between devices with their start and end apart: 11, of which 4 were waited for; matrix products, arithmetic and copies ran while one was open for 0% of the time, Pallas kernels for 9%

profile of v3, /device:TPU:2, one launch (start us, length us, event | category | flops | bytes accessed | tf_op | source)
XLA Modules:
  0.0 108.6 jit_solution(362804881226452439)
XLA Ops:
  0.0 1.7 %pack_tiles.1 = bf16[1,512,128]{2,1,0:T(8,128)(2,1)} custom-call(s32[2,4]{1,0:T(2,128)} %bitcast.8, bf16[512,256]{1,0:T(8,128)(2,1)} %matrix.1), custom_call_target="tpu_custom_call" | custom-call | tf_op jit(solution)/shard_map/pack_tiles/pallas_call | solution.py:57
  1.7 10.9 %collective-permute-start = (bf16[1,512,128]{2,1,0:T(8,128)(2,1)}, bf16[1,512,128]{2,1,0:T(8,128)(2,1)S(1)}, u32[]{:S(2)}, u32[]{:S(2)}) collective-permute-start(bf16[1,512,128]{2,1,0:T(8,128)(2,1)} %pack_tiles.1), channel_id=1, source_target_pairs={{0,256},{256,0},{1,257},{257,1},{2,258},{258,2},{3,259},{259,3},{4... | collective-permute-start | bytes 393224 | tf_op jit(solution)/shard_map/ppermute | solution.py:242
  12.6 18.8 %all_gather.3 = bf16[4,512,128]{2,1,0:T(8,128)(2,1)S(1)} all-gather(bf16[1,512,128]{2,1,0:T(8,128)(2,1)} %pack_tiles.1), channel_id=1, replica_groups=mesh['zh'=2,'y'=8,'x'=4,'zl'=4,'core'=2] {'zl'}, dimensions={0}, use_global_device_ids=true | all-gather | bytes 655360 | tf_op jit(solution)/shard_map/all_gather | solution.py:249
  31.4 0.0 collective-permute-done
  31.4 1.7 %broadcast_in_dim.4 = bf16[4,4,512,128]{3,2,1,0:T(8,128)(2,1)} broadcast(bf16[4,512,128]{2,1,0:T(8,128)(2,1)S(1)} %all_gather.3), dimensions={1,2,3} | broadcast | bytes 2621440 | tf_op jit(solution)/shard_map/broadcast_in_dim | solution.py:252
  33.1 0.0 copy-start.1
  33.1 4.9 %all-to-all-start = ((bf16[4,4,512,128]{3,2,1,0:T(8,128)(2,1)}), bf16[4,4,512,128]{3,2,1,0:T(8,128)(2,1)S(1)}, u32[]{:S(2)}, u32[]{:S(2)}) async-start(bf16[4,4,512,128]{3,2,1,0:T(8,128)(2,1)} %broadcast_in_dim.4), calls=%async_computation | async-start | bytes 4194304 | tf_op jit(solution)/shard_map/all_to_all | solution.py:252
  38.1 0.0 copy-done.1
  38.1 3.5 %collective-permute-start.1 = (bf16[2,512,128]{2,1,0:T(8,128)(2,1)S(1)}, bf16[2,512,128]{2,1,0:T(8,128)(2,1)S(1)}, u32[]{:S(2)}, u32[]{:S(2)}) collective-permute-start(bf16[2,512,128]{2,1,0:T(8,128)(2,1)S(1)} %pad_maximum_fusion.rest_0_), channel_id=1, source_target_pairs={{0,32},{32,64},{64,96},{96,128},{128,160},{160,192},{192,224},{224... | collective-permute-start | bytes 786440 | tf_op jit(solution)/shard_map/ppermute | solution.py:242
  41.6 3.8 %collective-permute-start.5 = (bf16[2,512,128]{2,1,0:T(8,128)(2,1)S(1)}, bf16[2,512,128]{2,1,0:T(8,128)(2,1)S(1)}, u32[]{:S(2)}, u32[]{:S(2)}) collective-permute-start(bf16[2,512,128]{2,1,0:T(8,128)(2,1)S(1)} %pad_maximum_fusion.rest_0_), channel_id=1, source_target_pairs={{0,224},{32,0},{64,32},{96,64},{128,96},{160,128},{192,160},{224,1... | collective-permute-start | bytes 786440 | tf_op jit(solution)/shard_map/ppermute | solution.py:242
  45.4 2.4 %collective-permute-done.1.rest_1_ = bf16[2,512,128]{2,1,0:T(8,128)(2,1)S(1)} collective-permute-done((bf16[2,512,128]{2,1,0:T(8,128)(2,1)S(1)}, bf16[2,512,128]{2,1,0:T(8,128)(2,1)S(1)}, u32[]{:S(2)}, u32[]{:S(2)}) %collective-permute-start.1) | collective-permute-done | bytes 262176 | tf_op jit(solution)/shard_map/ppermute | solution.py:242
  47.8 2.0 %collective-permute-start.2 = (bf16[2,512,128]{2,1,0:T(8,128)(2,1)S(1)}, bf16[2,512,128]{2,1,0:T(8,128)(2,1)S(1)}, u32[]{:S(2)}, u32[]{:S(2)}) collective-permute-start(bf16[2,512,128]{2,1,0:T(8,128)(2,1)S(1)} %collective-permute-done.1.rest_1_), channel_id=1, source_target_pairs={{0,32},{32,64},{64,96},{96,128},{128,160},{160,192},{192,224},{224... | collective-permute-start | bytes 786440 | tf_op jit(solution)/shard_map/ppermute | solution.py:242
  49.9 0.0 collective-permute-done.5.rest_4_
  49.9 5.0 %collective-permute-start.6 = (bf16[2,512,128]{2,1,0:T(8,128)(2,1)S(1)}, bf16[2,512,128]{2,1,0:T(8,128)(2,1)}, u32[]{:S(2)}, u32[]{:S(2)}) collective-permute-start(bf16[2,512,128]{2,1,0:T(8,128)(2,1)S(1)} %collective-permute-done.5.rest_4_), channel_id=1, source_target_pairs={{0,224},{32,0},{64,32},{96,64},{128,96},{160,128},{192,160},{224,1... | collective-permute-start | bytes 786440 | tf_op jit(solution)/shard_map/ppermute | solution.py:242
  54.9 2.4 %collective-permute-done.2.rest_2_ = bf16[2,512,128]{2,1,0:T(8,128)(2,1)S(1)} collective-permute-done((bf16[2,512,128]{2,1,0:T(8,128)(2,1)S(1)}, bf16[2,512,128]{2,1,0:T(8,128)(2,1)S(1)}, u32[]{:S(2)}, u32[]{:S(2)}) %collective-permute-start.2) | collective-permute-done | bytes 262176 | tf_op jit(solution)/shard_map/ppermute | solution.py:242
  57.3 1.9 %collective-permute-start.3 = (bf16[2,512,128]{2,1,0:T(8,128)(2,1)S(1)}, bf16[2,512,128]{2,1,0:T(8,128)(2,1)S(1)}, u32[]{:S(2)}, u32[]{:S(2)}) collective-permute-start(bf16[2,512,128]{2,1,0:T(8,128)(2,1)S(1)} %collective-permute-done.2.rest_2_), channel_id=1, source_target_pairs={{0,32},{32,64},{64,96},{96,128},{128,160},{160,192},{192,224},{224... | collective-permute-start | bytes 786440 | tf_op jit(solution)/shard_map/ppermute | solution.py:242
  59.2 0.1 pad_add_fusion.place
  59.3 0.0 collective-permute-done.6.rest_3_
  59.3 5.2 %collective-permute-start.8 = (bf16[2,512,128]{2,1,0:T(8,128)(2,1)}, bf16[2,512,128]{2,1,0:T(8,128)(2,1)}, u32[]{:S(2)}, u32[]{:S(2)}) collective-permute-start(bf16[2,512,128]{2,1,0:T(8,128)(2,1)} %collective-permute-done.6.rest_3_), channel_id=1, source_target_pairs={{0,224},{32,0},{64,32},{96,64},{128,96},{160,128},{192,160},{224,1... | collective-permute-start | bytes 786440 | tf_op jit(solution)/shard_map/ppermute | solution.py:242
  64.5 3.0 %collective-permute-done.3.rest_0_ = bf16[2,512,128]{2,1,0:T(8,128)(2,1)S(1)} collective-permute-done((bf16[2,512,128]{2,1,0:T(8,128)(2,1)S(1)}, bf16[2,512,128]{2,1,0:T(8,128)(2,1)S(1)}, u32[]{:S(2)}, u32[]{:S(2)}) %collective-permute-start.3) | collective-permute-done | bytes 262176 | tf_op jit(solution)/shard_map/ppermute | solution.py:242
  67.4 1.9 %collective-permute-start.4 = (bf16[2,512,128]{2,1,0:T(8,128)(2,1)S(1)}, bf16[2,512,128]{2,1,0:T(8,128)(2,1)}, u32[]{:S(2)}, u32[]{:S(2)}) collective-permute-start(bf16[2,512,128]{2,1,0:T(8,128)(2,1)S(1)} %collective-permute-done.3.rest_0_), channel_id=1, source_target_pairs={{0,32},{32,64},{64,96},{96,128},{128,160},{160,192},{192,224},{224... | collective-permute-start | bytes 786440 | tf_op jit(solution)/shard_map/ppermute | solution.py:242
  69.3 0.0 all-to-all-done.mine
  69.4 1.9 %collective-permute-start.7 = (bf16[4,4,512,128]{3,2,1,0:T(8,128)(2,1)S(1)}, bf16[4,4,512,128]{3,2,1,0:T(8,128)(2,1)S(1)}, u32[]{:S(2)}, u32[]{:S(2)}) collective-permute-start(bf16[4,4,512,128]{3,2,1,0:T(8,128)(2,1)S(1)} %all-to-all-done.mine), channel_id=1, source_target_pairs={{0,1},{1,0},{2,3},{3,2},{4,5},{5,4},{6,7},{7,6},{8,9},{9,8},{10,11... | collective-permute-start | bytes 6291464 | tf_op jit(solution)/shard_map/ppermute | solution.py:242
  71.3 3.8 %own_part.2 = (f32[512,256]{1,0:T(8,128)S(1)}, bf16[2560,256]{1,0:T(8,128)(2,1)S(1)}) custom-call(s32[3]{0:T(128)S(1)} %pad_add_fusion.place, bf16[4,4,512,128]{3,2,1,0:T(8,128)(2,1)S(1)} %all-to-all-done.mine, bf16[2,512,128]{2,1,0:T(8,128)(2,1)S(1)} %pad_maximum_fusion.rest_0_, bf16[2,512,128]{2,1,0:T(8,128)(2,1)S(1)} %collective-permute-done.1.rest_1_, ...), custom_call_target="tpu_custom_call" | custom-call | flops 34359738368 | bytes 8388608 | tf_op jit(solution)/shard_map/own_part/pallas_call | solution.py:192
  75.1 0.0 collective-permute-done.8.rest_1_
  75.1 2.8 %own_part.3 = (f32[512,256]{1,0:T(8,128)S(1)}, bf16[1024,256]{1,0:T(8,128)(2,1)S(1)}, bf16[512,512]{1,0:T(8,128)(2,1)S(1)}) custom-call(s32[3]{0:T(128)S(1)} %pad_add_fusion.place, bf16[4,4,512,128]{3,2,1,0:T(8,128)(2,1)S(1)} %all-to-all-done.mine, bf16[2,512,128]{2,1,0:T(8,128)(2,1)S(1)} %collective-permute-done.3.rest_0_, ...), custom_call_target="tpu_custom_call" | custom-call | flops 34359738368 | bytes 8388608 | tf_op jit(solution)/shard_map/own_part/pallas_call | solution.py:192
  78.0 0.0 collective-permute-done.7.others
  78.0 0.0 copy-start
  78.0 3.0 %other_part.1 = (f32[512,256]{1,0:T(8,128)S(1)}, bf16[512,512]{1,0:T(8,128)(2,1)S(1)}) custom-call(s32[3]{0:T(128)S(1)} %pad_add_fusion.place, bf16[4,4,512,128]{3,2,1,0:T(8,128)(2,1)S(1)} %collective-permute-done.7.others, f32[512,256]{1,0:T(8,128)S(1)} %get-tuple-element.21.start, bf16[2560,256]{1,0:T(8,128)(2,1)S(1)} %get-tuple-element.22.rest_0_, ...), custom_call_target="tpu_custom_call" | custom-call | flops 34359738368 | bytes 8388608 | tf_op jit(solution)/shard_map/other_part/pallas_call | solution.py:192
  81.0 0.0 collective-permute-done.4.last
  81.0 0.0 copy-done
  81.0 2.2 %last_part.1 = (f32[512,256]{1,0:T(8,128)S(1)}, f32[1,256]{1,0:T(1,128)S(1)}) custom-call(s32[3]{0:T(128)S(1)} %pad_add_fusion.place, s32[2,4]{1,0:T(2,128)S(1)} %bitcast.6, bf16[2,512,128]{2,1,0:T(8,128)(2,1)} %collective-permute-done.4.last, f32[512,256]{1,0:T(8,128)S(1)} %get-tuple-element.24.start, bf16[512,512]{1,0:T(8,128)(2,1)S(1)} %get-tuple-element.25.far_mine, ...), custom_call_target="tpu_custom_call" | custom-call | flops 34359738368 | bytes 8388608 | tf_op jit(solution)/shard_map/last_part/pallas_call | solution.py:192
  83.2 2.4 %collective-permute-start.9 = (f32[1,256]{1,0:T(1,128)S(1)}, f32[1,256]{1,0:T(1,128)S(1)}, u32[]{:S(2)}, u32[]{:S(2)}) collective-permute-start(f32[1,256]{1,0:T(1,128)S(1)} %get-tuple-element.28), channel_id=1, source_target_pairs={{0,256},{256,0},{1,257},{257,1},{2,258},{258,2},{3,259},{259,3},{4... | collective-permute-start | bytes 3080 | tf_op jit(solution)/shard_map/ppermute | solution.py:242
  85.6 7.0 %collective-permute-done.9 = f32[1,256]{1,0:T(1,128)S(1)} collective-permute-done((f32[1,256]{1,0:T(1,128)S(1)}, f32[1,256]{1,0:T(1,128)S(1)}, u32[]{:S(2)}, u32[]{:S(2)}) %collective-permute-start.9) | collective-permute-done | bytes 1056 | tf_op jit(solution)/shard_map/ppermute | solution.py:242
  92.6 15.2 %all_to_all.11 = f32[8,1,256]{2,1,0:T(1,128)S(1)} all-to-all(f32[8,1,256]{2,1,0:T(1,128)S(1)} %broadcast_in_dim.10), channel_id=1, replica_groups=mesh['zh'=2,'y'=8,'x'=4,'zl'=4,'core'=2] {'y'}, dimensions={0} | all-to-all | bytes 16384 | tf_op jit(solution)/shard_map/all_to_all | solution.py:270
  107.8 0.8 maximum_convert_fusion
  (4 shorter events, 0.1 us)
Async XLA Ops:
  1.7 29.7 %collective-permute-start = (bf16[1,512,128]{2,1,0:T(8,128)(2,1)}, bf16[1,512,128]{2,1,0:T(8,128)(2,1)S(1)}, u32[]{:S(2)}, u32[]{:S(2)}) collective-permute-start(bf16[1,512,128]{2,1,0:T(8,128)(2,1)} %pack_tiles.1), channel_id=1, source_target_pairs={{0,256},{256,0},{1,257},{257,1},{2,258},{258,2},{3,259},{259,3},{4... | collective-permute-start | bytes 393224 | tf_op jit(solution)/shard_map/ppermute | solution.py:242
  33.1 4.9 %copy-start.1 = (bf16[1,512,128]{2,1,0:T(8,128)(2,1)S(1)}, bf16[1,512,128]{2,1,0:T(8,128)(2,1)}, u32[]{:S(2)}) copy-start(bf16[1,512,128]{2,1,0:T(8,128)(2,1)} %pack_tiles.1) | copy-start | bytes 393220
  33.1 36.2 %all-to-all-start = ((bf16[4,4,512,128]{3,2,1,0:T(8,128)(2,1)}), bf16[4,4,512,128]{3,2,1,0:T(8,128)(2,1)S(1)}, u32[]{:S(2)}, u32[]{:S(2)}) async-start(bf16[4,4,512,128]{3,2,1,0:T(8,128)(2,1)} %broadcast_in_dim.4), calls=%async_computation | async-start | bytes 4194304 | tf_op jit(solution)/shard_map/all_to_all | solution.py:252
  38.1 9.7 %collective-permute-start.1 = (bf16[2,512,128]{2,1,0:T(8,128)(2,1)S(1)}, bf16[2,512,128]{2,1,0:T(8,128)(2,1)S(1)}, u32[]{:S(2)}, u32[]{:S(2)}) collective-permute-start(bf16[2,512,128]{2,1,0:T(8,128)(2,1)S(1)} %pad_maximum_fusion.rest_0_), channel_id=1, source_target_pairs={{0,32},{32,64},{64,96},{96,128},{128,160},{160,192},{192,224},{224... | collective-permute-start | bytes 786440 | tf_op jit(solution)/shard_map/ppermute | solution.py:242
  41.6 8.3 %collective-permute-start.5 = (bf16[2,512,128]{2,1,0:T(8,128)(2,1)S(1)}, bf16[2,512,128]{2,1,0:T(8,128)(2,1)S(1)}, u32[]{:S(2)}, u32[]{:S(2)}) collective-permute-start(bf16[2,512,128]{2,1,0:T(8,128)(2,1)S(1)} %pad_maximum_fusion.rest_0_), channel_id=1, source_target_pairs={{0,224},{32,0},{64,32},{96,64},{128,96},{160,128},{192,160},{224,1... | collective-permute-start | bytes 786440 | tf_op jit(solution)/shard_map/ppermute | solution.py:242
  47.8 9.5 %collective-permute-start.2 = (bf16[2,512,128]{2,1,0:T(8,128)(2,1)S(1)}, bf16[2,512,128]{2,1,0:T(8,128)(2,1)S(1)}, u32[]{:S(2)}, u32[]{:S(2)}) collective-permute-start(bf16[2,512,128]{2,1,0:T(8,128)(2,1)S(1)} %collective-permute-done.1.rest_1_), channel_id=1, source_target_pairs={{0,32},{32,64},{64,96},{96,128},{128,160},{160,192},{192,224},{224... | collective-permute-start | bytes 786440 | tf_op jit(solution)/shard_map/ppermute | solution.py:242
  49.9 9.4 %collective-permute-start.6 = (bf16[2,512,128]{2,1,0:T(8,128)(2,1)S(1)}, bf16[2,512,128]{2,1,0:T(8,128)(2,1)}, u32[]{:S(2)}, u32[]{:S(2)}) collective-permute-start(bf16[2,512,128]{2,1,0:T(8,128)(2,1)S(1)} %collective-permute-done.5.rest_4_), channel_id=1, source_target_pairs={{0,224},{32,0},{64,32},{96,64},{128,96},{160,128},{192,160},{224,1... | collective-permute-start | bytes 786440 | tf_op jit(solution)/shard_map/ppermute | solution.py:242
  57.3 10.1 %collective-permute-start.3 = (bf16[2,512,128]{2,1,0:T(8,128)(2,1)S(1)}, bf16[2,512,128]{2,1,0:T(8,128)(2,1)S(1)}, u32[]{:S(2)}, u32[]{:S(2)}) collective-permute-start(bf16[2,512,128]{2,1,0:T(8,128)(2,1)S(1)} %collective-permute-done.2.rest_2_), channel_id=1, source_target_pairs={{0,32},{32,64},{64,96},{96,128},{128,160},{160,192},{192,224},{224... | collective-permute-start | bytes 786440 | tf_op jit(solution)/shard_map/ppermute | solution.py:242
  59.3 15.8 %collective-permute-start.8 = (bf16[2,512,128]{2,1,0:T(8,128)(2,1)}, bf16[2,512,128]{2,1,0:T(8,128)(2,1)}, u32[]{:S(2)}, u32[]{:S(2)}) collective-permute-start(bf16[2,512,128]{2,1,0:T(8,128)(2,1)} %collective-permute-done.6.rest_3_), channel_id=1, source_target_pairs={{0,224},{32,0},{64,32},{96,64},{128,96},{160,128},{192,160},{224,1... | collective-permute-start | bytes 786440 | tf_op jit(solution)/shard_map/ppermute | solution.py:242
  67.4 13.6 %collective-permute-start.4 = (bf16[2,512,128]{2,1,0:T(8,128)(2,1)S(1)}, bf16[2,512,128]{2,1,0:T(8,128)(2,1)}, u32[]{:S(2)}, u32[]{:S(2)}) collective-permute-start(bf16[2,512,128]{2,1,0:T(8,128)(2,1)S(1)} %collective-permute-done.3.rest_0_), channel_id=1, source_target_pairs={{0,32},{32,64},{64,96},{96,128},{128,160},{160,192},{192,224},{224... | collective-permute-start | bytes 786440 | tf_op jit(solution)/shard_map/ppermute | solution.py:242
  69.4 8.6 %collective-permute-start.7 = (bf16[4,4,512,128]{3,2,1,0:T(8,128)(2,1)S(1)}, bf16[4,4,512,128]{3,2,1,0:T(8,128)(2,1)S(1)}, u32[]{:S(2)}, u32[]{:S(2)}) collective-permute-start(bf16[4,4,512,128]{3,2,1,0:T(8,128)(2,1)S(1)} %all-to-all-done.mine), channel_id=1, source_target_pairs={{0,1},{1,0},{2,3},{3,2},{4,5},{5,4},{6,7},{7,6},{8,9},{9,8},{10,11... | collective-permute-start | bytes 6291464 | tf_op jit(solution)/shard_map/ppermute | solution.py:242
  78.0 3.0 %copy-start = (s32[4,2]{0,1:T(2,128)S(1)}, s32[4,2]{0,1:T(2,128)}, u32[]{:S(2)}) copy-start(s32[4,2]{0,1:T(2,128)} %param.5) | copy-start | bytes 100
  83.2 9.4 %collective-permute-start.9 = (f32[1,256]{1,0:T(1,128)S(1)}, f32[1,256]{1,0:T(1,128)S(1)}, u32[]{:S(2)}, u32[]{:S(2)}) collective-permute-start(f32[1,256]{1,0:T(1,128)S(1)} %get-tuple-element.28), channel_id=1, source_target_pairs={{0,256},{256,0},{1,257},{257,1},{2,258},{258,2},{3,259},{259,3},{4... | collective-permute-start | bytes 3080 | tf_op jit(solution)/shard_map/ppermute | solution.py:242

commit v4 on v3

--- a/solution.py
+++ b/solution.py
@@ -14,6 +14,7 @@
 CAP = 4
 HEAD = 16
 SIGNS = 4
+SLOT_BITS = 3
 LEAST = 2.0**-126
 PACK = CAP * TILE
 AXES = ("zh", "y", "x", "zl", "core")
@@ -64,7 +65,7 @@
 
 
 def put_tile(dense, at, ref, lead, table, row, t):
-    slot = table[row, t]
+    slot = lax.shift_right_logical(table[row], SLOT_BITS * t) & (2**SLOT_BITS - 1)
     start = pl.multiple_of(jnp.minimum(slot, CAP - 1) * TILE, TILE)
     head = jnp.abs(ref[(*lead, pl.ds(start, HEAD), slice(None))])
     rest = ref[(*lead, pl.ds(pl.multiple_of(start + HEAD, HEAD), TILE - HEAD), slice(None))]
@@ -73,21 +74,22 @@
     dense[r + HEAD:r + TILE, c:c + TILE] = jnp.where(slot < CAP, rest, jnp.zeros_like(rest))
 
 
-def read_slots(blocks, heads, meta, table, sem):
+def read_slots(blocks, heads, table):
     for i, (ref, lead) in enumerate(blocks):
         for slot in range(CAP):
             head = ref[(*lead, pl.ds(slot * TILE, HEAD), slice(None))].astype(jnp.float32)
             heads[slot, i:i + 1, :] = head[0:1]
-    lane = lax.broadcasted_iota(jnp.int32, meta.shape, 1)
+    lane = lax.broadcasted_iota(jnp.int32, heads.shape[1:], 1)
     weight = jnp.where(lane < SIGNS, lax.shift_left(jnp.ones_like(lane), jnp.minimum(lane, SIGNS)), 0)
-    slots = jnp.full(meta.shape, CAP, jnp.int32)
+    slots = jnp.full(lane.shape, CAP, jnp.int32)
     for slot in range(CAP):
         code = jnp.sum(jnp.where(heads[slot] < 0, weight, 0), axis=1, keepdims=True)
         slots = jnp.where(code == lane + RB * CB, slot, slots)
-    meta[...] = slots
-    copy = pltpu.make_async_copy(meta, table, sem)
-    copy.start()
-    copy.wait()
+    tiles = RB * CB
+    slots = jnp.where(lane < tiles, lax.shift_left(slots, SLOT_BITS * jnp.minimum(lane, tiles - 1)), 0)
+    slots = jnp.sum(slots, axis=1, keepdims=True)
+    for i in range(len(blocks)):
+        table[i] = slots[i, 0]
 
 
 def spread_band(band, table, entries, places, dense, col):
@@ -125,13 +127,13 @@
     start, rest = (rest[0], rest[1:]) if far else (None, rest)
     acc, spare, rest = rest[0], rest[1], rest[2:]
     far_dense, rest = (rest[0], rest[1:]) if far else (None, rest)
-    heads, meta, table, a_dense, b_dense, sem = rest
+    heads, table, a_dense, b_dense = rest
     hi, y, core = place[0], place[1], place[2]
     nl = mine.shape[1]
     blocks = all_blocks(mine)
     chips = len(blocks)
     blocks += [(panel, (z,)) for panel in panels for z in range(2)]
-    read_slots(blocks, heads, meta, table, sem)
+    read_slots(blocks, heads, table)
     for n, (entries, places) in enumerate(sources(hi, y, ny, nl, js)):
         spread_panel(panels[n], table, chips + 2 * n, core, ((b_dense, n * DEEP), (spare, n * DEEP)))
         spread_band(mine, table, entries, places, a_dense, n * DEEP)
@@ -143,10 +145,10 @@
 
 
 def other_kernel(ny, order, place, others, start, *rest):
-    spares, (acc, far_dense, heads, meta, table, a_dense, sem) = rest[:len(order)], rest[len(order):]
+    spares, (acc, far_dense, heads, table, a_dense) = rest[:len(order)], rest[len(order):]
     hi, y = place[0], place[1]
     nl = others.shape[1]
-    read_slots(all_blocks(others), heads, meta, table, sem)
+    read_slots(all_blocks(others), heads, table)
     total = start[...]
     col = 0
     for js, spare in zip(order, spares):
@@ -160,9 +162,9 @@
     spread_band(others, table, entries, places, far_dense, 0)
 
 
-def last_kernel(place, keep, last, start, far_mine, far_others, out, totals, heads, meta, table, b_dense, acc, sem):
+def last_kernel(place, keep, last, start, far_mine, far_others, out, totals, heads, table, b_dense, acc):
     core = place[2]
-    read_slots([(last, (z,)) for z in range(2)], heads, meta, table, sem)
+    read_slots([(last, (z,)) for z in range(2)], heads, table)
     mine_rows, others_rows = b_dense.at[pl.ds(0, DEEP)], b_dense.at[pl.ds(DEEP, DEEP)]
     spread_panel(last, table, 0, core, ((mine_rows, 0), (others_rows, 0)))
     total = start[...] + jnp.dot(far_mine[...], mine_rows[...], preferred_element_type=jnp.float32)
@@ -181,10 +183,8 @@
 def scratch(entries, *more):
     return [
         pltpu.VMEM((CAP, entries, TILE), jnp.float32),
-        pltpu.VMEM((entries, TILE), jnp.int32),
-        pltpu.SMEM((entries, TILE), jnp.int32),
+        pltpu.SMEM((entries,), jnp.int32),
         *more,
-        pltpu.SemaphoreType.DMA,
     ]
 
 
@@ -259,15 +259,14 @@
     early = [j for j in range(ny) if min(j, ny - j) < half - 1]
     late = [half - 1, half + 1]
     start, spare = own_part(ny, early, place, mine, [panels[j] for j in early])
-    sent, _, _ = lax.optimization_barrier((mine, panels[half - 2], panels[half + 2]))
+    sent, start, panels[half - 1] = lax.optimization_barrier((mine, start, panels[half - 1]))
     others = shifted(sent, "core", 1)
     last = shifted(panels[half - 1], "y", 1)
     start, late_spare, far_mine = own_part(ny, late, place, mine, [panels[j] for j in late], start)
     start, far_others = other_part(ny, [early, late], place, others, start, [spare, late_spare])
     inflated, totals = last_part(place, out_pattern, last, start, far_mine, far_others)
-    totals = totals + shifted(totals, "zh", 1)
-    copies = jnp.broadcast_to(totals, (ny, totals.shape[1]))
-    column_totals = jnp.sum(lax.all_to_all(copies, "y", 0, 0, tiled=True), axis=0, keepdims=True)
+    copies = jnp.broadcast_to(totals, (ny * lax.axis_size("zh"), totals.shape[1]))
+    column_totals = jnp.sum(lax.all_to_all(copies, BLK, 0, 0, tiled=True), axis=0, keepdims=True)
     scaled = inflated / column_totals * float(SIZES[0] * SIZES[1] * RB * TILE)
     return jnp.maximum(scaled - prune_level, 0.0).astype(jnp.bfloat16)
 

time: 109 us -> 103 us (0.945)
  the two profiles are of different devices: /device:TPU:2 before, /device:TPU:1 now
where the time goes in v4:
time: 103 us; the launch traced here: 101 us
  starting transfers between devices  47.7 us (46%)
  blocking collectives  32.4 us (31%)
  Pallas kernels  10.5 us (10%)
  waiting for transfers between devices  7.85 us (8%)
  local copies, waits for them, and re-layouts  1.77 us (2%)
    ppermute x9, starting transfers between devices, shifted(): return lax.ppermute(array, axis, [(i, (i + by) % n) for i in range(n)])  43.7 us
    all_gather x1, blocking collectives, body(): line = lax.all_gather(packed, 'zl', tiled=True)  16.5 us
    all_to_all x1, blocking collectives, body(): lax.all_to_all(copies, BLK, 0, 0, tiled=True)  15.9 us
    pallas_call x4, Pallas kernels, kernel_call(): pl.pallas_call(kernel, out_shape=outs, in_specs=[SMEM] * len(smems) + [VM...  8.85 us
    ppermute x9, waiting for transfers between devices, shifted(): return lax.ppermute(array, axis, [(i, (i + by) % n) for i in range(n)])  7.85 us
    all_to_all x1, starting transfers between devices, body(): mine = lax.all_to_all(jnp.broadcast_to(line, (nx, *line.shape)), 'x', 0, 0)  4.03 us
  transfers between devices with their start and end apart: 10, of which 4 were waited for; matrix products, arithmetic and copies ran while one was open for 0% of the time, Pallas kernels for 7%

profile of v4, /device:TPU:1, one launch (start us, length us, event | category | flops | bytes accessed | tf_op | source)
XLA Modules:
  0.0 101.4 jit_solution(9330233658583157085)
XLA Ops:
  0.0 1.7 %pack_tiles.1 = bf16[1,512,128]{2,1,0:T(8,128)(2,1)} custom-call(s32[2,4]{1,0:T(2,128)} %bitcast.8, bf16[512,256]{1,0:T(8,128)(2,1)} %matrix.1), custom_call_target="tpu_custom_call" | custom-call | tf_op jit(solution)/shard_map/pack_tiles/pallas_call | solution.py:58
  1.7 11.4 %collective-permute-start = (bf16[1,512,128]{2,1,0:T(8,128)(2,1)}, bf16[1,512,128]{2,1,0:T(8,128)(2,1)S(1)}, u32[]{:S(2)}, u32[]{:S(2)}) collective-permute-start(bf16[1,512,128]{2,1,0:T(8,128)(2,1)} %pack_tiles.1), channel_id=1, source_target_pairs={{0,256},{256,0},{1,257},{257,1},{2,258},{258,2},{3,259},{259,3},{4... | collective-permute-start | bytes 393224 | tf_op jit(solution)/shard_map/ppermute | solution.py:242
  13.2 16.5 %all_gather.3 = bf16[4,512,128]{2,1,0:T(8,128)(2,1)S(1)} all-gather(bf16[1,512,128]{2,1,0:T(8,128)(2,1)} %pack_tiles.1), channel_id=1, replica_groups=mesh['zh'=2,'y'=8,'x'=4,'zl'=4,'core'=2] {'zl'}, dimensions={0}, use_global_device_ids=true | all-gather | bytes 655360 | tf_op jit(solution)/shard_map/all_gather | solution.py:249
  29.6 0.0 collective-permute-done
  29.6 1.7 %broadcast_in_dim.4 = bf16[4,4,512,128]{3,2,1,0:T(8,128)(2,1)} broadcast(bf16[4,512,128]{2,1,0:T(8,128)(2,1)S(1)} %all_gather.3), dimensions={1,2,3} | broadcast | bytes 2621440 | tf_op jit(solution)/shard_map/broadcast_in_dim | solution.py:252
  31.4 0.0 copy-start.1
  31.4 4.0 %all-to-all-start = ((bf16[4,4,512,128]{3,2,1,0:T(8,128)(2,1)}), bf16[4,4,512,128]{3,2,1,0:T(8,128)(2,1)S(1)}, u32[]{:S(2)}, u32[]{:S(2)}) async-start(bf16[4,4,512,128]{3,2,1,0:T(8,128)(2,1)} %broadcast_in_dim.4), calls=%async_computation | async-start | bytes 4194304 | tf_op jit(solution)/shard_map/all_to_all | solution.py:252
  35.4 0.0 copy-done.1
  35.5 5.1 %collective-permute-start.3 = (bf16[2,512,128]{2,1,0:T(8,128)(2,1)S(1)}, bf16[2,512,128]{2,1,0:T(8,128)(2,1)S(1)}, u32[]{:S(2)}, u32[]{:S(2)}) collective-permute-start(bf16[2,512,128]{2,1,0:T(8,128)(2,1)S(1)} %pad_maximum_fusion.rest_0_), channel_id=1, source_target_pairs={{0,224},{32,0},{64,32},{96,64},{128,96},{160,128},{192,160},{224,1... | collective-permute-start | bytes 786440 | tf_op jit(solution)/shard_map/ppermute | solution.py:242
  40.6 1.9 %collective-permute-start.1 = (bf16[2,512,128]{2,1,0:T(8,128)(2,1)S(1)}, bf16[2,512,128]{2,1,0:T(8,128)(2,1)S(1)}, u32[]{:S(2)}, u32[]{:S(2)}) collective-permute-start(bf16[2,512,128]{2,1,0:T(8,128)(2,1)S(1)} %pad_maximum_fusion.rest_0_), channel_id=1, source_target_pairs={{0,32},{32,64},{64,96},{96,128},{128,160},{160,192},{192,224},{224... | collective-permute-start | bytes 786440 | tf_op jit(solution)/shard_map/ppermute | solution.py:242
  42.5 1.4 %collective-permute-done.3.rest_4_ = bf16[2,512,128]{2,1,0:T(8,128)(2,1)S(1)} collective-permute-done((bf16[2,512,128]{2,1,0:T(8,128)(2,1)S(1)}, bf16[2,512,128]{2,1,0:T(8,128)(2,1)S(1)}, u32[]{:S(2)}, u32[]{:S(2)}) %collective-permute-start.3) | collective-permute-done | bytes 262176 | tf_op jit(solution)/shard_map/ppermute | solution.py:242
  43.8 5.3 %collective-permute-start.4 = (bf16[2,512,128]{2,1,0:T(8,128)(2,1)S(1)}, bf16[2,512,128]{2,1,0:T(8,128)(2,1)S(1)}, u32[]{:S(2)}, u32[]{:S(2)}) collective-permute-start(bf16[2,512,128]{2,1,0:T(8,128)(2,1)S(1)} %collective-permute-done.3.rest_4_), channel_id=1, source_target_pairs={{0,224},{32,0},{64,32},{96,64},{128,96},{160,128},{192,160},{224,1... | collective-permute-start | bytes 786440 | tf_op jit(solution)/shard_map/ppermute | solution.py:242
  49.2 0.0 collective-permute-done.1.rest_1_
  49.2 1.9 %collective-permute-start.2 = (bf16[2,512,128]{2,1,0:T(8,128)(2,1)S(1)}, bf16[2,512,128]{2,1,0:T(8,128)(2,1)S(1)}, u32[]{:S(2)}, u32[]{:S(2)}) collective-permute-start(bf16[2,512,128]{2,1,0:T(8,128)(2,1)S(1)} %collective-permute-done.1.rest_1_), channel_id=1, source_target_pairs={{0,32},{32,64},{64,96},{96,128},{128,160},{160,192},{192,224},{224... | collective-permute-start | bytes 786440 | tf_op jit(solution)/shard_map/ppermute | solution.py:242
  51.1 0.1 pad_add_fusion.place
  51.2 1.3 %collective-permute-done.4.rest_3_ = bf16[2,512,128]{2,1,0:T(8,128)(2,1)S(1)} collective-permute-done((bf16[2,512,128]{2,1,0:T(8,128)(2,1)S(1)}, bf16[2,512,128]{2,1,0:T(8,128)(2,1)S(1)}, u32[]{:S(2)}, u32[]{:S(2)}) %collective-permute-start.4) | collective-permute-done | bytes 262176 | tf_op jit(solution)/shard_map/ppermute | solution.py:242
  52.5 5.3 %collective-permute-start.8 = (bf16[2,512,128]{2,1,0:T(8,128)(2,1)S(1)}, bf16[2,512,128]{2,1,0:T(8,128)(2,1)}, u32[]{:S(2)}, u32[]{:S(2)}) collective-permute-start(bf16[2,512,128]{2,1,0:T(8,128)(2,1)S(1)} %collective-permute-done.4.rest_3_), channel_id=1, source_target_pairs={{0,224},{32,0},{64,32},{96,64},{128,96},{160,128},{192,160},{224,1... | collective-permute-start | bytes 786440 | tf_op jit(solution)/shard_map/ppermute | solution.py:242
  57.8 0.0 collective-permute-done.2.rest_2_
  57.8 1.9 %collective-permute-start.5 = (bf16[2,512,128]{2,1,0:T(8,128)(2,1)S(1)}, bf16[2,512,128]{2,1,0:T(8,128)(2,1)}, u32[]{:S(2)}, u32[]{:S(2)}) collective-permute-start(bf16[2,512,128]{2,1,0:T(8,128)(2,1)S(1)} %collective-permute-done.2.rest_2_), channel_id=1, source_target_pairs={{0,32},{32,64},{64,96},{96,128},{128,160},{160,192},{192,224},{224... | collective-permute-start | bytes 786440 | tf_op jit(solution)/shard_map/ppermute | solution.py:242
  59.7 0.0 all-to-all-done.mine
  59.7 2.7 %own_part.2 = (f32[512,256]{1,0:T(8,128)S(1)}, bf16[2560,256]{1,0:T(8,128)(2,1)S(1)}) custom-call(s32[3]{0:T(128)S(1)} %pad_add_fusion.place, bf16[4,4,512,128]{3,2,1,0:T(8,128)(2,1)S(1)} %all-to-all-done.mine, bf16[2,512,128]{2,1,0:T(8,128)(2,1)S(1)} %pad_maximum_fusion.rest_0_, bf16[2,512,128]{2,1,0:T(8,128)(2,1)S(1)} %collective-permute-done.1.rest_1_, ...), custom_call_target="tpu_custom_call" | custom-call | flops 34359738368 | bytes 8388608 | tf_op jit(solution)/shard_map/own_part/pallas_call | solution.py:192
  62.5 3.8 %collective-permute-done.5.rest_0_ = bf16[2,512,128]{2,1,0:T(8,128)(2,1)} collective-permute-done((bf16[2,512,128]{2,1,0:T(8,128)(2,1)S(1)}, bf16[2,512,128]{2,1,0:T(8,128)(2,1)}, u32[]{:S(2)}, u32[]{:S(2)}) %collective-permute-start.5) | collective-permute-done | bytes 262176 | tf_op jit(solution)/shard_map/ppermute | solution.py:242
  66.2 1.9 %collective-permute-start.6 = (bf16[2,512,128]{2,1,0:T(8,128)(2,1)}, bf16[2,512,128]{2,1,0:T(8,128)(2,1)S(1)}, u32[]{:S(2)}, u32[]{:S(2)}) collective-permute-start(bf16[2,512,128]{2,1,0:T(8,128)(2,1)} %collective-permute-done.5.rest_0_), channel_id=1, source_target_pairs={{0,32},{32,64},{64,96},{96,128},{128,160},{160,192},{192,224},{224... | collective-permute-start | bytes 786440 | tf_op jit(solution)/shard_map/ppermute | solution.py:242
  68.1 8.9 %collective-permute-start.7 = (bf16[4,4,512,128]{3,2,1,0:T(8,128)(2,1)S(1)}, bf16[4,4,512,128]{3,2,1,0:T(8,128)(2,1)S(1)}, u32[]{:S(2)}, u32[]{:S(2)}) collective-permute-start(bf16[4,4,512,128]{3,2,1,0:T(8,128)(2,1)S(1)} %all-to-all-done.mine), channel_id=1, source_target_pairs={{0,1},{1,0},{2,3},{3,2},{4,5},{5,4},{6,7},{7,6},{8,9},{9,8},{10,11... | collective-permute-start | bytes 6291464 | tf_op jit(solution)/shard_map/ppermute | solution.py:242
  77.0 0.0 collective-permute-done.8.rest_1_
  77.1 2.3 %own_part.3 = (f32[512,256]{1,0:T(8,128)S(1)}, bf16[1024,256]{1,0:T(8,128)(2,1)S(1)}, bf16[512,512]{1,0:T(8,128)(2,1)S(1)}) custom-call(s32[3]{0:T(128)S(1)} %pad_add_fusion.place, bf16[4,4,512,128]{3,2,1,0:T(8,128)(2,1)S(1)} %all-to-all-done.mine, bf16[2,512,128]{2,1,0:T(8,128)(2,1)} %collective-permute-done.5.rest_0_, ...), custom_call_target="tpu_custom_call" | custom-call | flops 34359738368 | bytes 8388608 | tf_op jit(solution)/shard_map/own_part/pallas_call | solution.py:192
  79.4 1.4 %collective-permute-done.7.others = bf16[4,4,512,128]{3,2,1,0:T(8,128)(2,1)S(1)} collective-permute-done((bf16[4,4,512,128]{3,2,1,0:T(8,128)(2,1)S(1)}, bf16[4,4,512,128]{3,2,1,0:T(8,128)(2,1)S(1)}, u32[]{:S(2)}, u32[]{:S(2)}) %collective-permute-start.7) | collective-permute-done | bytes 2097184 | tf_op jit(solution)/shard_map/ppermute | solution.py:242
  80.8 0.0 copy-start
  80.8 2.4 %other_part.1 = (f32[512,256]{1,0:T(8,128)S(1)}, bf16[512,512]{1,0:T(8,128)(2,1)S(1)}) custom-call(s32[3]{0:T(128)S(1)} %pad_add_fusion.place, bf16[4,4,512,128]{3,2,1,0:T(8,128)(2,1)S(1)} %collective-permute-done.7.others, f32[512,256]{1,0:T(8,128)S(1)} %get-tuple-element.25.start, bf16[2560,256]{1,0:T(8,128)(2,1)S(1)} %get-tuple-element.26.rest_0_, ...), custom_call_target="tpu_custom_call" | custom-call | flops 34359738368 | bytes 8388608 | tf_op jit(solution)/shard_map/other_part/pallas_call | solution.py:192
  83.3 0.0 collective-permute-done.6.last
  83.3 0.0 copy-done
  83.3 1.3 %last_part.1 = (f32[512,256]{1,0:T(8,128)S(1)}, f32[1,256]{1,0:T(1,128)S(1)}) custom-call(s32[3]{0:T(128)S(1)} %pad_add_fusion.place, s32[2,4]{1,0:T(2,128)S(1)} %bitcast.7, bf16[2,512,128]{2,1,0:T(8,128)(2,1)S(1)} %collective-permute-done.6.last, f32[512,256]{1,0:T(8,128)S(1)} %get-tuple-element.28.start, bf16[512,512]{1,0:T(8,128)(2,1)S(1)} %get-tuple-element.29.far_mine, ...), custom_call_target="tpu_custom_call" | custom-call | flops 34359738368 | bytes 8388608 | tf_op jit(solution)/shard_map/last_part/pallas_call | solution.py:192
  84.6 15.9 %all_to_all.11 = f32[16,1,256]{2,1,0:T(1,128)S(1)} all-to-all(f32[16,1,256]{2,1,0:T(1,128)S(1)} %broadcast_in_dim.10), channel_id=1, replica_groups=mesh['zh'=2,'y'=8,'x'=4,'zl'=4,'core'=2] {'zh','y'}, dimensions={0} | all-to-all | bytes 32768 | tf_op jit(solution)/shard_map/all_to_all | solution.py:269
  100.6 0.8 maximum_convert_fusion
  (3 shorter events, 0.1 us)
Async XLA Ops:
  1.7 27.9 %collective-permute-start = (bf16[1,512,128]{2,1,0:T(8,128)(2,1)}, bf16[1,512,128]{2,1,0:T(8,128)(2,1)S(1)}, u32[]{:S(2)}, u32[]{:S(2)}) collective-permute-start(bf16[1,512,128]{2,1,0:T(8,128)(2,1)} %pack_tiles.1), channel_id=1, source_target_pairs={{0,256},{256,0},{1,257},{257,1},{2,258},{258,2},{3,259},{259,3},{4... | collective-permute-start | bytes 393224 | tf_op jit(solution)/shard_map/ppermute | solution.py:242
  31.4 4.0 %copy-start.1 = (bf16[1,512,128]{2,1,0:T(8,128)(2,1)S(1)}, bf16[1,512,128]{2,1,0:T(8,128)(2,1)}, u32[]{:S(2)}) copy-start(bf16[1,512,128]{2,1,0:T(8,128)(2,1)} %pack_tiles.1) | copy-start | bytes 393220
  31.4 28.3 %all-to-all-start = ((bf16[4,4,512,128]{3,2,1,0:T(8,128)(2,1)}), bf16[4,4,512,128]{3,2,1,0:T(8,128)(2,1)S(1)}, u32[]{:S(2)}, u32[]{:S(2)}) async-start(bf16[4,4,512,128]{3,2,1,0:T(8,128)(2,1)} %broadcast_in_dim.4), calls=%async_computation | async-start | bytes 4194304 | tf_op jit(solution)/shard_map/all_to_all | solution.py:252
  35.5 8.4 %collective-permute-start.3 = (bf16[2,512,128]{2,1,0:T(8,128)(2,1)S(1)}, bf16[2,512,128]{2,1,0:T(8,128)(2,1)S(1)}, u32[]{:S(2)}, u32[]{:S(2)}) collective-permute-start(bf16[2,512,128]{2,1,0:T(8,128)(2,1)S(1)} %pad_maximum_fusion.rest_0_), channel_id=1, source_target_pairs={{0,224},{32,0},{64,32},{96,64},{128,96},{160,128},{192,160},{224,1... | collective-permute-start | bytes 786440 | tf_op jit(solution)/shard_map/ppermute | solution.py:242
  40.6 8.6 %collective-permute-start.1 = (bf16[2,512,128]{2,1,0:T(8,128)(2,1)S(1)}, bf16[2,512,128]{2,1,0:T(8,128)(2,1)S(1)}, u32[]{:S(2)}, u32[]{:S(2)}) collective-permute-start(bf16[2,512,128]{2,1,0:T(8,128)(2,1)S(1)} %pad_maximum_fusion.rest_0_), channel_id=1, source_target_pairs={{0,32},{32,64},{64,96},{96,128},{128,160},{160,192},{192,224},{224... | collective-permute-start | bytes 786440 | tf_op jit(solution)/shard_map/ppermute | solution.py:242
  43.8 8.6 %collective-permute-start.4 = (bf16[2,512,128]{2,1,0:T(8,128)(2,1)S(1)}, bf16[2,512,128]{2,1,0:T(8,128)(2,1)S(1)}, u32[]{:S(2)}, u32[]{:S(2)}) collective-permute-start(bf16[2,512,128]{2,1,0:T(8,128)(2,1)S(1)} %collective-permute-done.3.rest_4_), channel_id=1, source_target_pairs={{0,224},{32,0},{64,32},{96,64},{128,96},{160,128},{192,160},{224,1... | collective-permute-start | bytes 786440 | tf_op jit(solution)/shard_map/ppermute | solution.py:242
  49.2 8.6 %collective-permute-start.2 = (bf16[2,512,128]{2,1,0:T(8,128)(2,1)S(1)}, bf16[2,512,128]{2,1,0:T(8,128)(2,1)S(1)}, u32[]{:S(2)}, u32[]{:S(2)}) collective-permute-start(bf16[2,512,128]{2,1,0:T(8,128)(2,1)S(1)} %collective-permute-done.1.rest_1_), channel_id=1, source_target_pairs={{0,32},{32,64},{64,96},{96,128},{128,160},{160,192},{192,224},{224... | collective-permute-start | bytes 786440 | tf_op jit(solution)/shard_map/ppermute | solution.py:242
  52.5 24.6 %collective-permute-start.8 = (bf16[2,512,128]{2,1,0:T(8,128)(2,1)S(1)}, bf16[2,512,128]{2,1,0:T(8,128)(2,1)}, u32[]{:S(2)}, u32[]{:S(2)}) collective-permute-start(bf16[2,512,128]{2,1,0:T(8,128)(2,1)S(1)} %collective-permute-done.4.rest_3_), channel_id=1, source_target_pairs={{0,224},{32,0},{64,32},{96,64},{128,96},{160,128},{192,160},{224,1... | collective-permute-start | bytes 786440 | tf_op jit(solution)/shard_map/ppermute | solution.py:242
  57.8 8.4 %collective-permute-start.5 = (bf16[2,512,128]{2,1,0:T(8,128)(2,1)S(1)}, bf16[2,512,128]{2,1,0:T(8,128)(2,1)}, u32[]{:S(2)}, u32[]{:S(2)}) collective-permute-start(bf16[2,512,128]{2,1,0:T(8,128)(2,1)S(1)} %collective-permute-done.2.rest_2_), channel_id=1, source_target_pairs={{0,32},{32,64},{64,96},{96,128},{128,160},{160,192},{192,224},{224... | collective-permute-start | bytes 786440 | tf_op jit(solution)/shard_map/ppermute | solution.py:242
  66.2 17.0 %collective-permute-start.6 = (bf16[2,512,128]{2,1,0:T(8,128)(2,1)}, bf16[2,512,128]{2,1,0:T(8,128)(2,1)S(1)}, u32[]{:S(2)}, u32[]{:S(2)}) collective-permute-start(bf16[2,512,128]{2,1,0:T(8,128)(2,1)} %collective-permute-done.5.rest_0_), channel_id=1, source_target_pairs={{0,32},{32,64},{64,96},{96,128},{128,160},{160,192},{192,224},{224... | collective-permute-start | bytes 786440 | tf_op jit(solution)/shard_map/ppermute | solution.py:242
  68.1 12.7 %collective-permute-start.7 = (bf16[4,4,512,128]{3,2,1,0:T(8,128)(2,1)S(1)}, bf16[4,4,512,128]{3,2,1,0:T(8,128)(2,1)S(1)}, u32[]{:S(2)}, u32[]{:S(2)}) collective-permute-start(bf16[4,4,512,128]{3,2,1,0:T(8,128)(2,1)S(1)} %all-to-all-done.mine), channel_id=1, source_target_pairs={{0,1},{1,0},{2,3},{3,2},{4,5},{5,4},{6,7},{7,6},{8,9},{9,8},{10,11... | collective-permute-start | bytes 6291464 | tf_op jit(solution)/shard_map/ppermute | solution.py:242
  80.8 2.5 %copy-start = (s32[4,2]{0,1:T(2,128)S(1)}, s32[4,2]{0,1:T(2,128)}, u32[]{:S(2)}) copy-start(s32[4,2]{0,1:T(2,128)} %param.5) | copy-start | bytes 100

commit v5 on v4

--- a/solution.py
+++ b/solution.py
@@ -122,9 +122,9 @@
     return [(band, (x, k)) for x in range(band.shape[0]) for k in range(band.shape[1])]
 
 
-def own_kernel(ny, js, far, place, mine, *rest):
+def own_kernel(ny, js, more, far, place, mine, *rest):
     panels, rest = rest[:len(js)], rest[len(js):]
-    start, rest = (rest[0], rest[1:]) if far else (None, rest)
+    start, rest = (rest[0], rest[1:]) if more else (None, rest)
     acc, spare, rest = rest[0], rest[1], rest[2:]
     far_dense, rest = (rest[0], rest[1:]) if far else (None, rest)
     heads, table, a_dense, b_dense = rest
@@ -188,7 +188,7 @@
     ]
 
 
-def kernel_call(kernel, name, outs, smems, vmems, scratch_shapes):
+def kernel_call(kernel, name, outs, smems, vmems, scratch_shapes, flops=2**30):
     return pl.pallas_call(
         kernel,
         out_shape=outs,
@@ -196,7 +196,7 @@
         out_specs=jax.tree.map(lambda _: VMEM, outs),
         scratch_shapes=scratch_shapes,
         compiler_params=pltpu.CompilerParams(vmem_limit_bytes=24 * 2**20),
-        cost_estimate=pl.CostEstimate(flops=2**35, bytes_accessed=2**23, transcendentals=0),
+        cost_estimate=pl.CostEstimate(flops=flops, bytes_accessed=2**23, transcendentals=0),
         name=name,
     )(*smems, *vmems)
 
@@ -210,17 +210,17 @@
     return (count * DEEP, CB * TILE)
 
 
-def own_part(ny, js, place, mine, panels, start=None):
+def own_part(ny, js, place, mine, panels, start=None, far=False):
     chips = mine.shape[0] * mine.shape[1]
-    far = start is not None
+    more = start is not None
     outs = (BLOCK_SUM, jax.ShapeDtypeStruct(rows_of(len(js)), jnp.bfloat16)) + ((FAR,) if far else ())
     shapes = scratch(
         chips + 2 * len(js),
         pltpu.VMEM((RB * TILE, len(js) * DEEP), jnp.bfloat16),
         pltpu.VMEM(rows_of(len(js)), jnp.bfloat16),
     )
-    arrays = [mine, *panels] + ([start] if far else [])
-    return kernel_call(functools.partial(own_kernel, ny, js, far), "own_part", outs, [place], arrays, shapes)
+    arrays = [mine, *panels] + ([start] if more else [])
+    return kernel_call(functools.partial(own_kernel, ny, js, more, far), "own_part", outs, [place], arrays, shapes, 2**30 if far else 2**35)
 
 
 def other_part(ny, order, place, others, start, spares):
@@ -256,14 +256,16 @@
     for i in range(1, half):
         panels[i] = shifted(panels[i - 1], "y", 1)
         panels[ny - i] = shifted(panels[(ny - i + 1) % ny], "y", -1)
-    early = [j for j in range(ny) if min(j, ny - j) < half - 1]
+    first = [j for j in range(ny) if min(j, ny - j) < half - 2]
+    second = [half - 2, half + 2]
     late = [half - 1, half + 1]
-    start, spare = own_part(ny, early, place, mine, [panels[j] for j in early])
-    sent, start, panels[half - 1] = lax.optimization_barrier((mine, start, panels[half - 1]))
+    start, spare = own_part(ny, first, place, mine, [panels[j] for j in first])
+    sent, start, panels[half + 1] = lax.optimization_barrier((mine, start, panels[half + 1]))
     others = shifted(sent, "core", 1)
-    last = shifted(panels[half - 1], "y", 1)
-    start, late_spare, far_mine = own_part(ny, late, place, mine, [panels[j] for j in late], start)
-    start, far_others = other_part(ny, [early, late], place, others, start, [spare, late_spare])
+    start, second_spare = own_part(ny, second, place, mine, [panels[j] for j in second], start)
+    last = shifted(panels[half + 1], "y", -1)
+    start, late_spare, far_mine = own_part(ny, late, place, mine, [panels[j] for j in late], start, True)
+    start, far_others = other_part(ny, [first, second, late], place, others, start, [spare, second_spare, late_spare])
     inflated, totals = last_part(place, out_pattern, last, start, far_mine, far_others)
     copies = jnp.broadcast_to(totals, (ny * lax.axis_size("zh"), totals.shape[1]))
     column_totals = jnp.sum(lax.all_to_all(copies, BLK, 0, 0, tiled=True), axis=0, keepdims=True)

time: 103 us -> 100 us (0.971)
  waiting for transfers between devices: 7.85 us -> 2.69 us
  starting transfers between devices: 47.7 us -> 50 us
    ppermute x9, waiting for transfers between devices: 7.85 us -> 2.68 us  [shifted(): return lax.ppermute(array, axis, [(i, (i + by) % n) for i in range(n)])]
    ppermute x9, starting transfers between devices: 43.7 us -> 46 us  [shifted(): return lax.ppermute(array, axis, [(i, (i + by) % n) for i in range(n)])]
    pallas_call x4 -> x5, Pallas kernels: 8.85 us -> 9.8 us  [kernel_call(): pl.pallas_call(kernel, out_shape=outs, in_specs=[SMEM] * len(smems) + [VM...]
  transfers between devices with their start and end apart: 10 -> 10, of which waited for: 4 -> 2; matrix products, arithmetic and copies ran while one was open for 0% -> 0% of each run, Pallas kernels for 7% -> 9%
where the time goes in v5:
time: 100 us; the launch traced here: 99.1 us
  starting transfers between devices  50 us (50%)
  blocking collectives  32 us (32%)
  Pallas kernels  11.5 us (12%)
  waiting for transfers between devices  2.69 us (3%)
  local copies, waits for them, and re-layouts  1.76 us (2%)
    ppermute x9, starting transfers between devices, shifted(): return lax.ppermute(array, axis, [(i, (i + by) % n) for i in range(n)])  46 us
    all_gather x1, blocking collectives, body(): line = lax.all_gather(packed, 'zl', tiled=True)  16.5 us
    all_to_all x1, blocking collectives, body(): lax.all_to_all(copies, BLK, 0, 0, tiled=True)  15.5 us
    pallas_call x5, Pallas kernels, kernel_call(): pl.pallas_call(kernel, out_shape=outs, in_specs=[SMEM] * len(smems) + [VM...  9.8 us
    all_to_all x1, starting transfers between devices, body(): mine = lax.all_to_all(jnp.broadcast_to(line, (nx, *line.shape)), 'x', 0, 0)  4.01 us
    ppermute x9, waiting for transfers between devices, shifted(): return lax.ppermute(array, axis, [(i, (i + by) % n) for i in range(n)])  2.68 us
  transfers between devices with their start and end apart: 10, of which 2 were waited for; matrix products, arithmetic and copies ran while one was open for 0% of the time, Pallas kernels for 9%

profile of v5, /device:TPU:1, one launch (start us, length us, event | category | flops | bytes accessed | tf_op | source)
XLA Modules:
  0.0 99.1 jit_solution(16602985396056330133)
XLA Ops:
  0.0 1.7 %pack_tiles.1 = bf16[1,512,128]{2,1,0:T(8,128)(2,1)} custom-call(s32[2,4]{1,0:T(2,128)} %bitcast.8, bf16[512,256]{1,0:T(8,128)(2,1)} %matrix.1), custom_call_target="tpu_custom_call" | custom-call | tf_op jit(solution)/shard_map/pack_tiles/pallas_call | solution.py:58
  1.7 11.5 %collective-permute-start = (bf16[1,512,128]{2,1,0:T(8,128)(2,1)}, bf16[1,512,128]{2,1,0:T(8,128)(2,1)S(1)}, u32[]{:S(2)}, u32[]{:S(2)}) collective-permute-start(bf16[1,512,128]{2,1,0:T(8,128)(2,1)} %pack_tiles.1), channel_id=1, source_target_pairs={{0,256},{256,0},{1,257},{257,1},{2,258},{258,2},{3,259},{259,3},{4... | collective-permute-start | bytes 393224 | tf_op jit(solution)/shard_map/ppermute | solution.py:242
  13.2 16.5 %all_gather.3 = bf16[4,512,128]{2,1,0:T(8,128)(2,1)S(1)} all-gather(bf16[1,512,128]{2,1,0:T(8,128)(2,1)} %pack_tiles.1), channel_id=1, replica_groups=mesh['zh'=2,'y'=8,'x'=4,'zl'=4,'core'=2] {'zl'}, dimensions={0}, use_global_device_ids=true | all-gather | bytes 655360 | tf_op jit(solution)/shard_map/all_gather | solution.py:249
  29.7 0.0 collective-permute-done
  29.7 1.7 %broadcast_in_dim.4 = bf16[4,4,512,128]{3,2,1,0:T(8,128)(2,1)} broadcast(bf16[4,512,128]{2,1,0:T(8,128)(2,1)S(1)} %all_gather.3), dimensions={1,2,3} | broadcast | bytes 2621440 | tf_op jit(solution)/shard_map/broadcast_in_dim | solution.py:252
  31.4 0.0 copy-start.1
  31.4 4.0 %all-to-all-start = ((bf16[4,4,512,128]{3,2,1,0:T(8,128)(2,1)}), bf16[4,4,512,128]{3,2,1,0:T(8,128)(2,1)S(1)}, u32[]{:S(2)}, u32[]{:S(2)}) async-start(bf16[4,4,512,128]{3,2,1,0:T(8,128)(2,1)} %broadcast_in_dim.4), calls=%async_computation | async-start | bytes 4194304 | tf_op jit(solution)/shard_map/all_to_all | solution.py:252
  35.4 0.0 copy-done.1
  35.5 5.1 %collective-permute-start.2 = (bf16[2,512,128]{2,1,0:T(8,128)(2,1)S(1)}, bf16[2,512,128]{2,1,0:T(8,128)(2,1)S(1)}, u32[]{:S(2)}, u32[]{:S(2)}) collective-permute-start(bf16[2,512,128]{2,1,0:T(8,128)(2,1)S(1)} %pad_maximum_fusion.rest_0_), channel_id=1, source_target_pairs={{0,224},{32,0},{64,32},{96,64},{128,96},{160,128},{192,160},{224,1... | collective-permute-start | bytes 786440 | tf_op jit(solution)/shard_map/ppermute | solution.py:242
  40.6 1.9 %collective-permute-start.1 = (bf16[2,512,128]{2,1,0:T(8,128)(2,1)S(1)}, bf16[2,512,128]{2,1,0:T(8,128)(2,1)S(1)}, u32[]{:S(2)}, u32[]{:S(2)}) collective-permute-start(bf16[2,512,128]{2,1,0:T(8,128)(2,1)S(1)} %pad_maximum_fusion.rest_0_), channel_id=1, source_target_pairs={{0,32},{32,64},{64,96},{96,128},{128,160},{160,192},{192,224},{224... | collective-permute-start | bytes 786440 | tf_op jit(solution)/shard_map/ppermute | solution.py:242
  42.5 1.4 %collective-permute-done.2.rest_2_ = bf16[2,512,128]{2,1,0:T(8,128)(2,1)S(1)} collective-permute-done((bf16[2,512,128]{2,1,0:T(8,128)(2,1)S(1)}, bf16[2,512,128]{2,1,0:T(8,128)(2,1)S(1)}, u32[]{:S(2)}, u32[]{:S(2)}) %collective-permute-start.2) | collective-permute-done | bytes 262176 | tf_op jit(solution)/shard_map/ppermute | solution.py:242
  43.8 5.3 %collective-permute-start.3 = (bf16[2,512,128]{2,1,0:T(8,128)(2,1)S(1)}, bf16[2,512,128]{2,1,0:T(8,128)(2,1)S(1)}, u32[]{:S(2)}, u32[]{:S(2)}) collective-permute-start(bf16[2,512,128]{2,1,0:T(8,128)(2,1)S(1)} %collective-permute-done.2.rest_2_), channel_id=1, source_target_pairs={{0,224},{32,0},{64,32},{96,64},{128,96},{160,128},{192,160},{224,1... | collective-permute-start | bytes 786440 | tf_op jit(solution)/shard_map/ppermute | solution.py:242
  49.2 0.0 collective-permute-done.1.rest_1_
  49.2 1.9 %collective-permute-start.7 = (bf16[2,512,128]{2,1,0:T(8,128)(2,1)S(1)}, bf16[2,512,128]{2,1,0:T(8,128)(2,1)S(1)}, u32[]{:S(2)}, u32[]{:S(2)}) collective-permute-start(bf16[2,512,128]{2,1,0:T(8,128)(2,1)S(1)} %collective-permute-done.1.rest_1_), channel_id=1, source_target_pairs={{0,32},{32,64},{64,96},{96,128},{128,160},{160,192},{192,224},{224... | collective-permute-start | bytes 786440 | tf_op jit(solution)/shard_map/ppermute | solution.py:242
  51.1 0.1 pad_add_fusion.place
  51.2 1.3 %collective-permute-done.3.rest_1_ = bf16[2,512,128]{2,1,0:T(8,128)(2,1)S(1)} collective-permute-done((bf16[2,512,128]{2,1,0:T(8,128)(2,1)S(1)}, bf16[2,512,128]{2,1,0:T(8,128)(2,1)S(1)}, u32[]{:S(2)}, u32[]{:S(2)}) %collective-permute-start.3) | collective-permute-done | bytes 262176 | tf_op jit(solution)/shard_map/ppermute | solution.py:242
  52.5 5.3 %collective-permute-start.4 = (bf16[2,512,128]{2,1,0:T(8,128)(2,1)S(1)}, bf16[2,512,128]{2,1,0:T(8,128)(2,1)}, u32[]{:S(2)}, u32[]{:S(2)}) collective-permute-start(bf16[2,512,128]{2,1,0:T(8,128)(2,1)S(1)} %collective-permute-done.3.rest_1_), channel_id=1, source_target_pairs={{0,224},{32,0},{64,32},{96,64},{128,96},{160,128},{192,160},{224,1... | collective-permute-start | bytes 786440 | tf_op jit(solution)/shard_map/ppermute | solution.py:242
  57.8 0.0 collective-permute-done.7.rest_0_
  57.8 1.9 %collective-permute-start.8 = (bf16[2,512,128]{2,1,0:T(8,128)(2,1)S(1)}, bf16[2,512,128]{2,1,0:T(8,128)(2,1)}, u32[]{:S(2)}, u32[]{:S(2)}) collective-permute-start(bf16[2,512,128]{2,1,0:T(8,128)(2,1)S(1)} %collective-permute-done.7.rest_0_), channel_id=1, source_target_pairs={{0,32},{32,64},{64,96},{96,128},{128,160},{160,192},{192,224},{224... | collective-permute-start | bytes 786440 | tf_op jit(solution)/shard_map/ppermute | solution.py:242
  59.7 0.0 all-to-all-done.mine
  59.7 2.0 %own_part.3 = (f32[512,256]{1,0:T(8,128)S(1)}, bf16[1536,256]{1,0:T(8,128)(2,1)S(1)}) custom-call(s32[3]{0:T(128)S(1)} %pad_add_fusion.place, bf16[4,4,512,128]{3,2,1,0:T(8,128)(2,1)S(1)} %all-to-all-done.mine, bf16[2,512,128]{2,1,0:T(8,128)(2,1)S(1)} %pad_maximum_fusion.rest_0_, bf16[2,512,128]{2,1,0:T(8,128)(2,1)S(1)} %collective-permute-done.1.rest_1_, ...), custom_call_target="tpu_custom_call" | custom-call | flops 34359738368 | bytes 8388608 | tf_op jit(solution)/shard_map/own_part/pallas_call | solution.py:192
  61.7 0.0 collective-permute-done.4.rest_1_
  61.8 4.6 %collective-permute-start.5 = (bf16[2,512,128]{2,1,0:T(8,128)(2,1)}, bf16[2,512,128]{2,1,0:T(8,128)(2,1)S(1)}, u32[]{:S(2)}, u32[]{:S(2)}) collective-permute-start(bf16[2,512,128]{2,1,0:T(8,128)(2,1)} %collective-permute-done.4.rest_1_), channel_id=1, source_target_pairs={{0,224},{32,0},{64,32},{96,64},{128,96},{160,128},{192,160},{224,1... | collective-permute-start | bytes 786440 | tf_op jit(solution)/shard_map/ppermute | solution.py:242
  66.4 8.5 %collective-permute-start.6 = (bf16[4,4,512,128]{3,2,1,0:T(8,128)(2,1)S(1)}, bf16[4,4,512,128]{3,2,1,0:T(8,128)(2,1)S(1)}, u32[]{:S(2)}, u32[]{:S(2)}) collective-permute-start(bf16[4,4,512,128]{3,2,1,0:T(8,128)(2,1)S(1)} %all-to-all-done.mine), channel_id=1, source_target_pairs={{0,1},{1,0},{2,3},{3,2},{4,5},{5,4},{6,7},{7,6},{8,9},{9,8},{10,11... | collective-permute-start | bytes 6291464 | tf_op jit(solution)/shard_map/ppermute | solution.py:242
  74.9 1.7 %own_part.4 = (f32[512,256]{1,0:T(8,128)S(1)}, bf16[1024,256]{1,0:T(8,128)(2,1)S(1)}) custom-call(s32[3]{0:T(128)S(1)} %pad_add_fusion.place, bf16[4,4,512,128]{3,2,1,0:T(8,128)(2,1)S(1)} %all-to-all-done.mine, bf16[2,512,128]{2,1,0:T(8,128)(2,1)S(1)} %collective-permute-done.7.rest_0_, bf16[2,512,128]{2,1,0:T(8,128)(2,1)S(1)} %collective-permute-done.3.rest_1_, ...), custom_call_target="tpu_custom_call" | custom-call | flops 34359738368 | bytes 8388608 | tf_op jit(solution)/shard_map/own_part/pallas_call | solution.py:192
  76.6 0.0 collective-permute-done.8.rest_0_
  76.6 2.3 %own_part.5 = (f32[512,256]{1,0:T(8,128)S(1)}, bf16[1024,256]{1,0:T(8,128)(2,1)S(1)}, bf16[512,512]{1,0:T(8,128)(2,1)S(1)}) custom-call(s32[3]{0:T(128)S(1)} %pad_add_fusion.place, bf16[4,4,512,128]{3,2,1,0:T(8,128)(2,1)S(1)} %all-to-all-done.mine, bf16[2,512,128]{2,1,0:T(8,128)(2,1)} %collective-permute-done.8.rest_0_, ...), custom_call_target="tpu_custom_call" | custom-call | flops 1073741824 | bytes 8388608 | tf_op jit(solution)/shard_map/own_part/pallas_call | solution.py:192
  78.9 0.0 collective-permute-done.6.others
  78.9 0.0 copy-start
  78.9 2.5 %other_part.1 = (f32[512,256]{1,0:T(8,128)S(1)}, bf16[512,512]{1,0:T(8,128)(2,1)S(1)}) custom-call(s32[3]{0:T(128)S(1)} %pad_add_fusion.place, bf16[4,4,512,128]{3,2,1,0:T(8,128)(2,1)S(1)} %collective-permute-done.6.others, f32[512,256]{1,0:T(8,128)S(1)} %get-tuple-element.28.start, bf16[1536,256]{1,0:T(8,128)(2,1)S(1)} %get-tuple-element.29.rest_0_, ...), custom_call_target="tpu_custom_call" | custom-call | flops 1073741824 | bytes 8388608 | tf_op jit(solution)/shard_map/other_part/pallas_call | solution.py:192
  81.4 0.0 collective-permute-done.5.last
  81.4 0.0 copy-done
  81.4 1.3 %last_part.1 = (f32[512,256]{1,0:T(8,128)S(1)}, f32[1,256]{1,0:T(1,128)S(1)}) custom-call(s32[3]{0:T(128)S(1)} %pad_add_fusion.place, s32[2,4]{1,0:T(2,128)S(1)} %bitcast.7, bf16[2,512,128]{2,1,0:T(8,128)(2,1)S(1)} %collective-permute-done.5.last, f32[512,256]{1,0:T(8,128)S(1)} %get-tuple-element.32.start, bf16[512,512]{1,0:T(8,128)(2,1)S(1)} %get-tuple-element.33.far_mine, ...), custom_call_target="tpu_custom_call" | custom-call | flops 1073741824 | bytes 8388608 | tf_op jit(solution)/shard_map/last_part/pallas_call | solution.py:192
  82.8 15.5 %all_to_all.11 = f32[16,1,256]{2,1,0:T(1,128)S(1)} all-to-all(f32[16,1,256]{2,1,0:T(1,128)S(1)} %broadcast_in_dim.10), channel_id=1, replica_groups=mesh['zh'=2,'y'=8,'x'=4,'zl'=4,'core'=2] {'zh','y'}, dimensions={0} | all-to-all | bytes 32768 | tf_op jit(solution)/shard_map/all_to_all | solution.py:271
  98.3 0.8 maximum_convert_fusion
  (3 shorter events, 0.1 us)
Async XLA Ops:
  1.7 28.0 %collective-permute-start = (bf16[1,512,128]{2,1,0:T(8,128)(2,1)}, bf16[1,512,128]{2,1,0:T(8,128)(2,1)S(1)}, u32[]{:S(2)}, u32[]{:S(2)}) collective-permute-start(bf16[1,512,128]{2,1,0:T(8,128)(2,1)} %pack_tiles.1), channel_id=1, source_target_pairs={{0,256},{256,0},{1,257},{257,1},{2,258},{258,2},{3,259},{259,3},{4... | collective-permute-start | bytes 393224 | tf_op jit(solution)/shard_map/ppermute | solution.py:242
  31.4 4.0 %copy-start.1 = (bf16[1,512,128]{2,1,0:T(8,128)(2,1)S(1)}, bf16[1,512,128]{2,1,0:T(8,128)(2,1)}, u32[]{:S(2)}) copy-start(bf16[1,512,128]{2,1,0:T(8,128)(2,1)} %pack_tiles.1) | copy-start | bytes 393220
  31.4 28.3 %all-to-all-start = ((bf16[4,4,512,128]{3,2,1,0:T(8,128)(2,1)}), bf16[4,4,512,128]{3,2,1,0:T(8,128)(2,1)S(1)}, u32[]{:S(2)}, u32[]{:S(2)}) async-start(bf16[4,4,512,128]{3,2,1,0:T(8,128)(2,1)} %broadcast_in_dim.4), calls=%async_computation | async-start | bytes 4194304 | tf_op jit(solution)/shard_map/all_to_all | solution.py:252
  35.5 8.4 %collective-permute-start.2 = (bf16[2,512,128]{2,1,0:T(8,128)(2,1)S(1)}, bf16[2,512,128]{2,1,0:T(8,128)(2,1)S(1)}, u32[]{:S(2)}, u32[]{:S(2)}) collective-permute-start(bf16[2,512,128]{2,1,0:T(8,128)(2,1)S(1)} %pad_maximum_fusion.rest_0_), channel_id=1, source_target_pairs={{0,224},{32,0},{64,32},{96,64},{128,96},{160,128},{192,160},{224,1... | collective-permute-start | bytes 786440 | tf_op jit(solution)/shard_map/ppermute | solution.py:242
  40.6 8.6 %collective-permute-start.1 = (bf16[2,512,128]{2,1,0:T(8,128)(2,1)S(1)}, bf16[2,512,128]{2,1,0:T(8,128)(2,1)S(1)}, u32[]{:S(2)}, u32[]{:S(2)}) collective-permute-start(bf16[2,512,128]{2,1,0:T(8,128)(2,1)S(1)} %pad_maximum_fusion.rest_0_), channel_id=1, source_target_pairs={{0,32},{32,64},{64,96},{96,128},{128,160},{160,192},{192,224},{224... | collective-permute-start | bytes 786440 | tf_op jit(solution)/shard_map/ppermute | solution.py:242
  43.8 8.6 %collective-permute-start.3 = (bf16[2,512,128]{2,1,0:T(8,128)(2,1)S(1)}, bf16[2,512,128]{2,1,0:T(8,128)(2,1)S(1)}, u32[]{:S(2)}, u32[]{:S(2)}) collective-permute-start(bf16[2,512,128]{2,1,0:T(8,128)(2,1)S(1)} %collective-permute-done.2.rest_2_), channel_id=1, source_target_pairs={{0,224},{32,0},{64,32},{96,64},{128,96},{160,128},{192,160},{224,1... | collective-permute-start | bytes 786440 | tf_op jit(solution)/shard_map/ppermute | solution.py:242
  49.2 8.6 %collective-permute-start.7 = (bf16[2,512,128]{2,1,0:T(8,128)(2,1)S(1)}, bf16[2,512,128]{2,1,0:T(8,128)(2,1)S(1)}, u32[]{:S(2)}, u32[]{:S(2)}) collective-permute-start(bf16[2,512,128]{2,1,0:T(8,128)(2,1)S(1)} %collective-permute-done.1.rest_1_), channel_id=1, source_target_pairs={{0,32},{32,64},{64,96},{96,128},{128,160},{160,192},{192,224},{224... | collective-permute-start | bytes 786440 | tf_op jit(solution)/shard_map/ppermute | solution.py:242
  52.5 9.3 %collective-permute-start.4 = (bf16[2,512,128]{2,1,0:T(8,128)(2,1)S(1)}, bf16[2,512,128]{2,1,0:T(8,128)(2,1)}, u32[]{:S(2)}, u32[]{:S(2)}) collective-permute-start(bf16[2,512,128]{2,1,0:T(8,128)(2,1)S(1)} %collective-permute-done.3.rest_1_), channel_id=1, source_target_pairs={{0,224},{32,0},{64,32},{96,64},{128,96},{160,128},{192,160},{224,1... | collective-permute-start | bytes 786440 | tf_op jit(solution)/shard_map/ppermute | solution.py:242
  57.8 18.8 %collective-permute-start.8 = (bf16[2,512,128]{2,1,0:T(8,128)(2,1)S(1)}, bf16[2,512,128]{2,1,0:T(8,128)(2,1)}, u32[]{:S(2)}, u32[]{:S(2)}) collective-permute-start(bf16[2,512,128]{2,1,0:T(8,128)(2,1)S(1)} %collective-permute-done.7.rest_0_), channel_id=1, source_target_pairs={{0,32},{32,64},{64,96},{96,128},{128,160},{160,192},{192,224},{224... | collective-permute-start | bytes 786440 | tf_op jit(solution)/shard_map/ppermute | solution.py:242
  61.8 19.6 %collective-permute-start.5 = (bf16[2,512,128]{2,1,0:T(8,128)(2,1)}, bf16[2,512,128]{2,1,0:T(8,128)(2,1)S(1)}, u32[]{:S(2)}, u32[]{:S(2)}) collective-permute-start(bf16[2,512,128]{2,1,0:T(8,128)(2,1)} %collective-permute-done.4.rest_1_), channel_id=1, source_target_pairs={{0,224},{32,0},{64,32},{96,64},{128,96},{160,128},{192,160},{224,1... | collective-permute-start | bytes 786440 | tf_op jit(solution)/shard_map/ppermute | solution.py:242
  66.4 12.5 %collective-permute-start.6 = (bf16[4,4,512,128]{3,2,1,0:T(8,128)(2,1)S(1)}, bf16[4,4,512,128]{3,2,1,0:T(8,128)(2,1)S(1)}, u32[]{:S(2)}, u32[]{:S(2)}) collective-permute-start(bf16[4,4,512,128]{3,2,1,0:T(8,128)(2,1)S(1)} %all-to-all-done.mine), channel_id=1, source_target_pairs={{0,1},{1,0},{2,3},{3,2},{4,5},{5,4},{6,7},{7,6},{8,9},{9,8},{10,11... | collective-permute-start | bytes 6291464 | tf_op jit(solution)/shard_map/ppermute | solution.py:242
  78.9 2.5 %copy-start = (s32[4,2]{0,1:T(2,128)S(1)}, s32[4,2]{0,1:T(2,128)}, u32[]{:S(2)}) copy-start(s32[4,2]{0,1:T(2,128)} %param.5) | copy-start | bytes 100

commit v6 on v5

--- a/solution.py
+++ b/solution.py
@@ -144,11 +144,12 @@
         spread_band(mine, table, entries, places, far_dense, 0)
 
 
-def other_kernel(ny, order, place, others, start, *rest):
-    spares, (acc, far_dense, heads, table, a_dense) = rest[:len(order)], rest[len(order):]
-    hi, y = place[0], place[1]
+def final_kernel(ny, order, place, keep, others, last, start, far_mine, *rest):
+    spares, (out, totals, heads, table, last_heads, last_table, a_dense, b_dense, acc) = rest[:len(order)], rest[len(order):]
+    hi, y, core = place[0], place[1], place[2]
     nl = others.shape[1]
     read_slots(all_blocks(others), heads, table)
+    read_slots([(last, (z,)) for z in range(2)], last_heads, last_table)
     total = start[...]
     col = 0
     for js, spare in zip(order, spares):
@@ -157,18 +158,12 @@
             spread_band(others, table, entries, places, a_dense, col + n * DEEP)
         total += jnp.dot(a_dense[:, col:col + depth], spare[...], preferred_element_type=jnp.float32)
         col += depth
-    acc[...] = total
     ((entries, places),) = sources(hi, y, ny, nl, [ny // 2])
-    spread_band(others, table, entries, places, far_dense, 0)
-
-
-def last_kernel(place, keep, last, start, far_mine, far_others, out, totals, heads, table, b_dense, acc):
-    core = place[2]
-    read_slots([(last, (z,)) for z in range(2)], heads, table)
+    spread_band(others, table, entries, places, a_dense, col)
     mine_rows, others_rows = b_dense.at[pl.ds(0, DEEP)], b_dense.at[pl.ds(DEEP, DEEP)]
-    spread_panel(last, table, 0, core, ((mine_rows, 0), (others_rows, 0)))
-    total = start[...] + jnp.dot(far_mine[...], mine_rows[...], preferred_element_type=jnp.float32)
-    acc[...] = total + jnp.dot(far_others[...], others_rows[...], preferred_element_type=jnp.float32)
+    spread_panel(last, last_table, 0, core, ((mine_rows, 0), (others_rows, 0)))
+    total += jnp.dot(far_mine[...], mine_rows[...], preferred_element_type=jnp.float32)
+    acc[...] = total + jnp.dot(a_dense[:, col:col + DEEP], others_rows[...], preferred_element_type=jnp.float32)
     for s in range(CB):
         total = jnp.zeros((1, TILE), jnp.float32)
         for r in range(RB):
@@ -178,6 +173,26 @@
             out[at] = inflated
             total = total + jnp.sum(inflated, axis=0, keepdims=True)
         totals[:, s * TILE:(s + 1) * TILE] = total
+
+
+def copies_kernel(line, out, sems):
+    copies = [pltpu.make_async_copy(line, out.at[i], sems.at[i]) for i in range(out.shape[0])]
+    for copy in copies:
+        copy.start()
+    for copy in copies:
+        copy.wait()
+
+
+def copies_of(line, count):
+    return pl.pallas_call(
+        copies_kernel,
+        out_shape=jax.ShapeDtypeStruct((count, *line.shape), line.dtype),
+        in_specs=[VMEM],
+        out_specs=pl.BlockSpec(memory_space=pl.ANY),
+        scratch_shapes=[pltpu.SemaphoreType.DMA((count,))],
+        compiler_params=pltpu.CompilerParams(vmem_limit_bytes=8 * 2**20),
+        name="line_copies",
+    )(line)
 
 
 def scratch(entries, *more):
@@ -220,21 +235,20 @@
         pltpu.VMEM(rows_of(len(js)), jnp.bfloat16),
     )
     arrays = [mine, *panels] + ([start] if more else [])
-    return kernel_call(functools.partial(own_kernel, ny, js, more, far), "own_part", outs, [place], arrays, shapes, 2**30 if far else 2**35)
-
-
-def other_part(ny, order, place, others, start, spares):
+    return kernel_call(functools.partial(own_kernel, ny, js, more, far), "own_part", outs, [place], arrays, shapes, 2**35)
+
+
+def final_part(ny, order, place, keep, others, last, start, far_mine, spares):
     chips = others.shape[0] * others.shape[1]
-    shapes = scratch(chips, pltpu.VMEM((RB * TILE, sum(map(len, order)) * DEEP), jnp.bfloat16))
-    arrays = [others, start, *spares]
-    return kernel_call(functools.partial(other_kernel, ny, order), "other_part", (BLOCK_SUM, FAR), [place], arrays, shapes)
-
-
-def last_part(place, keep, last, start, far_mine, far_others):
     outs = (BLOCK_SUM, jax.ShapeDtypeStruct((1, CB * TILE), jnp.float32))
-    shapes = scratch(2, pltpu.VMEM(rows_of(2), jnp.bfloat16), pltpu.VMEM(BLOCK, jnp.float32))
-    arrays = [last, start, far_mine, far_others]
-    return kernel_call(last_kernel, "last_part", outs, [place, keep.T], arrays, shapes)
+    shapes = scratch(chips) + scratch(
+        2,
+        pltpu.VMEM((RB * TILE, ny * DEEP), jnp.bfloat16),
+        pltpu.VMEM(rows_of(2), jnp.bfloat16),
+        pltpu.VMEM(BLOCK, jnp.float32),
+    )
+    arrays = [others, last, start, far_mine, *spares]
+    return kernel_call(functools.partial(final_kernel, ny, order), "final_part", outs, [place, keep.T], arrays, shapes)
 
 
 def shifted(array, axis, by):
@@ -249,7 +263,7 @@
     line = lax.all_gather(packed, "zl", tiled=True)
     line, other = lax.optimization_barrier((line, other))
     own = jnp.concatenate([packed, other])
-    mine = lax.all_to_all(jnp.broadcast_to(line, (nx, *line.shape)), "x", 0, 0)
+    mine = lax.all_to_all(copies_of(line, nx), "x", 0, 0)
     place = jnp.stack([lax.axis_index(a) for a in ("zh", "y", "core")])
     half = ny // 2
     panels = {0: own}
@@ -257,16 +271,13 @@
         panels[i] = shifted(panels[i - 1], "y", 1)
         panels[ny - i] = shifted(panels[(ny - i + 1) % ny], "y", -1)
     first = [j for j in range(ny) if min(j, ny - j) < half - 2]
-    second = [half - 2, half + 2]
-    late = [half - 1, half + 1]
+    late = [half - 2, half + 2, half - 1, half + 1]
     start, spare = own_part(ny, first, place, mine, [panels[j] for j in first])
     sent, start, panels[half + 1] = lax.optimization_barrier((mine, start, panels[half + 1]))
     others = shifted(sent, "core", 1)
-    start, second_spare = own_part(ny, second, place, mine, [panels[j] for j in second], start)
     last = shifted(panels[half + 1], "y", -1)
     start, late_spare, far_mine = own_part(ny, late, place, mine, [panels[j] for j in late], start, True)
-    start, far_others = other_part(ny, [first, second, late], place, others, start, [spare, second_spare, late_spare])
-    inflated, totals = last_part(place, out_pattern, last, start, far_mine, far_others)
+    inflated, totals = final_part(ny, [first, late], place, out_pattern, others, last, start, far_mine, [spare, late_spare])
     copies = jnp.broadcast_to(totals, (ny * lax.axis_size("zh"), totals.shape[1]))
     column_totals = jnp.sum(lax.all_to_all(copies, BLK, 0, 0, tiled=True), axis=0, keepdims=True)
     scaled = inflated / column_totals * float(SIZES[0] * SIZES[1] * RB * TILE)

time: 100 us -> 98.7 us (0.987)
  local copies, waits for them, and re-layouts: 1.76 us -> 0.02 us
    pallas_call x5 -> x3, Pallas kernels: 9.8 us -> 7.75 us  [kernel_call(): pl.pallas_call(kernel, out_shape=outs, in_specs=[SMEM] * len(smems) + [VM...]
    broadcast_in_dim x1 -> x0, local copies, waits for them, and re-layouts: 1.74 us -> none  [body(): mine = lax.all_to_all(jnp.broadcast_to(line, (nx, *line.shape)), 'x', 0, 0)]
    pallas_call x0 -> x1, Pallas kernels: none -> 1.36 us  [copies_of(): pl.pallas_call(copies_kernel, out_shape=jax.ShapeDtypeStruct((count, *lin...]
  transfers between devices with their start and end apart: 10 -> 10, of which waited for: 2 -> 3; matrix products, arithmetic and copies ran while one was open for 0% -> 0% of each run, Pallas kernels for 9% -> 5%
where the time goes in v6:
time: 98.7 us; the launch traced here: 97.3 us
  starting transfers between devices  50.2 us (51%)
  blocking collectives  31.9 us (32%)
  Pallas kernels  10.8 us (11%)
  waiting for transfers between devices  3.35 us (3%)
    ppermute x9, starting transfers between devices, shifted(): return lax.ppermute(array, axis, [(i, (i + by) % n) for i in range(n)])  46.1 us
    all_gather x1, blocking collectives, body(): line = lax.all_gather(packed, 'zl', tiled=True)  16.5 us
    all_to_all x1, blocking collectives, body(): lax.all_to_all(copies, BLK, 0, 0, tiled=True)  15.4 us
    pallas_call x3, Pallas kernels, kernel_call(): pl.pallas_call(kernel, out_shape=outs, in_specs=[SMEM] * len(smems) + [VM...  7.75 us
    all_to_all x1, starting transfers between devices, body(): mine = lax.all_to_all(copies_of(line, nx), 'x', 0, 0)  4.03 us
    ppermute x9, waiting for transfers between devices, shifted(): return lax.ppermute(array, axis, [(i, (i + by) % n) for i in range(n)])  3.34 us
  transfers between devices with their start and end apart: 10, of which 3 were waited for; matrix products, arithmetic and copies ran while one was open for 0% of the time, Pallas kernels for 5%

profile of v6, /device:TPU:1, one launch (start us, length us, event | category | flops | bytes accessed | tf_op | source)
XLA Modules:
  0.0 97.3 jit_solution(667610097813292527)
XLA Ops:
  0.0 1.7 %pack_tiles.1 = bf16[1,512,128]{2,1,0:T(8,128)(2,1)} custom-call(s32[2,4]{1,0:T(2,128)} %bitcast.8, bf16[512,256]{1,0:T(8,128)(2,1)} %matrix.1), custom_call_target="tpu_custom_call" | custom-call | tf_op jit(solution)/shard_map/pack_tiles/pallas_call | solution.py:58
  1.7 11.4 %collective-permute-start = (bf16[1,512,128]{2,1,0:T(8,128)(2,1)}, bf16[1,512,128]{2,1,0:T(8,128)(2,1)S(1)}, u32[]{:S(2)}, u32[]{:S(2)}) collective-permute-start(bf16[1,512,128]{2,1,0:T(8,128)(2,1)} %pack_tiles.1), channel_id=1, source_target_pairs={{0,256},{256,0},{1,257},{257,1},{2,258},{258,2},{3,259},{259,3},{4... | collective-permute-start | bytes 393224 | tf_op jit(solution)/shard_map/ppermute | solution.py:256
  13.2 16.5 %all_gather.3.line = bf16[4,512,128]{2,1,0:T(8,128)(2,1)S(1)} all-gather(bf16[1,512,128]{2,1,0:T(8,128)(2,1)} %pack_tiles.1), channel_id=1, replica_groups=mesh['zh'=2,'y'=8,'x'=4,'zl'=4,'core'=2] {'zl'}, dimensions={0}, use_global_device_ids=true | all-gather | bytes 655360 | tf_op jit(solution)/shard_map/all_gather | solution.py:263
  29.7 0.0 collective-permute-done
  29.7 1.4 %line_copies.1 = bf16[4,4,512,128]{3,2,1,0:T(8,128)(2,1)} custom-call(bf16[4,512,128]{2,1,0:T(8,128)(2,1)S(1)} %all_gather.3.line), custom_call_target="tpu_custom_call" | custom-call | tf_op jit(solution)/shard_map/line_copies/pallas_call | solution.py:187
  31.0 0.0 copy-start.1
  31.0 4.0 %all-to-all-start = ((bf16[4,4,512,128]{3,2,1,0:T(8,128)(2,1)}), bf16[4,4,512,128]{3,2,1,0:T(8,128)(2,1)S(1)}, u32[]{:S(2)}, u32[]{:S(2)}) async-start(bf16[4,4,512,128]{3,2,1,0:T(8,128)(2,1)} %line_copies.1), calls=%async_computation | async-start | bytes 4194304 | tf_op jit(solution)/shard_map/all_to_all | solution.py:266
  35.1 0.0 copy-done.1
  35.1 5.1 %collective-permute-start.2 = (bf16[2,512,128]{2,1,0:T(8,128)(2,1)S(1)}, bf16[2,512,128]{2,1,0:T(8,128)(2,1)S(1)}, u32[]{:S(2)}, u32[]{:S(2)}) collective-permute-start(bf16[2,512,128]{2,1,0:T(8,128)(2,1)S(1)} %pad_maximum_fusion.rest_0_), channel_id=1, source_target_pairs={{0,224},{32,0},{64,32},{96,64},{128,96},{160,128},{192,160},{224,1... | collective-permute-start | bytes 786440 | tf_op jit(solution)/shard_map/ppermute | solution.py:256
  40.2 1.9 %collective-permute-start.1 = (bf16[2,512,128]{2,1,0:T(8,128)(2,1)S(1)}, bf16[2,512,128]{2,1,0:T(8,128)(2,1)S(1)}, u32[]{:S(2)}, u32[]{:S(2)}) collective-permute-start(bf16[2,512,128]{2,1,0:T(8,128)(2,1)S(1)} %pad_maximum_fusion.rest_0_), channel_id=1, source_target_pairs={{0,32},{32,64},{64,96},{96,128},{128,160},{160,192},{192,224},{224... | collective-permute-start | bytes 786440 | tf_op jit(solution)/shard_map/ppermute | solution.py:256
  42.1 1.4 %collective-permute-done.2.rest_2_ = bf16[2,512,128]{2,1,0:T(8,128)(2,1)S(1)} collective-permute-done((bf16[2,512,128]{2,1,0:T(8,128)(2,1)S(1)}, bf16[2,512,128]{2,1,0:T(8,128)(2,1)S(1)}, u32[]{:S(2)}, u32[]{:S(2)}) %collective-permute-start.2) | collective-permute-done | bytes 262176 | tf_op jit(solution)/shard_map/ppermute | solution.py:256
  43.5 5.3 %collective-permute-start.3 = (bf16[2,512,128]{2,1,0:T(8,128)(2,1)S(1)}, bf16[2,512,128]{2,1,0:T(8,128)(2,1)S(1)}, u32[]{:S(2)}, u32[]{:S(2)}) collective-permute-start(bf16[2,512,128]{2,1,0:T(8,128)(2,1)S(1)} %collective-permute-done.2.rest_2_), channel_id=1, source_target_pairs={{0,224},{32,0},{64,32},{96,64},{128,96},{160,128},{192,160},{224,1... | collective-permute-start | bytes 786440 | tf_op jit(solution)/shard_map/ppermute | solution.py:256
  48.8 0.0 collective-permute-done.1.rest_1_
  48.8 1.9 %collective-permute-start.7 = (bf16[2,512,128]{2,1,0:T(8,128)(2,1)S(1)}, bf16[2,512,128]{2,1,0:T(8,128)(2,1)S(1)}, u32[]{:S(2)}, u32[]{:S(2)}) collective-permute-start(bf16[2,512,128]{2,1,0:T(8,128)(2,1)S(1)} %collective-permute-done.1.rest_1_), channel_id=1, source_target_pairs={{0,32},{32,64},{64,96},{96,128},{128,160},{160,192},{192,224},{224... | collective-permute-start | bytes 786440 | tf_op jit(solution)/shard_map/ppermute | solution.py:256
  50.8 0.1 pad_add_fusion.place
  50.8 1.3 %collective-permute-done.3.rest_1_ = bf16[2,512,128]{2,1,0:T(8,128)(2,1)S(1)} collective-permute-done((bf16[2,512,128]{2,1,0:T(8,128)(2,1)S(1)}, bf16[2,512,128]{2,1,0:T(8,128)(2,1)S(1)}, u32[]{:S(2)}, u32[]{:S(2)}) %collective-permute-start.3) | collective-permute-done | bytes 262176 | tf_op jit(solution)/shard_map/ppermute | solution.py:256
  52.1 5.3 %collective-permute-start.4 = (bf16[2,512,128]{2,1,0:T(8,128)(2,1)S(1)}, bf16[2,512,128]{2,1,0:T(8,128)(2,1)}, u32[]{:S(2)}, u32[]{:S(2)}) collective-permute-start(bf16[2,512,128]{2,1,0:T(8,128)(2,1)S(1)} %collective-permute-done.3.rest_1_), channel_id=1, source_target_pairs={{0,224},{32,0},{64,32},{96,64},{128,96},{160,128},{192,160},{224,1... | collective-permute-start | bytes 786440 | tf_op jit(solution)/shard_map/ppermute | solution.py:256
  57.4 0.0 collective-permute-done.7.rest_0_
  57.4 1.9 %collective-permute-start.8 = (bf16[2,512,128]{2,1,0:T(8,128)(2,1)S(1)}, bf16[2,512,128]{2,1,0:T(8,128)(2,1)}, u32[]{:S(2)}, u32[]{:S(2)}) collective-permute-start(bf16[2,512,128]{2,1,0:T(8,128)(2,1)S(1)} %collective-permute-done.7.rest_0_), channel_id=1, source_target_pairs={{0,32},{32,64},{64,96},{96,128},{128,160},{160,192},{192,224},{224... | collective-permute-start | bytes 786440 | tf_op jit(solution)/shard_map/ppermute | solution.py:256
  59.4 0.0 all-to-all-done.mine
  59.4 2.0 %own_part.2 = (f32[512,256]{1,0:T(8,128)S(1)}, bf16[1536,256]{1,0:T(8,128)(2,1)S(1)}) custom-call(s32[3]{0:T(128)S(1)} %pad_add_fusion.place, bf16[4,4,512,128]{3,2,1,0:T(8,128)(2,1)S(1)} %all-to-all-done.mine, bf16[2,512,128]{2,1,0:T(8,128)(2,1)S(1)} %pad_maximum_fusion.rest_0_, bf16[2,512,128]{2,1,0:T(8,128)(2,1)S(1)} %collective-permute-done.1.rest_1_, ...), custom_call_target="tpu_custom_call" | custom-call | flops 34359738368 | bytes 8388608 | tf_op jit(solution)/shard_map/own_part/pallas_call | solution.py:207
  61.4 0.0 collective-permute-done.4.rest_3_
  61.4 0.0 copy-start
  61.4 4.7 %collective-permute-start.6 = (bf16[2,512,128]{2,1,0:T(8,128)(2,1)}, bf16[2,512,128]{2,1,0:T(8,128)(2,1)S(1)}, u32[]{:S(2)}, u32[]{:S(2)}) collective-permute-start(bf16[2,512,128]{2,1,0:T(8,128)(2,1)} %collective-permute-done.4.rest_3_), channel_id=1, source_target_pairs={{0,224},{32,0},{64,32},{96,64},{128,96},{160,128},{192,160},{224,1... | collective-permute-start | bytes 786440 | tf_op jit(solution)/shard_map/ppermute | solution.py:256
  66.2 8.5 %collective-permute-start.5 = (bf16[4,4,512,128]{3,2,1,0:T(8,128)(2,1)S(1)}, bf16[4,4,512,128]{3,2,1,0:T(8,128)(2,1)S(1)}, u32[]{:S(2)}, u32[]{:S(2)}) collective-permute-start(bf16[4,4,512,128]{3,2,1,0:T(8,128)(2,1)S(1)} %all-to-all-done.mine), channel_id=1, source_target_pairs={{0,1},{1,0},{2,3},{3,2},{4,5},{5,4},{6,7},{7,6},{8,9},{9,8},{10,11... | collective-permute-start | bytes 6291464 | tf_op jit(solution)/shard_map/ppermute | solution.py:256
  74.7 0.0 collective-permute-done.8.rest_2_
  74.7 3.1 %own_part.3 = (f32[512,256]{1,0:T(8,128)S(1)}, bf16[2048,256]{1,0:T(8,128)(2,1)S(1)}, bf16[512,512]{1,0:T(8,128)(2,1)S(1)}) custom-call(s32[3]{0:T(128)S(1)} %pad_add_fusion.place, bf16[4,4,512,128]{3,2,1,0:T(8,128)(2,1)S(1)} %all-to-all-done.mine, bf16[2,512,128]{2,1,0:T(8,128)(2,1)S(1)} %collective-permute-done.7.rest_0_, ...), custom_call_target="tpu_custom_call" | custom-call | flops 34359738368 | bytes 8388608 | tf_op jit(solution)/shard_map/own_part/pallas_call | solution.py:207
  77.8 0.0 collective-permute-done.6.last
  77.8 0.7 collective-permute-done.5.others
  78.4 0.0 copy-done
  78.4 2.7 %final_part.1 = (f32[512,256]{1,0:T(8,128)S(1)}, f32[1,256]{1,0:T(1,128)S(1)}) custom-call(s32[3]{0:T(128)S(1)} %pad_add_fusion.place, s32[2,4]{1,0:T(2,128)S(1)} %bitcast.6, bf16[4,4,512,128]{3,2,1,0:T(8,128)(2,1)S(1)} %collective-permute-done.5.others, bf16[2,512,128]{2,1,0:T(8,128)(2,1)S(1)} %collective-permute-done.6.last, ...), custom_call_target="tpu_custom_call" | custom-call | flops 1073741824 | bytes 8388608 | tf_op jit(solution)/shard_map/final_part/pallas_call | solution.py:207
  81.1 15.4 %all_to_all.11 = f32[16,1,256]{2,1,0:T(1,128)S(1)} all-to-all(f32[16,1,256]{2,1,0:T(1,128)S(1)} %broadcast_in_dim.2), channel_id=1, replica_groups=mesh['zh'=2,'y'=8,'x'=4,'zl'=4,'core'=2] {'zh','y'}, dimensions={0} | all-to-all | bytes 32768 | tf_op jit(solution)/shard_map/all_to_all | solution.py:282
  96.5 0.8 maximum_convert_fusion
  (3 shorter events, 0.1 us)
Async XLA Ops:
  1.7 28.0 %collective-permute-start = (bf16[1,512,128]{2,1,0:T(8,128)(2,1)}, bf16[1,512,128]{2,1,0:T(8,128)(2,1)S(1)}, u32[]{:S(2)}, u32[]{:S(2)}) collective-permute-start(bf16[1,512,128]{2,1,0:T(8,128)(2,1)} %pack_tiles.1), channel_id=1, source_target_pairs={{0,256},{256,0},{1,257},{257,1},{2,258},{258,2},{3,259},{259,3},{4... | collective-permute-start | bytes 393224 | tf_op jit(solution)/shard_map/ppermute | solution.py:256
  31.0 4.0 %copy-start.1 = (bf16[1,512,128]{2,1,0:T(8,128)(2,1)S(1)}, bf16[1,512,128]{2,1,0:T(8,128)(2,1)}, u32[]{:S(2)}) copy-start(bf16[1,512,128]{2,1,0:T(8,128)(2,1)} %pack_tiles.1) | copy-start | bytes 393220
  31.0 28.3 %all-to-all-start = ((bf16[4,4,512,128]{3,2,1,0:T(8,128)(2,1)}), bf16[4,4,512,128]{3,2,1,0:T(8,128)(2,1)S(1)}, u32[]{:S(2)}, u32[]{:S(2)}) async-start(bf16[4,4,512,128]{3,2,1,0:T(8,128)(2,1)} %line_copies.1), calls=%async_computation | async-start | bytes 4194304 | tf_op jit(solution)/shard_map/all_to_all | solution.py:266
  35.1 8.4 %collective-permute-start.2 = (bf16[2,512,128]{2,1,0:T(8,128)(2,1)S(1)}, bf16[2,512,128]{2,1,0:T(8,128)(2,1)S(1)}, u32[]{:S(2)}, u32[]{:S(2)}) collective-permute-start(bf16[2,512,128]{2,1,0:T(8,128)(2,1)S(1)} %pad_maximum_fusion.rest_0_), channel_id=1, source_target_pairs={{0,224},{32,0},{64,32},{96,64},{128,96},{160,128},{192,160},{224,1... | collective-permute-start | bytes 786440 | tf_op jit(solution)/shard_map/ppermute | solution.py:256
  40.2 8.6 %collective-permute-start.1 = (bf16[2,512,128]{2,1,0:T(8,128)(2,1)S(1)}, bf16[2,512,128]{2,1,0:T(8,128)(2,1)S(1)}, u32[]{:S(2)}, u32[]{:S(2)}) collective-permute-start(bf16[2,512,128]{2,1,0:T(8,128)(2,1)S(1)} %pad_maximum_fusion.rest_0_), channel_id=1, source_target_pairs={{0,32},{32,64},{64,96},{96,128},{128,160},{160,192},{192,224},{224... | collective-permute-start | bytes 786440 | tf_op jit(solution)/shard_map/ppermute | solution.py:256
  43.5 8.6 %collective-permute-start.3 = (bf16[2,512,128]{2,1,0:T(8,128)(2,1)S(1)}, bf16[2,512,128]{2,1,0:T(8,128)(2,1)S(1)}, u32[]{:S(2)}, u32[]{:S(2)}) collective-permute-start(bf16[2,512,128]{2,1,0:T(8,128)(2,1)S(1)} %collective-permute-done.2.rest_2_), channel_id=1, source_target_pairs={{0,224},{32,0},{64,32},{96,64},{128,96},{160,128},{192,160},{224,1... | collective-permute-start | bytes 786440 | tf_op jit(solution)/shard_map/ppermute | solution.py:256
  48.8 8.6 %collective-permute-start.7 = (bf16[2,512,128]{2,1,0:T(8,128)(2,1)S(1)}, bf16[2,512,128]{2,1,0:T(8,128)(2,1)S(1)}, u32[]{:S(2)}, u32[]{:S(2)}) collective-permute-start(bf16[2,512,128]{2,1,0:T(8,128)(2,1)S(1)} %collective-permute-done.1.rest_1_), channel_id=1, source_target_pairs={{0,32},{32,64},{64,96},{96,128},{128,160},{160,192},{192,224},{224... | collective-permute-start | bytes 786440 | tf_op jit(solution)/shard_map/ppermute | solution.py:256
  52.1 9.3 %collective-permute-start.4 = (bf16[2,512,128]{2,1,0:T(8,128)(2,1)S(1)}, bf16[2,512,128]{2,1,0:T(8,128)(2,1)}, u32[]{:S(2)}, u32[]{:S(2)}) collective-permute-start(bf16[2,512,128]{2,1,0:T(8,128)(2,1)S(1)} %collective-permute-done.3.rest_1_), channel_id=1, source_target_pairs={{0,224},{32,0},{64,32},{96,64},{128,96},{160,128},{192,160},{224,1... | collective-permute-start | bytes 786440 | tf_op jit(solution)/shard_map/ppermute | solution.py:256
  57.4 17.2 %collective-permute-start.8 = (bf16[2,512,128]{2,1,0:T(8,128)(2,1)S(1)}, bf16[2,512,128]{2,1,0:T(8,128)(2,1)}, u32[]{:S(2)}, u32[]{:S(2)}) collective-permute-start(bf16[2,512,128]{2,1,0:T(8,128)(2,1)S(1)} %collective-permute-done.7.rest_0_), channel_id=1, source_target_pairs={{0,32},{32,64},{64,96},{96,128},{128,160},{160,192},{192,224},{224... | collective-permute-start | bytes 786440 | tf_op jit(solution)/shard_map/ppermute | solution.py:256
  61.4 17.0 %copy-start = (s32[4,2]{0,1:T(2,128)S(1)}, s32[4,2]{0,1:T(2,128)}, u32[]{:S(2)}) copy-start(s32[4,2]{0,1:T(2,128)} %param.5) | copy-start | bytes 100
  61.4 16.3 %collective-permute-start.6 = (bf16[2,512,128]{2,1,0:T(8,128)(2,1)}, bf16[2,512,128]{2,1,0:T(8,128)(2,1)S(1)}, u32[]{:S(2)}, u32[]{:S(2)}) collective-permute-start(bf16[2,512,128]{2,1,0:T(8,128)(2,1)} %collective-permute-done.4.rest_3_), channel_id=1, source_target_pairs={{0,224},{32,0},{64,32},{96,64},{128,96},{160,128},{192,160},{224,1... | collective-permute-start | bytes 786440 | tf_op jit(solution)/shard_map/ppermute | solution.py:256
  66.2 12.3 %collective-permute-start.5 = (bf16[4,4,512,128]{3,2,1,0:T(8,128)(2,1)S(1)}, bf16[4,4,512,128]{3,2,1,0:T(8,128)(2,1)S(1)}, u32[]{:S(2)}, u32[]{:S(2)}) collective-permute-start(bf16[4,4,512,128]{3,2,1,0:T(8,128)(2,1)S(1)} %all-to-all-done.mine), channel_id=1, source_target_pairs={{0,1},{1,0},{2,3},{3,2},{4,5},{5,4},{6,7},{7,6},{8,9},{9,8},{10,11... | collective-permute-start | bytes 6291464 | tf_op jit(solution)/shard_map/ppermute | solution.py:256

commit v7 on v6

--- a/solution.py
+++ b/solution.py
@@ -64,8 +64,12 @@
     )(pattern.T, matrix)
 
 
+def slot_of(table, row, t):
+    return lax.shift_right_logical(table[row], SLOT_BITS * t) & (2**SLOT_BITS - 1)
+
+
 def put_tile(dense, at, ref, lead, table, row, t):
-    slot = lax.shift_right_logical(table[row], SLOT_BITS * t) & (2**SLOT_BITS - 1)
+    slot = slot_of(table, row, t)
     start = pl.multiple_of(jnp.minimum(slot, CAP - 1) * TILE, TILE)
     head = jnp.abs(ref[(*lead, pl.ds(start, HEAD), slice(None))])
     rest = ref[(*lead, pl.ds(pl.multiple_of(start + HEAD, HEAD), TILE - HEAD), slice(None))]
@@ -92,12 +96,18 @@
         table[i] = slots[i, 0]
 
 
-def spread_band(band, table, entries, places, dense, col):
-    for i, (entry, lead) in enumerate(zip(entries, places)):
-        for t in range(RB * CB):
-            r, s = divmod(t, CB)
-            k = col + (i * CB + s) * TILE
-            put_tile(dense, (r * TILE, k), band, lead, table, entry, t)
+def band_columns(band, table, entries, places):
+    rows = []
+    for r in range(RB):
+        tiles = []
+        for entry, lead in zip(entries, places):
+            for s in range(CB):
+                slot = slot_of(table, entry, r * CB + s)
+                start = pl.multiple_of(jnp.minimum(slot, CAP - 1) * TILE, TILE)
+                tile = jnp.abs(band[(*lead, pl.ds(start, TILE), slice(None))])
+                tiles.append(jnp.where(slot < CAP, tile, jnp.zeros_like(tile)))
+        rows.append(jnp.concatenate(tiles, axis=1))
+    return jnp.concatenate(rows, axis=0)
 
 
 def spread_panel(panel, table, entry, core, owns):
@@ -122,12 +132,8 @@
     return [(band, (x, k)) for x in range(band.shape[0]) for k in range(band.shape[1])]
 
 
-def own_kernel(ny, js, more, far, place, mine, *rest):
-    panels, rest = rest[:len(js)], rest[len(js):]
-    start, rest = (rest[0], rest[1:]) if more else (None, rest)
-    acc, spare, rest = rest[0], rest[1], rest[2:]
-    far_dense, rest = (rest[0], rest[1:]) if far else (None, rest)
-    heads, table, a_dense, b_dense = rest
+def own_kernel(ny, js, place, mine, *rest):
+    panels, (acc, spare, far_dense, heads, table, b_dense) = rest[:len(js)], rest[len(js):]
     hi, y, core = place[0], place[1], place[2]
     nl = mine.shape[1]
     blocks = all_blocks(mine)
@@ -136,34 +142,31 @@
     read_slots(blocks, heads, table)
     for n, (entries, places) in enumerate(sources(hi, y, ny, nl, js)):
         spread_panel(panels[n], table, chips + 2 * n, core, ((b_dense, n * DEEP), (spare, n * DEEP)))
-        spread_band(mine, table, entries, places, a_dense, n * DEEP)
-    total = jnp.dot(a_dense[...], b_dense[...], preferred_element_type=jnp.float32)
-    acc[...] = total if start is None else start[...] + total
-    if far:
-        ((entries, places),) = sources(hi, y, ny, nl, [ny // 2])
-        spread_band(mine, table, entries, places, far_dense, 0)
-
-
-def final_kernel(ny, order, place, keep, others, last, start, far_mine, *rest):
-    spares, (out, totals, heads, table, last_heads, last_table, a_dense, b_dense, acc) = rest[:len(order)], rest[len(order):]
+        columns = band_columns(mine, table, entries, places)
+        part = jnp.dot(columns, b_dense[n * DEEP:(n + 1) * DEEP], preferred_element_type=jnp.float32)
+        acc[...] = part if n == 0 else acc[...] + part
+    ((entries, places),) = sources(hi, y, ny, nl, [ny // 2])
+    far_dense[...] = band_columns(mine, table, entries, places)
+
+
+def final_kernel(
+    ny, js, place, keep, others, last, start, far_mine, spare, out, totals,
+    heads, table, last_heads, last_table, b_dense, acc,
+):
     hi, y, core = place[0], place[1], place[2]
     nl = others.shape[1]
     read_slots(all_blocks(others), heads, table)
     read_slots([(last, (z,)) for z in range(2)], last_heads, last_table)
-    total = start[...]
-    col = 0
-    for js, spare in zip(order, spares):
-        depth = len(js) * DEEP
-        for n, (entries, places) in enumerate(sources(hi, y, ny, nl, js)):
-            spread_band(others, table, entries, places, a_dense, col + n * DEEP)
-        total += jnp.dot(a_dense[:, col:col + depth], spare[...], preferred_element_type=jnp.float32)
-        col += depth
-    ((entries, places),) = sources(hi, y, ny, nl, [ny // 2])
-    spread_band(others, table, entries, places, a_dense, col)
+    acc[...] = start[...]
+    for n, (entries, places) in enumerate(sources(hi, y, ny, nl, js)):
+        columns = band_columns(others, table, entries, places)
+        acc[...] += jnp.dot(columns, spare[n * DEEP:(n + 1) * DEEP], preferred_element_type=jnp.float32)
     mine_rows, others_rows = b_dense.at[pl.ds(0, DEEP)], b_dense.at[pl.ds(DEEP, DEEP)]
     spread_panel(last, last_table, 0, core, ((mine_rows, 0), (others_rows, 0)))
-    total += jnp.dot(far_mine[...], mine_rows[...], preferred_element_type=jnp.float32)
-    acc[...] = total + jnp.dot(a_dense[:, col:col + DEEP], others_rows[...], preferred_element_type=jnp.float32)
+    acc[...] += jnp.dot(far_mine[...], mine_rows[...], preferred_element_type=jnp.float32)
+    ((entries, places),) = sources(hi, y, ny, nl, [ny // 2])
+    columns = band_columns(others, table, entries, places)
+    acc[...] += jnp.dot(columns, others_rows[...], preferred_element_type=jnp.float32)
     for s in range(CB):
         total = jnp.zeros((1, TILE), jnp.float32)
         for r in range(RB):
@@ -203,7 +206,7 @@
     ]
 
 
-def kernel_call(kernel, name, outs, smems, vmems, scratch_shapes, flops=2**30):
+def kernel_call(kernel, name, outs, smems, vmems, scratch_shapes):
     return pl.pallas_call(
         kernel,
         out_shape=outs,
@@ -211,7 +214,7 @@
         out_specs=jax.tree.map(lambda _: VMEM, outs),
         scratch_shapes=scratch_shapes,
         compiler_params=pltpu.CompilerParams(vmem_limit_bytes=24 * 2**20),
-        cost_estimate=pl.CostEstimate(flops=flops, bytes_accessed=2**23, transcendentals=0),
+        cost_estimate=pl.CostEstimate(flops=2**35, bytes_accessed=2**23, transcendentals=0),
         name=name,
     )(*smems, *vmems)
 
@@ -225,30 +228,42 @@
     return (count * DEEP, CB * TILE)
 
 
-def own_part(ny, js, place, mine, panels, start=None, far=False):
+def own_part(ny, js, place, mine, panels):
     chips = mine.shape[0] * mine.shape[1]
-    more = start is not None
-    outs = (BLOCK_SUM, jax.ShapeDtypeStruct(rows_of(len(js)), jnp.bfloat16)) + ((FAR,) if far else ())
+    outs = (BLOCK_SUM, jax.ShapeDtypeStruct(rows_of(len(js)), jnp.bfloat16), FAR)
     shapes = scratch(
         chips + 2 * len(js),
-        pltpu.VMEM((RB * TILE, len(js) * DEEP), jnp.bfloat16),
         pltpu.VMEM(rows_of(len(js)), jnp.bfloat16),
     )
-    arrays = [mine, *panels] + ([start] if more else [])
-    return kernel_call(functools.partial(own_kernel, ny, js, more, far), "own_part", outs, [place], arrays, shapes, 2**35)
-
-
-def final_part(ny, order, place, keep, others, last, start, far_mine, spares):
+    return kernel_call(functools.partial(own_kernel, ny, js), "own_part", outs, [place], [mine, *panels], shapes)
+
+
+def final_part(ny, js, place, keep, others, last, start, far_mine, spare):
     chips = others.shape[0] * others.shape[1]
     outs = (BLOCK_SUM, jax.ShapeDtypeStruct((1, CB * TILE), jnp.float32))
     shapes = scratch(chips) + scratch(
         2,
-        pltpu.VMEM((RB * TILE, ny * DEEP), jnp.bfloat16),
         pltpu.VMEM(rows_of(2), jnp.bfloat16),
         pltpu.VMEM(BLOCK, jnp.float32),
     )
-    arrays = [others, last, start, far_mine, *spares]
-    return kernel_call(functools.partial(final_kernel, ny, order), "final_part", outs, [place, keep.T], arrays, shapes)
+    arrays = [others, last, start, far_mine, spare]
+    return kernel_call(functools.partial(final_kernel, ny, js), "final_part", outs, [place, keep.T], arrays, shapes)
+
+
+def again_kernel(block, out):
+    out[...] = block[...]
+
+
+def again(block):
+    return pl.pallas_call(
+        again_kernel,
+        out_shape=jax.ShapeDtypeStruct(block.shape, block.dtype),
+        in_specs=[VMEM],
+        out_specs=VMEM,
+        compiler_params=pltpu.CompilerParams(vmem_limit_bytes=4 * 2**20),
+        cost_estimate=pl.CostEstimate(flops=2**36, bytes_accessed=2**20, transcendentals=0),
+        name="both_again",
+    )(block)
 
 
 def shifted(array, axis, by):
@@ -268,16 +283,14 @@
     half = ny // 2
     panels = {0: own}
     for i in range(1, half):
-        panels[i] = shifted(panels[i - 1], "y", 1)
+        panels[i] = shifted(again(own) if i == 1 else panels[i - 1], "y", 1)
         panels[ny - i] = shifted(panels[(ny - i + 1) % ny], "y", -1)
-    first = [j for j in range(ny) if min(j, ny - j) < half - 2]
-    late = [half - 2, half + 2, half - 1, half + 1]
-    start, spare = own_part(ny, first, place, mine, [panels[j] for j in first])
-    sent, start, panels[half + 1] = lax.optimization_barrier((mine, start, panels[half + 1]))
+    near = [j for j in range(ny) if j != half]
+    sent, panels[half + 1] = lax.optimization_barrier((mine, panels[half + 1]))
     others = shifted(sent, "core", 1)
     last = shifted(panels[half + 1], "y", -1)
-    start, late_spare, far_mine = own_part(ny, late, place, mine, [panels[j] for j in late], start, True)
-    inflated, totals = final_part(ny, [first, late], place, out_pattern, others, last, start, far_mine, [spare, late_spare])
+    start, spare, far_mine = own_part(ny, near, place, mine, [panels[j] for j in near])
+    inflated, totals = final_part(ny, near, place, out_pattern, others, last, start, far_mine, spare)
     copies = jnp.broadcast_to(totals, (ny * lax.axis_size("zh"), totals.shape[1]))
     column_totals = jnp.sum(lax.all_to_all(copies, BLK, 0, 0, tiled=True), axis=0, keepdims=True)
     scaled = inflated / column_totals * float(SIZES[0] * SIZES[1] * RB * TILE)

time: 98.7 us -> 97.2 us (0.985)
  starting transfers between devices: 50.2 us -> 45.3 us
  waiting for transfers between devices: 3.35 us -> 7.42 us
  Pallas kernels: 10.8 us -> 9.3 us
    ppermute x9, starting transfers between devices: 46.1 us -> 41.3 us  [shifted(): return lax.ppermute(array, axis, [(i, (i + by) % n) for i in range(n)])]
    all_to_all x1, waiting for transfers between devices: 0.01 us -> 3.2 us  [body(): mine = lax.all_to_all(copies_of(line, nx), 'x', 0, 0)]
    pallas_call x3 -> x2, Pallas kernels: 7.75 us -> 6.22 us  [kernel_call(): pl.pallas_call(kernel, out_shape=outs, in_specs=[SMEM] * len(smems) + [VM...]
where the time goes in v7:
time: 97.2 us; the launch traced here: 96.7 us
  starting transfers between devices  45.3 us (47%)
  blocking collectives  32.6 us (34%)
  Pallas kernels  9.3 us (10%)
  waiting for transfers between devices  7.42 us (8%)
  other arithmetic  1.83 us (2%)
    ppermute x9, starting transfers between devices, shifted(): return lax.ppermute(array, axis, [(i, (i + by) % n) for i in range(n)])  41.3 us
    all_gather x1, blocking collectives, body(): line = lax.all_gather(packed, 'zl', tiled=True)  16.5 us
    all_to_all x1, blocking collectives, body(): lax.all_to_all(copies, BLK, 0, 0, tiled=True)  16.1 us
    pallas_call x2, Pallas kernels, kernel_call(): pl.pallas_call(kernel, out_shape=outs, in_specs=[SMEM] * len(smems) + [VM...  6.22 us
    ppermute x9, waiting for transfers between devices, shifted(): return lax.ppermute(array, axis, [(i, (i + by) % n) for i in range(n)])  4.22 us
    all_to_all x1, starting transfers between devices, body(): mine = lax.all_to_all(copies_of(line, nx), 'x', 0, 0)  4.03 us
    all_to_all x1, waiting for transfers between devices, body(): mine = lax.all_to_all(copies_of(line, nx), 'x', 0, 0)  3.2 us
  transfers between devices with their start and end apart: 10, of which 3 were waited for; matrix products, arithmetic and copies ran while one was open for 0% of the time, Pallas kernels for 5%

profile of v7, /device:TPU:1, one launch (start us, length us, event | category | flops | bytes accessed | tf_op | source)
XLA Modules:
  0.0 96.7 jit_solution(1368062776102154132)
XLA Ops:
  0.0 1.7 %pack_tiles.1 = bf16[1,512,128]{2,1,0:T(8,128)(2,1)} custom-call(s32[2,4]{1,0:T(2,128)} %bitcast.8, bf16[512,256]{1,0:T(8,128)(2,1)} %matrix.1), custom_call_target="tpu_custom_call" | custom-call | tf_op jit(solution)/shard_map/pack_tiles/pallas_call | solution.py:58
  1.7 11.5 %collective-permute-start = (bf16[1,512,128]{2,1,0:T(8,128)(2,1)}, bf16[1,512,128]{2,1,0:T(8,128)(2,1)S(1)}, u32[]{:S(2)}, u32[]{:S(2)}) collective-permute-start(bf16[1,512,128]{2,1,0:T(8,128)(2,1)} %pack_tiles.1), channel_id=1, source_target_pairs={{0,256},{256,0},{1,257},{257,1},{2,258},{258,2},{3,259},{259,3},{4... | collective-permute-start | bytes 393224 | tf_op jit(solution)/shard_map/ppermute | solution.py:271
  13.2 16.5 %all_gather.3.line = bf16[4,512,128]{2,1,0:T(8,128)(2,1)S(1)} all-gather(bf16[1,512,128]{2,1,0:T(8,128)(2,1)} %pack_tiles.1), channel_id=1, replica_groups=mesh['zh'=2,'y'=8,'x'=4,'zl'=4,'core'=2] {'zl'}, dimensions={0}, use_global_device_ids=true | all-gather | bytes 655360 | tf_op jit(solution)/shard_map/all_gather | solution.py:278
  29.6 0.0 collective-permute-done
  29.6 0.9 pad_maximum_fusion.block.rest_0_
  30.6 5.0 %collective-permute-start.1 = (bf16[2,512,128]{2,1,0:T(8,128)(2,1)S(1)}, bf16[2,512,128]{2,1,0:T(8,128)(2,1)S(1)}, u32[]{:S(2)}, u32[]{:S(2)}) collective-permute-start(bf16[2,512,128]{2,1,0:T(8,128)(2,1)S(1)} %pad_maximum_fusion.block.rest_0_), channel_id=1, source_target_pairs={{0,224},{32,0},{64,32},{96,64},{128,96},{160,128},{192,160},{224,1... | collective-permute-start | bytes 786440 | tf_op jit(solution)/shard_map/ppermute | solution.py:271
  35.6 1.4 %line_copies.1 = bf16[4,4,512,128]{3,2,1,0:T(8,128)(2,1)} custom-call(bf16[4,512,128]{2,1,0:T(8,128)(2,1)S(1)} %all_gather.3.line), custom_call_target="tpu_custom_call" | custom-call | tf_op jit(solution)/shard_map/line_copies/pallas_call | solution.py:190
  36.9 4.0 %all-to-all-start = ((bf16[4,4,512,128]{3,2,1,0:T(8,128)(2,1)}), bf16[4,4,512,128]{3,2,1,0:T(8,128)(2,1)S(1)}, u32[]{:S(2)}, u32[]{:S(2)}) async-start(bf16[4,4,512,128]{3,2,1,0:T(8,128)(2,1)} %line_copies.1), calls=%async_computation | async-start | bytes 4194304 | tf_op jit(solution)/shard_map/all_to_all | solution.py:281
  41.0 1.9 %collective-permute-start.6 = (bf16[2,512,128]{2,1,0:T(8,128)(2,1)S(1)}, bf16[2,512,128]{2,1,0:T(8,128)(2,1)S(1)}, u32[]{:S(2)}, u32[]{:S(2)}) collective-permute-start(bf16[2,512,128]{2,1,0:T(8,128)(2,1)S(1)} %both_again.1), channel_id=1, source_target_pairs={{0,32},{32,64},{64,96},{96,128},{128,160},{160,192},{192,224},{224... | collective-permute-start | bytes 786440 | tf_op jit(solution)/shard_map/ppermute | solution.py:271
  42.9 0.0 collective-permute-done.1.rest_6_
  42.9 4.6 %collective-permute-start.2 = (bf16[2,512,128]{2,1,0:T(8,128)(2,1)S(1)}, bf16[2,512,128]{2,1,0:T(8,128)(2,1)S(1)}, u32[]{:S(2)}, u32[]{:S(2)}) collective-permute-start(bf16[2,512,128]{2,1,0:T(8,128)(2,1)S(1)} %collective-permute-done.1.rest_6_), channel_id=1, source_target_pairs={{0,224},{32,0},{64,32},{96,64},{128,96},{160,128},{192,160},{224,1... | collective-permute-start | bytes 786440 | tf_op jit(solution)/shard_map/ppermute | solution.py:271
  47.5 2.1 %collective-permute-done.6.rest_1_ = bf16[2,512,128]{2,1,0:T(8,128)(2,1)S(1)} collective-permute-done((bf16[2,512,128]{2,1,0:T(8,128)(2,1)S(1)}, bf16[2,512,128]{2,1,0:T(8,128)(2,1)S(1)}, u32[]{:S(2)}, u32[]{:S(2)}) %collective-permute-start.6) | collective-permute-done | bytes 262176 | tf_op jit(solution)/shard_map/ppermute | solution.py:271
  49.6 1.9 %collective-permute-start.7 = (bf16[2,512,128]{2,1,0:T(8,128)(2,1)S(1)}, bf16[2,512,128]{2,1,0:T(8,128)(2,1)S(1)}, u32[]{:S(2)}, u32[]{:S(2)}) collective-permute-start(bf16[2,512,128]{2,1,0:T(8,128)(2,1)S(1)} %collective-permute-done.6.rest_1_), channel_id=1, source_target_pairs={{0,32},{32,64},{64,96},{96,128},{128,160},{160,192},{192,224},{224... | collective-permute-start | bytes 786440 | tf_op jit(solution)/shard_map/ppermute | solution.py:271
  51.5 0.0 collective-permute-done.2.rest_5_
  51.5 4.6 %collective-permute-start.3 = (bf16[2,512,128]{2,1,0:T(8,128)(2,1)S(1)}, bf16[2,512,128]{2,1,0:T(8,128)(2,1)}, u32[]{:S(2)}, u32[]{:S(2)}) collective-permute-start(bf16[2,512,128]{2,1,0:T(8,128)(2,1)S(1)} %collective-permute-done.2.rest_5_), channel_id=1, source_target_pairs={{0,224},{32,0},{64,32},{96,64},{128,96},{160,128},{192,160},{224,1... | collective-permute-start | bytes 786440 | tf_op jit(solution)/shard_map/ppermute | solution.py:271
  56.1 2.1 %collective-permute-done.7.rest_2_ = bf16[2,512,128]{2,1,0:T(8,128)(2,1)S(1)} collective-permute-done((bf16[2,512,128]{2,1,0:T(8,128)(2,1)S(1)}, bf16[2,512,128]{2,1,0:T(8,128)(2,1)S(1)}, u32[]{:S(2)}, u32[]{:S(2)}) %collective-permute-start.7) | collective-permute-done | bytes 262176 | tf_op jit(solution)/shard_map/ppermute | solution.py:271
  58.2 1.9 %collective-permute-start.8 = (bf16[2,512,128]{2,1,0:T(8,128)(2,1)S(1)}, bf16[2,512,128]{2,1,0:T(8,128)(2,1)}, u32[]{:S(2)}, u32[]{:S(2)}) collective-permute-start(bf16[2,512,128]{2,1,0:T(8,128)(2,1)S(1)} %collective-permute-done.7.rest_2_), channel_id=1, source_target_pairs={{0,32},{32,64},{64,96},{96,128},{128,160},{160,192},{192,224},{224... | collective-permute-start | bytes 786440 | tf_op jit(solution)/shard_map/ppermute | solution.py:271
  60.1 0.1 pad_add_fusion.place
  60.2 0.0 copy-start
  60.2 0.0 collective-permute-done.3.rest_4_
  60.2 3.2 %all-to-all-done.mine = bf16[4,4,512,128]{3,2,1,0:T(8,128)(2,1)S(1)} async-done(((bf16[4,4,512,128]{3,2,1,0:T(8,128)(2,1)}), bf16[4,4,512,128]{3,2,1,0:T(8,128)(2,1)S(1)}, u32[]{:S(2)}, u32[]{:S(2)}) %all-to-all-start) | async-done | bytes 2097184 | tf_op jit(solution)/shard_map/all_to_all | solution.py:281
  63.4 3.0 %collective-permute-start.5 = (bf16[2,512,128]{2,1,0:T(8,128)(2,1)}, bf16[2,512,128]{2,1,0:T(8,128)(2,1)S(1)}, u32[]{:S(2)}, u32[]{:S(2)}) collective-permute-start(bf16[2,512,128]{2,1,0:T(8,128)(2,1)} %collective-permute-done.3.rest_4_), channel_id=1, source_target_pairs={{0,224},{32,0},{64,32},{96,64},{128,96},{160,128},{192,160},{224,1... | collective-permute-start | bytes 786440 | tf_op jit(solution)/shard_map/ppermute | solution.py:271
  66.4 7.0 %collective-permute-start.4 = (bf16[4,4,512,128]{3,2,1,0:T(8,128)(2,1)S(1)}, bf16[4,4,512,128]{3,2,1,0:T(8,128)(2,1)S(1)}, u32[]{:S(2)}, u32[]{:S(2)}) collective-permute-start(bf16[4,4,512,128]{3,2,1,0:T(8,128)(2,1)S(1)} %all-to-all-done.mine), channel_id=1, source_target_pairs={{0,1},{1,0},{2,3},{3,2},{4,5},{5,4},{6,7},{7,6},{8,9},{9,8},{10,11... | collective-permute-start | bytes 6291464 | tf_op jit(solution)/shard_map/ppermute | solution.py:271
  73.4 0.0 collective-permute-done.8.rest_3_
  73.4 3.8 %own_part.1 = (f32[512,256]{1,0:T(8,128)S(1)}, bf16[3584,256]{1,0:T(8,128)(2,1)S(1)}, bf16[512,512]{1,0:T(8,128)(2,1)S(1)}) custom-call(s32[3]{0:T(128)S(1)} %pad_add_fusion.place, bf16[4,4,512,128]{3,2,1,0:T(8,128)(2,1)S(1)} %all-to-all-done.mine, bf16[2,512,128]{2,1,0:T(8,128)(2,1)S(1)} %pad_maximum_fusion.block.rest_0_, ...), custom_call_target="tpu_custom_call" | custom-call | flops 34359738368 | bytes 8388608 | tf_op jit(solution)/shard_map/own_part/pallas_call | solution.py:210
  77.3 0.0 collective-permute-done.5.last
  77.3 0.0 collective-permute-done.4.others
  77.3 0.0 copy-done
  77.3 2.4 %final_part.1 = (f32[512,256]{1,0:T(8,128)S(1)}, f32[1,256]{1,0:T(1,128)S(1)}) custom-call(s32[3]{0:T(128)S(1)} %pad_add_fusion.place, s32[2,4]{1,0:T(2,128)S(1)} %bitcast.7, bf16[4,4,512,128]{3,2,1,0:T(8,128)(2,1)S(1)} %collective-permute-done.4.others, bf16[2,512,128]{2,1,0:T(8,128)(2,1)S(1)} %collective-permute-done.5.last, ...), custom_call_target="tpu_custom_call" | custom-call | flops 34359738368 | bytes 8388608 | tf_op jit(solution)/shard_map/final_part/pallas_call | solution.py:210
  79.7 16.1 %all_to_all.11 = f32[16,1,256]{2,1,0:T(1,128)S(1)} all-to-all(f32[16,1,256]{2,1,0:T(1,128)S(1)} %broadcast_in_dim.2), channel_id=1, replica_groups=mesh['zh'=2,'y'=8,'x'=4,'zl'=4,'core'=2] {'zh','y'}, dimensions={0} | all-to-all | bytes 32768 | tf_op jit(solution)/shard_map/all_to_all | solution.py:295
  95.9 0.8 maximum_convert_fusion
  (3 shorter events, 0.1 us)
Async XLA Ops:
  1.7 28.0 %collective-permute-start = (bf16[1,512,128]{2,1,0:T(8,128)(2,1)}, bf16[1,512,128]{2,1,0:T(8,128)(2,1)S(1)}, u32[]{:S(2)}, u32[]{:S(2)}) collective-permute-start(bf16[1,512,128]{2,1,0:T(8,128)(2,1)} %pack_tiles.1), channel_id=1, source_target_pairs={{0,256},{256,0},{1,257},{257,1},{2,258},{258,2},{3,259},{259,3},{4... | collective-permute-start | bytes 393224 | tf_op jit(solution)/shard_map/ppermute | solution.py:271
  30.6 12.3 %collective-permute-start.1 = (bf16[2,512,128]{2,1,0:T(8,128)(2,1)S(1)}, bf16[2,512,128]{2,1,0:T(8,128)(2,1)S(1)}, u32[]{:S(2)}, u32[]{:S(2)}) collective-permute-start(bf16[2,512,128]{2,1,0:T(8,128)(2,1)S(1)} %pad_maximum_fusion.block.rest_0_), channel_id=1, source_target_pairs={{0,224},{32,0},{64,32},{96,64},{128,96},{160,128},{192,160},{224,1... | collective-permute-start | bytes 786440 | tf_op jit(solution)/shard_map/ppermute | solution.py:271
  36.9 26.5 %all-to-all-start = ((bf16[4,4,512,128]{3,2,1,0:T(8,128)(2,1)}), bf16[4,4,512,128]{3,2,1,0:T(8,128)(2,1)S(1)}, u32[]{:S(2)}, u32[]{:S(2)}) async-start(bf16[4,4,512,128]{3,2,1,0:T(8,128)(2,1)} %line_copies.1), calls=%async_computation | async-start | bytes 4194304 | tf_op jit(solution)/shard_map/all_to_all | solution.py:281
  41.0 8.6 %collective-permute-start.6 = (bf16[2,512,128]{2,1,0:T(8,128)(2,1)S(1)}, bf16[2,512,128]{2,1,0:T(8,128)(2,1)S(1)}, u32[]{:S(2)}, u32[]{:S(2)}) collective-permute-start(bf16[2,512,128]{2,1,0:T(8,128)(2,1)S(1)} %both_again.1), channel_id=1, source_target_pairs={{0,32},{32,64},{64,96},{96,128},{128,160},{160,192},{192,224},{224... | collective-permute-start | bytes 786440 | tf_op jit(solution)/shard_map/ppermute | solution.py:271
  42.9 8.6 %collective-permute-start.2 = (bf16[2,512,128]{2,1,0:T(8,128)(2,1)S(1)}, bf16[2,512,128]{2,1,0:T(8,128)(2,1)S(1)}, u32[]{:S(2)}, u32[]{:S(2)}) collective-permute-start(bf16[2,512,128]{2,1,0:T(8,128)(2,1)S(1)} %collective-permute-done.1.rest_6_), channel_id=1, source_target_pairs={{0,224},{32,0},{64,32},{96,64},{128,96},{160,128},{192,160},{224,1... | collective-permute-start | bytes 786440 | tf_op jit(solution)/shard_map/ppermute | solution.py:271
  49.6 8.6 %collective-permute-start.7 = (bf16[2,512,128]{2,1,0:T(8,128)(2,1)S(1)}, bf16[2,512,128]{2,1,0:T(8,128)(2,1)S(1)}, u32[]{:S(2)}, u32[]{:S(2)}) collective-permute-start(bf16[2,512,128]{2,1,0:T(8,128)(2,1)S(1)} %collective-permute-done.6.rest_1_), channel_id=1, source_target_pairs={{0,32},{32,64},{64,96},{96,128},{128,160},{160,192},{192,224},{224... | collective-permute-start | bytes 786440 | tf_op jit(solution)/shard_map/ppermute | solution.py:271
  51.5 8.7 %collective-permute-start.3 = (bf16[2,512,128]{2,1,0:T(8,128)(2,1)S(1)}, bf16[2,512,128]{2,1,0:T(8,128)(2,1)}, u32[]{:S(2)}, u32[]{:S(2)}) collective-permute-start(bf16[2,512,128]{2,1,0:T(8,128)(2,1)S(1)} %collective-permute-done.2.rest_5_), channel_id=1, source_target_pairs={{0,224},{32,0},{64,32},{96,64},{128,96},{160,128},{192,160},{224,1... | collective-permute-start | bytes 786440 | tf_op jit(solution)/shard_map/ppermute | solution.py:271
  58.2 15.2 %collective-permute-start.8 = (bf16[2,512,128]{2,1,0:T(8,128)(2,1)S(1)}, bf16[2,512,128]{2,1,0:T(8,128)(2,1)}, u32[]{:S(2)}, u32[]{:S(2)}) collective-permute-start(bf16[2,512,128]{2,1,0:T(8,128)(2,1)S(1)} %collective-permute-done.7.rest_2_), channel_id=1, source_target_pairs={{0,32},{32,64},{64,96},{96,128},{128,160},{160,192},{192,224},{224... | collective-permute-start | bytes 786440 | tf_op jit(solution)/shard_map/ppermute | solution.py:271
  60.2 17.1 %copy-start = (s32[4,2]{0,1:T(2,128)S(1)}, s32[4,2]{0,1:T(2,128)}, u32[]{:S(2)}) copy-start(s32[4,2]{0,1:T(2,128)} %param.5) | copy-start | bytes 100
  63.4 13.8 %collective-permute-start.5 = (bf16[2,512,128]{2,1,0:T(8,128)(2,1)}, bf16[2,512,128]{2,1,0:T(8,128)(2,1)S(1)}, u32[]{:S(2)}, u32[]{:S(2)}) collective-permute-start(bf16[2,512,128]{2,1,0:T(8,128)(2,1)} %collective-permute-done.3.rest_4_), channel_id=1, source_target_pairs={{0,224},{32,0},{64,32},{96,64},{128,96},{160,128},{192,160},{224,1... | collective-permute-start | bytes 786440 | tf_op jit(solution)/shard_map/ppermute | solution.py:271
  66.4 10.9 %collective-permute-start.4 = (bf16[4,4,512,128]{3,2,1,0:T(8,128)(2,1)S(1)}, bf16[4,4,512,128]{3,2,1,0:T(8,128)(2,1)S(1)}, u32[]{:S(2)}, u32[]{:S(2)}) collective-permute-start(bf16[4,4,512,128]{3,2,1,0:T(8,128)(2,1)S(1)} %all-to-all-done.mine), channel_id=1, source_target_pairs={{0,1},{1,0},{2,3},{3,2},{4,5},{5,4},{6,7},{7,6},{8,9},{9,8},{10,11... | collective-permute-start | bytes 6291464 | tf_op jit(solution)/shard_map/ppermute | solution.py:271

commit v8 on v7

--- a/solution.py
+++ b/solution.py
@@ -28,12 +28,18 @@
 BLOCK = (RB * TILE, CB * TILE)
 
 
-def pack_kernel(pattern, matrix, out):
+def pack_kernel(pattern_in, matrix_in, out, pattern, matrix, sems):
+    pattern_copy = pltpu.make_async_copy(pattern_in, pattern, sems.at[0])
+    matrix_copy = pltpu.make_async_copy(matrix_in, matrix, sems.at[1])
+    matrix_copy.start()
+    pattern_copy.start()
     lane = lax.broadcasted_iota(jnp.int32, (HEAD, TILE), 1)
     row = lax.broadcasted_iota(jnp.int32, (HEAD, TILE), 0)
     signs = (row == 0) & (lane < SIGNS)
     for slot in range(CAP):
         out[0, slot * TILE:slot * TILE + HEAD, :] = jnp.ones((HEAD, TILE), jnp.bfloat16)
+    pattern_copy.wait()
+    matrix_copy.wait()
     count = jnp.int32(0)
     for t in range(RB * CB):
         r, s = divmod(t, CB)
@@ -58,8 +64,13 @@
     return pl.pallas_call(
         pack_kernel,
         out_shape=jax.ShapeDtypeStruct((1, PACK, TILE), jnp.bfloat16),
-        in_specs=[SMEM, VMEM],
+        in_specs=[pl.BlockSpec(memory_space=pl.ANY)] * 2,
         out_specs=VMEM,
+        scratch_shapes=[
+            pltpu.SMEM((CB, RB), jnp.int32),
+            pltpu.VMEM(BLOCK, jnp.bfloat16),
+            pltpu.SemaphoreType.DMA((2,)),
+        ],
         name="pack_tiles",
     )(pattern.T, matrix)
 

time: 97.2 us -> 97.2 us (level)
  no operation moved by 1% of the time
where the time goes in v8:
time: 97.2 us; the launch traced here: 96.6 us
  starting transfers between devices  45.3 us (47%)
  blocking collectives  32.6 us (34%)
  Pallas kernels  9.24 us (10%)
  waiting for transfers between devices  7.42 us (8%)
  other arithmetic  1.83 us (2%)
    ppermute x9, starting transfers between devices, shifted(): return lax.ppermute(array, axis, [(i, (i + by) % n) for i in range(n)])  41.3 us
    all_gather x1, blocking collectives, body(): line = lax.all_gather(packed, 'zl', tiled=True)  16.5 us
    all_to_all x1, blocking collectives, body(): lax.all_to_all(copies, BLK, 0, 0, tiled=True)  16.1 us
    pallas_call x2, Pallas kernels, kernel_call(): pl.pallas_call(kernel, out_shape=outs, in_specs=[SMEM] * len(smems) + [VM...  6.22 us
    ppermute x9, waiting for transfers between devices, shifted(): return lax.ppermute(array, axis, [(i, (i + by) % n) for i in range(n)])  4.22 us
    all_to_all x1, starting transfers between devices, body(): mine = lax.all_to_all(copies_of(line, nx), 'x', 0, 0)  4.04 us
    all_to_all x1, waiting for transfers between devices, body(): mine = lax.all_to_all(copies_of(line, nx), 'x', 0, 0)  3.2 us
  transfers between devices with their start and end apart: 10, of which 3 were waited for; matrix products, arithmetic and copies ran while one was open for 0% of the time, Pallas kernels for 5%

profile of v8, /device:TPU:1, one launch (start us, length us, event | category | flops | bytes accessed | tf_op | source)
XLA Modules:
  0.0 96.6 jit_solution(7092048640297913256)
XLA Ops:
  0.0 1.6 %pack_tiles.1 = bf16[1,512,128]{2,1,0:T(8,128)(2,1)} custom-call(s32[2,4]{1,0:T(2,128)} %bitcast.8, bf16[512,256]{1,0:T(8,128)(2,1)} %matrix_in.1), custom_call_target="tpu_custom_call" | custom-call | tf_op jit(solution)/shard_map/pack_tiles/pallas_call | solution.py:64
  1.6 11.5 %collective-permute-start = (bf16[1,512,128]{2,1,0:T(8,128)(2,1)}, bf16[1,512,128]{2,1,0:T(8,128)(2,1)S(1)}, u32[]{:S(2)}, u32[]{:S(2)}) collective-permute-start(bf16[1,512,128]{2,1,0:T(8,128)(2,1)} %pack_tiles.1), channel_id=1, source_target_pairs={{0,256},{256,0},{1,257},{257,1},{2,258},{258,2},{3,259},{259,3},{4... | collective-permute-start | bytes 393224 | tf_op jit(solution)/shard_map/ppermute | solution.py:282
  13.2 16.5 %all_gather.3.line = bf16[4,512,128]{2,1,0:T(8,128)(2,1)S(1)} all-gather(bf16[1,512,128]{2,1,0:T(8,128)(2,1)} %pack_tiles.1), channel_id=1, replica_groups=mesh['zh'=2,'y'=8,'x'=4,'zl'=4,'core'=2] {'zl'}, dimensions={0}, use_global_device_ids=true | all-gather | bytes 655360 | tf_op jit(solution)/shard_map/all_gather | solution.py:289
  29.7 0.0 collective-permute-done
  29.7 0.9 pad_maximum_fusion.block.rest_0_
  30.6 4.9 %collective-permute-start.1 = (bf16[2,512,128]{2,1,0:T(8,128)(2,1)S(1)}, bf16[2,512,128]{2,1,0:T(8,128)(2,1)S(1)}, u32[]{:S(2)}, u32[]{:S(2)}) collective-permute-start(bf16[2,512,128]{2,1,0:T(8,128)(2,1)S(1)} %pad_maximum_fusion.block.rest_0_), channel_id=1, source_target_pairs={{0,224},{32,0},{64,32},{96,64},{128,96},{160,128},{192,160},{224,1... | collective-permute-start | bytes 786440 | tf_op jit(solution)/shard_map/ppermute | solution.py:282
  35.5 1.4 %line_copies.1 = bf16[4,4,512,128]{3,2,1,0:T(8,128)(2,1)} custom-call(bf16[4,512,128]{2,1,0:T(8,128)(2,1)S(1)} %all_gather.3.line), custom_call_target="tpu_custom_call" | custom-call | tf_op jit(solution)/shard_map/line_copies/pallas_call | solution.py:201
  36.9 4.0 %all-to-all-start = ((bf16[4,4,512,128]{3,2,1,0:T(8,128)(2,1)}), bf16[4,4,512,128]{3,2,1,0:T(8,128)(2,1)S(1)}, u32[]{:S(2)}, u32[]{:S(2)}) async-start(bf16[4,4,512,128]{3,2,1,0:T(8,128)(2,1)} %line_copies.1), calls=%async_computation | async-start | bytes 4194304 | tf_op jit(solution)/shard_map/all_to_all | solution.py:292
  40.9 1.9 %collective-permute-start.6 = (bf16[2,512,128]{2,1,0:T(8,128)(2,1)S(1)}, bf16[2,512,128]{2,1,0:T(8,128)(2,1)S(1)}, u32[]{:S(2)}, u32[]{:S(2)}) collective-permute-start(bf16[2,512,128]{2,1,0:T(8,128)(2,1)S(1)} %both_again.1), channel_id=1, source_target_pairs={{0,32},{32,64},{64,96},{96,128},{128,160},{160,192},{192,224},{224... | collective-permute-start | bytes 786440 | tf_op jit(solution)/shard_map/ppermute | solution.py:282
  42.9 0.0 collective-permute-done.1.rest_6_
  42.9 4.6 %collective-permute-start.2 = (bf16[2,512,128]{2,1,0:T(8,128)(2,1)S(1)}, bf16[2,512,128]{2,1,0:T(8,128)(2,1)S(1)}, u32[]{:S(2)}, u32[]{:S(2)}) collective-permute-start(bf16[2,512,128]{2,1,0:T(8,128)(2,1)S(1)} %collective-permute-done.1.rest_6_), channel_id=1, source_target_pairs={{0,224},{32,0},{64,32},{96,64},{128,96},{160,128},{192,160},{224,1... | collective-permute-start | bytes 786440 | tf_op jit(solution)/shard_map/ppermute | solution.py:282
  47.5 2.1 %collective-permute-done.6.rest_1_ = bf16[2,512,128]{2,1,0:T(8,128)(2,1)S(1)} collective-permute-done((bf16[2,512,128]{2,1,0:T(8,128)(2,1)S(1)}, bf16[2,512,128]{2,1,0:T(8,128)(2,1)S(1)}, u32[]{:S(2)}, u32[]{:S(2)}) %collective-permute-start.6) | collective-permute-done | bytes 262176 | tf_op jit(solution)/shard_map/ppermute | solution.py:282
  49.6 1.9 %collective-permute-start.7 = (bf16[2,512,128]{2,1,0:T(8,128)(2,1)S(1)}, bf16[2,512,128]{2,1,0:T(8,128)(2,1)S(1)}, u32[]{:S(2)}, u32[]{:S(2)}) collective-permute-start(bf16[2,512,128]{2,1,0:T(8,128)(2,1)S(1)} %collective-permute-done.6.rest_1_), channel_id=1, source_target_pairs={{0,32},{32,64},{64,96},{96,128},{128,160},{160,192},{192,224},{224... | collective-permute-start | bytes 786440 | tf_op jit(solution)/shard_map/ppermute | solution.py:282
  51.5 0.0 collective-permute-done.2.rest_5_
  51.5 4.6 %collective-permute-start.3 = (bf16[2,512,128]{2,1,0:T(8,128)(2,1)S(1)}, bf16[2,512,128]{2,1,0:T(8,128)(2,1)}, u32[]{:S(2)}, u32[]{:S(2)}) collective-permute-start(bf16[2,512,128]{2,1,0:T(8,128)(2,1)S(1)} %collective-permute-done.2.rest_5_), channel_id=1, source_target_pairs={{0,224},{32,0},{64,32},{96,64},{128,96},{160,128},{192,160},{224,1... | collective-permute-start | bytes 786440 | tf_op jit(solution)/shard_map/ppermute | solution.py:282
  56.1 2.1 %collective-permute-done.7.rest_2_ = bf16[2,512,128]{2,1,0:T(8,128)(2,1)S(1)} collective-permute-done((bf16[2,512,128]{2,1,0:T(8,128)(2,1)S(1)}, bf16[2,512,128]{2,1,0:T(8,128)(2,1)S(1)}, u32[]{:S(2)}, u32[]{:S(2)}) %collective-permute-start.7) | collective-permute-done | bytes 262176 | tf_op jit(solution)/shard_map/ppermute | solution.py:282
  58.2 1.9 %collective-permute-start.8 = (bf16[2,512,128]{2,1,0:T(8,128)(2,1)S(1)}, bf16[2,512,128]{2,1,0:T(8,128)(2,1)}, u32[]{:S(2)}, u32[]{:S(2)}) collective-permute-start(bf16[2,512,128]{2,1,0:T(8,128)(2,1)S(1)} %collective-permute-done.7.rest_2_), channel_id=1, source_target_pairs={{0,32},{32,64},{64,96},{96,128},{128,160},{160,192},{192,224},{224... | collective-permute-start | bytes 786440 | tf_op jit(solution)/shard_map/ppermute | solution.py:282
  60.1 0.1 pad_add_fusion.place
  60.2 0.0 copy-start
  60.2 0.0 collective-permute-done.3.rest_4_
  60.2 3.2 %all-to-all-done.mine = bf16[4,4,512,128]{3,2,1,0:T(8,128)(2,1)S(1)} async-done(((bf16[4,4,512,128]{3,2,1,0:T(8,128)(2,1)}), bf16[4,4,512,128]{3,2,1,0:T(8,128)(2,1)S(1)}, u32[]{:S(2)}, u32[]{:S(2)}) %all-to-all-start) | async-done | bytes 2097184 | tf_op jit(solution)/shard_map/all_to_all | solution.py:292
  63.4 2.9 %collective-permute-start.5 = (bf16[2,512,128]{2,1,0:T(8,128)(2,1)}, bf16[2,512,128]{2,1,0:T(8,128)(2,1)S(1)}, u32[]{:S(2)}, u32[]{:S(2)}) collective-permute-start(bf16[2,512,128]{2,1,0:T(8,128)(2,1)} %collective-permute-done.3.rest_4_), channel_id=1, source_target_pairs={{0,224},{32,0},{64,32},{96,64},{128,96},{160,128},{192,160},{224,1... | collective-permute-start | bytes 786440 | tf_op jit(solution)/shard_map/ppermute | solution.py:282
  66.3 7.1 %collective-permute-start.4 = (bf16[4,4,512,128]{3,2,1,0:T(8,128)(2,1)S(1)}, bf16[4,4,512,128]{3,2,1,0:T(8,128)(2,1)S(1)}, u32[]{:S(2)}, u32[]{:S(2)}) collective-permute-start(bf16[4,4,512,128]{3,2,1,0:T(8,128)(2,1)S(1)} %all-to-all-done.mine), channel_id=1, source_target_pairs={{0,1},{1,0},{2,3},{3,2},{4,5},{5,4},{6,7},{7,6},{8,9},{9,8},{10,11... | collective-permute-start | bytes 6291464 | tf_op jit(solution)/shard_map/ppermute | solution.py:282
  73.4 0.0 collective-permute-done.8.rest_3_
  73.4 3.8 %own_part.1 = (f32[512,256]{1,0:T(8,128)S(1)}, bf16[3584,256]{1,0:T(8,128)(2,1)S(1)}, bf16[512,512]{1,0:T(8,128)(2,1)S(1)}) custom-call(s32[3]{0:T(128)S(1)} %pad_add_fusion.place, bf16[4,4,512,128]{3,2,1,0:T(8,128)(2,1)S(1)} %all-to-all-done.mine, bf16[2,512,128]{2,1,0:T(8,128)(2,1)S(1)} %pad_maximum_fusion.block.rest_0_, ...), custom_call_target="tpu_custom_call" | custom-call | flops 34359738368 | bytes 8388608 | tf_op jit(solution)/shard_map/own_part/pallas_call | solution.py:221
  77.2 0.0 collective-permute-done.5.last
  77.2 0.0 collective-permute-done.4.others
  77.3 0.0 copy-done
  77.3 2.4 %final_part.1 = (f32[512,256]{1,0:T(8,128)S(1)}, f32[1,256]{1,0:T(1,128)S(1)}) custom-call(s32[3]{0:T(128)S(1)} %pad_add_fusion.place, s32[2,4]{1,0:T(2,128)S(1)} %bitcast.7, bf16[4,4,512,128]{3,2,1,0:T(8,128)(2,1)S(1)} %collective-permute-done.4.others, bf16[2,512,128]{2,1,0:T(8,128)(2,1)S(1)} %collective-permute-done.5.last, ...), custom_call_target="tpu_custom_call" | custom-call | flops 34359738368 | bytes 8388608 | tf_op jit(solution)/shard_map/final_part/pallas_call | solution.py:221
  79.7 16.1 %all_to_all.11 = f32[16,1,256]{2,1,0:T(1,128)S(1)} all-to-all(f32[16,1,256]{2,1,0:T(1,128)S(1)} %broadcast_in_dim.2), channel_id=1, replica_groups=mesh['zh'=2,'y'=8,'x'=4,'zl'=4,'core'=2] {'zh','y'}, dimensions={0} | all-to-all | bytes 32768 | tf_op jit(solution)/shard_map/all_to_all | solution.py:306
  95.8 0.8 maximum_convert_fusion
  (3 shorter events, 0.1 us)
Async XLA Ops:
  1.6 28.0 %collective-permute-start = (bf16[1,512,128]{2,1,0:T(8,128)(2,1)}, bf16[1,512,128]{2,1,0:T(8,128)(2,1)S(1)}, u32[]{:S(2)}, u32[]{:S(2)}) collective-permute-start(bf16[1,512,128]{2,1,0:T(8,128)(2,1)} %pack_tiles.1), channel_id=1, source_target_pairs={{0,256},{256,0},{1,257},{257,1},{2,258},{258,2},{3,259},{259,3},{4... | collective-permute-start | bytes 393224 | tf_op jit(solution)/shard_map/ppermute | solution.py:282
  30.6 12.3 %collective-permute-start.1 = (bf16[2,512,128]{2,1,0:T(8,128)(2,1)S(1)}, bf16[2,512,128]{2,1,0:T(8,128)(2,1)S(1)}, u32[]{:S(2)}, u32[]{:S(2)}) collective-permute-start(bf16[2,512,128]{2,1,0:T(8,128)(2,1)S(1)} %pad_maximum_fusion.block.rest_0_), channel_id=1, source_target_pairs={{0,224},{32,0},{64,32},{96,64},{128,96},{160,128},{192,160},{224,1... | collective-permute-start | bytes 786440 | tf_op jit(solution)/shard_map/ppermute | solution.py:282
  36.9 26.5 %all-to-all-start = ((bf16[4,4,512,128]{3,2,1,0:T(8,128)(2,1)}), bf16[4,4,512,128]{3,2,1,0:T(8,128)(2,1)S(1)}, u32[]{:S(2)}, u32[]{:S(2)}) async-start(bf16[4,4,512,128]{3,2,1,0:T(8,128)(2,1)} %line_copies.1), calls=%async_computation | async-start | bytes 4194304 | tf_op jit(solution)/shard_map/all_to_all | solution.py:292
  40.9 8.6 %collective-permute-start.6 = (bf16[2,512,128]{2,1,0:T(8,128)(2,1)S(1)}, bf16[2,512,128]{2,1,0:T(8,128)(2,1)S(1)}, u32[]{:S(2)}, u32[]{:S(2)}) collective-permute-start(bf16[2,512,128]{2,1,0:T(8,128)(2,1)S(1)} %both_again.1), channel_id=1, source_target_pairs={{0,32},{32,64},{64,96},{96,128},{128,160},{160,192},{192,224},{224... | collective-permute-start | bytes 786440 | tf_op jit(solution)/shard_map/ppermute | solution.py:282
  42.9 8.6 %collective-permute-start.2 = (bf16[2,512,128]{2,1,0:T(8,128)(2,1)S(1)}, bf16[2,512,128]{2,1,0:T(8,128)(2,1)S(1)}, u32[]{:S(2)}, u32[]{:S(2)}) collective-permute-start(bf16[2,512,128]{2,1,0:T(8,128)(2,1)S(1)} %collective-permute-done.1.rest_6_), channel_id=1, source_target_pairs={{0,224},{32,0},{64,32},{96,64},{128,96},{160,128},{192,160},{224,1... | collective-permute-start | bytes 786440 | tf_op jit(solution)/shard_map/ppermute | solution.py:282
  49.6 8.6 %collective-permute-start.7 = (bf16[2,512,128]{2,1,0:T(8,128)(2,1)S(1)}, bf16[2,512,128]{2,1,0:T(8,128)(2,1)S(1)}, u32[]{:S(2)}, u32[]{:S(2)}) collective-permute-start(bf16[2,512,128]{2,1,0:T(8,128)(2,1)S(1)} %collective-permute-done.6.rest_1_), channel_id=1, source_target_pairs={{0,32},{32,64},{64,96},{96,128},{128,160},{160,192},{192,224},{224... | collective-permute-start | bytes 786440 | tf_op jit(solution)/shard_map/ppermute | solution.py:282
  51.5 8.7 %collective-permute-start.3 = (bf16[2,512,128]{2,1,0:T(8,128)(2,1)S(1)}, bf16[2,512,128]{2,1,0:T(8,128)(2,1)}, u32[]{:S(2)}, u32[]{:S(2)}) collective-permute-start(bf16[2,512,128]{2,1,0:T(8,128)(2,1)S(1)} %collective-permute-done.2.rest_5_), channel_id=1, source_target_pairs={{0,224},{32,0},{64,32},{96,64},{128,96},{160,128},{192,160},{224,1... | collective-permute-start | bytes 786440 | tf_op jit(solution)/shard_map/ppermute | solution.py:282
  58.2 15.2 %collective-permute-start.8 = (bf16[2,512,128]{2,1,0:T(8,128)(2,1)S(1)}, bf16[2,512,128]{2,1,0:T(8,128)(2,1)}, u32[]{:S(2)}, u32[]{:S(2)}) collective-permute-start(bf16[2,512,128]{2,1,0:T(8,128)(2,1)S(1)} %collective-permute-done.7.rest_2_), channel_id=1, source_target_pairs={{0,32},{32,64},{64,96},{96,128},{128,160},{160,192},{192,224},{224... | collective-permute-start | bytes 786440 | tf_op jit(solution)/shard_map/ppermute | solution.py:282
  60.2 17.1 %copy-start = (s32[4,2]{0,1:T(2,128)S(1)}, s32[4,2]{0,1:T(2,128)}, u32[]{:S(2)}) copy-start(s32[4,2]{0,1:T(2,128)} %param.5) | copy-start | bytes 100
  63.4 13.9 %collective-permute-start.5 = (bf16[2,512,128]{2,1,0:T(8,128)(2,1)}, bf16[2,512,128]{2,1,0:T(8,128)(2,1)S(1)}, u32[]{:S(2)}, u32[]{:S(2)}) collective-permute-start(bf16[2,512,128]{2,1,0:T(8,128)(2,1)} %collective-permute-done.3.rest_4_), channel_id=1, source_target_pairs={{0,224},{32,0},{64,32},{96,64},{128,96},{160,128},{192,160},{224,1... | collective-permute-start | bytes 786440 | tf_op jit(solution)/shard_map/ppermute | solution.py:282
  66.3 10.9 %collective-permute-start.4 = (bf16[4,4,512,128]{3,2,1,0:T(8,128)(2,1)S(1)}, bf16[4,4,512,128]{3,2,1,0:T(8,128)(2,1)S(1)}, u32[]{:S(2)}, u32[]{:S(2)}) collective-permute-start(bf16[4,4,512,128]{3,2,1,0:T(8,128)(2,1)S(1)} %all-to-all-done.mine), channel_id=1, source_target_pairs={{0,1},{1,0},{2,3},{3,2},{4,5},{5,4},{6,7},{7,6},{8,9},{9,8},{10,11... | collective-permute-start | bytes 6291464 | tf_op jit(solution)/shard_map/ppermute | solution.py:282

commit v9 on v8

--- a/solution.py
+++ b/solution.py
@@ -303,7 +303,7 @@
     start, spare, far_mine = own_part(ny, near, place, mine, [panels[j] for j in near])
     inflated, totals = final_part(ny, near, place, out_pattern, others, last, start, far_mine, spare)
     copies = jnp.broadcast_to(totals, (ny * lax.axis_size("zh"), totals.shape[1]))
-    column_totals = jnp.sum(lax.all_to_all(copies, BLK, 0, 0, tiled=True), axis=0, keepdims=True)
+    column_totals = jnp.sum(lax.all_to_all(copies, ("y", "zh"), 0, 0, tiled=True), axis=0, keepdims=True)
     scaled = inflated / column_totals * float(SIZES[0] * SIZES[1] * RB * TILE)
     return jnp.maximum(scaled - prune_level, 0.0).astype(jnp.bfloat16)
 

time: 97.2 us -> 97.4 us (level)
  no operation moved by 1% of the time
where the time goes in v9:
time: 97.4 us; the launch traced here: 96.9 us
  starting transfers between devices  45.1 us (46%)
  blocking collectives  33 us (34%)
  Pallas kernels  9.26 us (10%)
  waiting for transfers between devices  7.5 us (8%)
  other arithmetic  1.83 us (2%)
    ppermute x9, starting transfers between devices, shifted(): return lax.ppermute(array, axis, [(i, (i + by) % n) for i in range(n)])  41 us
    all_gather x1, blocking collectives, body(): line = lax.all_gather(packed, 'zl', tiled=True)  16.6 us
    all_to_all x1, blocking collectives, body(): lax.all_to_all(copies, ('y', 'zh'), 0, 0, tiled=True)  16.3 us
    pallas_call x2, Pallas kernels, kernel_call(): pl.pallas_call(kernel, out_shape=outs, in_specs=[SMEM] * len(smems) + [VM...  6.22 us
    ppermute x9, waiting for transfers between devices, shifted(): return lax.ppermute(array, axis, [(i, (i + by) % n) for i in range(n)])  4.22 us
    all_to_all x1, starting transfers between devices, body(): mine = lax.all_to_all(copies_of(line, nx), 'x', 0, 0)  4.06 us
    all_to_all x1, waiting for transfers between devices, body(): mine = lax.all_to_all(copies_of(line, nx), 'x', 0, 0)  3.28 us
  transfers between devices with their start and end apart: 10, of which 3 were waited for; matrix products, arithmetic and copies ran while one was open for 0% of the time, Pallas kernels for 5%

profile of v9, /device:TPU:1, one launch (start us, length us, event | category | flops | bytes accessed | tf_op | source)
XLA Modules:
  0.0 96.9 jit_solution(18349083941599199922)
XLA Ops:
  0.0 1.7 %pack_tiles.1 = bf16[1,512,128]{2,1,0:T(8,128)(2,1)} custom-call(s32[2,4]{1,0:T(2,128)} %bitcast.8, bf16[512,256]{1,0:T(8,128)(2,1)} %matrix_in.1), custom_call_target="tpu_custom_call" | custom-call | tf_op jit(solution)/shard_map/pack_tiles/pallas_call | solution.py:64
  1.7 11.5 %collective-permute-start = (bf16[1,512,128]{2,1,0:T(8,128)(2,1)}, bf16[1,512,128]{2,1,0:T(8,128)(2,1)S(1)}, u32[]{:S(2)}, u32[]{:S(2)}) collective-permute-start(bf16[1,512,128]{2,1,0:T(8,128)(2,1)} %pack_tiles.1), channel_id=1, source_target_pairs={{0,256},{256,0},{1,257},{257,1},{2,258},{258,2},{3,259},{259,3},{4... | collective-permute-start | bytes 393224 | tf_op jit(solution)/shard_map/ppermute | solution.py:282
  13.2 16.6 %all_gather.3.line = bf16[4,512,128]{2,1,0:T(8,128)(2,1)S(1)} all-gather(bf16[1,512,128]{2,1,0:T(8,128)(2,1)} %pack_tiles.1), channel_id=1, replica_groups=mesh['zh'=2,'y'=8,'x'=4,'zl'=4,'core'=2] {'zl'}, dimensions={0}, use_global_device_ids=true | all-gather | bytes 655360 | tf_op jit(solution)/shard_map/all_gather | solution.py:289
  29.8 0.0 collective-permute-done
  29.8 0.9 pad_maximum_fusion.block.rest_0_
  30.7 4.8 %collective-permute-start.1 = (bf16[2,512,128]{2,1,0:T(8,128)(2,1)S(1)}, bf16[2,512,128]{2,1,0:T(8,128)(2,1)S(1)}, u32[]{:S(2)}, u32[]{:S(2)}) collective-permute-start(bf16[2,512,128]{2,1,0:T(8,128)(2,1)S(1)} %pad_maximum_fusion.block.rest_0_), channel_id=1, source_target_pairs={{0,224},{32,0},{64,32},{96,64},{128,96},{160,128},{192,160},{224,1... | collective-permute-start | bytes 786440 | tf_op jit(solution)/shard_map/ppermute | solution.py:282
  35.5 1.4 %line_copies.1 = bf16[4,4,512,128]{3,2,1,0:T(8,128)(2,1)} custom-call(bf16[4,512,128]{2,1,0:T(8,128)(2,1)S(1)} %all_gather.3.line), custom_call_target="tpu_custom_call" | custom-call | tf_op jit(solution)/shard_map/line_copies/pallas_call | solution.py:201
  36.9 4.1 %all-to-all-start = ((bf16[4,4,512,128]{3,2,1,0:T(8,128)(2,1)}), bf16[4,4,512,128]{3,2,1,0:T(8,128)(2,1)S(1)}, u32[]{:S(2)}, u32[]{:S(2)}) async-start(bf16[4,4,512,128]{3,2,1,0:T(8,128)(2,1)} %line_copies.1), calls=%async_computation | async-start | bytes 4194304 | tf_op jit(solution)/shard_map/all_to_all | solution.py:292
  41.0 1.9 %collective-permute-start.6 = (bf16[2,512,128]{2,1,0:T(8,128)(2,1)S(1)}, bf16[2,512,128]{2,1,0:T(8,128)(2,1)S(1)}, u32[]{:S(2)}, u32[]{:S(2)}) collective-permute-start(bf16[2,512,128]{2,1,0:T(8,128)(2,1)S(1)} %both_again.1), channel_id=1, source_target_pairs={{0,32},{32,64},{64,96},{96,128},{128,160},{160,192},{192,224},{224... | collective-permute-start | bytes 786440 | tf_op jit(solution)/shard_map/ppermute | solution.py:282
  42.9 0.0 collective-permute-done.1.rest_6_
  42.9 4.6 %collective-permute-start.2 = (bf16[2,512,128]{2,1,0:T(8,128)(2,1)S(1)}, bf16[2,512,128]{2,1,0:T(8,128)(2,1)S(1)}, u32[]{:S(2)}, u32[]{:S(2)}) collective-permute-start(bf16[2,512,128]{2,1,0:T(8,128)(2,1)S(1)} %collective-permute-done.1.rest_6_), channel_id=1, source_target_pairs={{0,224},{32,0},{64,32},{96,64},{128,96},{160,128},{192,160},{224,1... | collective-permute-start | bytes 786440 | tf_op jit(solution)/shard_map/ppermute | solution.py:282
  47.5 2.1 %collective-permute-done.6.rest_1_ = bf16[2,512,128]{2,1,0:T(8,128)(2,1)S(1)} collective-permute-done((bf16[2,512,128]{2,1,0:T(8,128)(2,1)S(1)}, bf16[2,512,128]{2,1,0:T(8,128)(2,1)S(1)}, u32[]{:S(2)}, u32[]{:S(2)}) %collective-permute-start.6) | collective-permute-done | bytes 262176 | tf_op jit(solution)/shard_map/ppermute | solution.py:282
  49.6 1.9 %collective-permute-start.7 = (bf16[2,512,128]{2,1,0:T(8,128)(2,1)S(1)}, bf16[2,512,128]{2,1,0:T(8,128)(2,1)S(1)}, u32[]{:S(2)}, u32[]{:S(2)}) collective-permute-start(bf16[2,512,128]{2,1,0:T(8,128)(2,1)S(1)} %collective-permute-done.6.rest_1_), channel_id=1, source_target_pairs={{0,32},{32,64},{64,96},{96,128},{128,160},{160,192},{192,224},{224... | collective-permute-start | bytes 786440 | tf_op jit(solution)/shard_map/ppermute | solution.py:282
  51.5 0.0 collective-permute-done.2.rest_5_
  51.5 4.6 %collective-permute-start.3 = (bf16[2,512,128]{2,1,0:T(8,128)(2,1)S(1)}, bf16[2,512,128]{2,1,0:T(8,128)(2,1)}, u32[]{:S(2)}, u32[]{:S(2)}) collective-permute-start(bf16[2,512,128]{2,1,0:T(8,128)(2,1)S(1)} %collective-permute-done.2.rest_5_), channel_id=1, source_target_pairs={{0,224},{32,0},{64,32},{96,64},{128,96},{160,128},{192,160},{224,1... | collective-permute-start | bytes 786440 | tf_op jit(solution)/shard_map/ppermute | solution.py:282
  56.1 2.1 %collective-permute-done.7.rest_2_ = bf16[2,512,128]{2,1,0:T(8,128)(2,1)S(1)} collective-permute-done((bf16[2,512,128]{2,1,0:T(8,128)(2,1)S(1)}, bf16[2,512,128]{2,1,0:T(8,128)(2,1)S(1)}, u32[]{:S(2)}, u32[]{:S(2)}) %collective-permute-start.7) | collective-permute-done | bytes 262176 | tf_op jit(solution)/shard_map/ppermute | solution.py:282
  58.2 1.9 %collective-permute-start.8 = (bf16[2,512,128]{2,1,0:T(8,128)(2,1)S(1)}, bf16[2,512,128]{2,1,0:T(8,128)(2,1)}, u32[]{:S(2)}, u32[]{:S(2)}) collective-permute-start(bf16[2,512,128]{2,1,0:T(8,128)(2,1)S(1)} %collective-permute-done.7.rest_2_), channel_id=1, source_target_pairs={{0,32},{32,64},{64,96},{96,128},{128,160},{160,192},{192,224},{224... | collective-permute-start | bytes 786440 | tf_op jit(solution)/shard_map/ppermute | solution.py:282
  60.1 0.1 pad_add_fusion.place
  60.2 0.0 copy-start
  60.2 0.0 collective-permute-done.3.rest_4_
  60.2 3.3 %all-to-all-done.mine = bf16[4,4,512,128]{3,2,1,0:T(8,128)(2,1)S(1)} async-done(((bf16[4,4,512,128]{3,2,1,0:T(8,128)(2,1)}), bf16[4,4,512,128]{3,2,1,0:T(8,128)(2,1)S(1)}, u32[]{:S(2)}, u32[]{:S(2)}) %all-to-all-start) | async-done | bytes 2097184 | tf_op jit(solution)/shard_map/all_to_all | solution.py:292
  63.5 3.1 %collective-permute-start.5 = (bf16[2,512,128]{2,1,0:T(8,128)(2,1)}, bf16[2,512,128]{2,1,0:T(8,128)(2,1)S(1)}, u32[]{:S(2)}, u32[]{:S(2)}) collective-permute-start(bf16[2,512,128]{2,1,0:T(8,128)(2,1)} %collective-permute-done.3.rest_4_), channel_id=1, source_target_pairs={{0,224},{32,0},{64,32},{96,64},{128,96},{160,128},{192,160},{224,1... | collective-permute-start | bytes 786440 | tf_op jit(solution)/shard_map/ppermute | solution.py:282
  66.6 6.8 %collective-permute-start.4 = (bf16[4,4,512,128]{3,2,1,0:T(8,128)(2,1)S(1)}, bf16[4,4,512,128]{3,2,1,0:T(8,128)(2,1)S(1)}, u32[]{:S(2)}, u32[]{:S(2)}) collective-permute-start(bf16[4,4,512,128]{3,2,1,0:T(8,128)(2,1)S(1)} %all-to-all-done.mine), channel_id=1, source_target_pairs={{0,1},{1,0},{2,3},{3,2},{4,5},{5,4},{6,7},{7,6},{8,9},{9,8},{10,11... | collective-permute-start | bytes 6291464 | tf_op jit(solution)/shard_map/ppermute | solution.py:282
  73.4 0.0 collective-permute-done.8.rest_3_
  73.4 3.8 %own_part.1 = (f32[512,256]{1,0:T(8,128)S(1)}, bf16[3584,256]{1,0:T(8,128)(2,1)S(1)}, bf16[512,512]{1,0:T(8,128)(2,1)S(1)}) custom-call(s32[3]{0:T(128)S(1)} %pad_add_fusion.place, bf16[4,4,512,128]{3,2,1,0:T(8,128)(2,1)S(1)} %all-to-all-done.mine, bf16[2,512,128]{2,1,0:T(8,128)(2,1)S(1)} %pad_maximum_fusion.block.rest_0_, ...), custom_call_target="tpu_custom_call" | custom-call | flops 34359738368 | bytes 8388608 | tf_op jit(solution)/shard_map/own_part/pallas_call | solution.py:221
  77.2 0.0 collective-permute-done.5.last
  77.3 0.0 collective-permute-done.4.others
  77.3 0.0 copy-done
  77.3 2.4 %final_part.1 = (f32[512,256]{1,0:T(8,128)S(1)}, f32[1,256]{1,0:T(1,128)S(1)}) custom-call(s32[3]{0:T(128)S(1)} %pad_add_fusion.place, s32[2,4]{1,0:T(2,128)S(1)} %bitcast.7, bf16[4,4,512,128]{3,2,1,0:T(8,128)(2,1)S(1)} %collective-permute-done.4.others, bf16[2,512,128]{2,1,0:T(8,128)(2,1)S(1)} %collective-permute-done.5.last, ...), custom_call_target="tpu_custom_call" | custom-call | flops 34359738368 | bytes 8388608 | tf_op jit(solution)/shard_map/final_part/pallas_call | solution.py:221
  79.7 16.3 %all_to_all.11 = f32[16,1,256]{2,1,0:T(1,128)S(1)} all-to-all(f32[16,1,256]{2,1,0:T(1,128)S(1)} %broadcast_in_dim.2), channel_id=1, replica_groups=mesh['zh'=2,'y'=8,'x'=4,'zl'=4,'core'=2] {'y','zh'}, dimensions={0} | all-to-all | bytes 32768 | tf_op jit(solution)/shard_map/all_to_all | solution.py:306
  96.1 0.8 maximum_convert_fusion
  (3 shorter events, 0.1 us)
Async XLA Ops:
  1.7 28.1 %collective-permute-start = (bf16[1,512,128]{2,1,0:T(8,128)(2,1)}, bf16[1,512,128]{2,1,0:T(8,128)(2,1)S(1)}, u32[]{:S(2)}, u32[]{:S(2)}) collective-permute-start(bf16[1,512,128]{2,1,0:T(8,128)(2,1)} %pack_tiles.1), channel_id=1, source_target_pairs={{0,256},{256,0},{1,257},{257,1},{2,258},{258,2},{3,259},{259,3},{4... | collective-permute-start | bytes 393224 | tf_op jit(solution)/shard_map/ppermute | solution.py:282
  30.7 12.2 %collective-permute-start.1 = (bf16[2,512,128]{2,1,0:T(8,128)(2,1)S(1)}, bf16[2,512,128]{2,1,0:T(8,128)(2,1)S(1)}, u32[]{:S(2)}, u32[]{:S(2)}) collective-permute-start(bf16[2,512,128]{2,1,0:T(8,128)(2,1)S(1)} %pad_maximum_fusion.block.rest_0_), channel_id=1, source_target_pairs={{0,224},{32,0},{64,32},{96,64},{128,96},{160,128},{192,160},{224,1... | collective-permute-start | bytes 786440 | tf_op jit(solution)/shard_map/ppermute | solution.py:282
  36.9 26.6 %all-to-all-start = ((bf16[4,4,512,128]{3,2,1,0:T(8,128)(2,1)}), bf16[4,4,512,128]{3,2,1,0:T(8,128)(2,1)S(1)}, u32[]{:S(2)}, u32[]{:S(2)}) async-start(bf16[4,4,512,128]{3,2,1,0:T(8,128)(2,1)} %line_copies.1), calls=%async_computation | async-start | bytes 4194304 | tf_op jit(solution)/shard_map/all_to_all | solution.py:292
  41.0 8.6 %collective-permute-start.6 = (bf16[2,512,128]{2,1,0:T(8,128)(2,1)S(1)}, bf16[2,512,128]{2,1,0:T(8,128)(2,1)S(1)}, u32[]{:S(2)}, u32[]{:S(2)}) collective-permute-start(bf16[2,512,128]{2,1,0:T(8,128)(2,1)S(1)} %both_again.1), channel_id=1, source_target_pairs={{0,32},{32,64},{64,96},{96,128},{128,160},{160,192},{192,224},{224... | collective-permute-start | bytes 786440 | tf_op jit(solution)/shard_map/ppermute | solution.py:282
  42.9 8.6 %collective-permute-start.2 = (bf16[2,512,128]{2,1,0:T(8,128)(2,1)S(1)}, bf16[2,512,128]{2,1,0:T(8,128)(2,1)S(1)}, u32[]{:S(2)}, u32[]{:S(2)}) collective-permute-start(bf16[2,512,128]{2,1,0:T(8,128)(2,1)S(1)} %collective-permute-done.1.rest_6_), channel_id=1, source_target_pairs={{0,224},{32,0},{64,32},{96,64},{128,96},{160,128},{192,160},{224,1... | collective-permute-start | bytes 786440 | tf_op jit(solution)/shard_map/ppermute | solution.py:282
  49.6 8.6 %collective-permute-start.7 = (bf16[2,512,128]{2,1,0:T(8,128)(2,1)S(1)}, bf16[2,512,128]{2,1,0:T(8,128)(2,1)S(1)}, u32[]{:S(2)}, u32[]{:S(2)}) collective-permute-start(bf16[2,512,128]{2,1,0:T(8,128)(2,1)S(1)} %collective-permute-done.6.rest_1_), channel_id=1, source_target_pairs={{0,32},{32,64},{64,96},{96,128},{128,160},{160,192},{192,224},{224... | collective-permute-start | bytes 786440 | tf_op jit(solution)/shard_map/ppermute | solution.py:282
  51.5 8.7 %collective-permute-start.3 = (bf16[2,512,128]{2,1,0:T(8,128)(2,1)S(1)}, bf16[2,512,128]{2,1,0:T(8,128)(2,1)}, u32[]{:S(2)}, u32[]{:S(2)}) collective-permute-start(bf16[2,512,128]{2,1,0:T(8,128)(2,1)S(1)} %collective-permute-done.2.rest_5_), channel_id=1, source_target_pairs={{0,224},{32,0},{64,32},{96,64},{128,96},{160,128},{192,160},{224,1... | collective-permute-start | bytes 786440 | tf_op jit(solution)/shard_map/ppermute | solution.py:282
  58.2 15.2 %collective-permute-start.8 = (bf16[2,512,128]{2,1,0:T(8,128)(2,1)S(1)}, bf16[2,512,128]{2,1,0:T(8,128)(2,1)}, u32[]{:S(2)}, u32[]{:S(2)}) collective-permute-start(bf16[2,512,128]{2,1,0:T(8,128)(2,1)S(1)} %collective-permute-done.7.rest_2_), channel_id=1, source_target_pairs={{0,32},{32,64},{64,96},{96,128},{128,160},{160,192},{192,224},{224... | collective-permute-start | bytes 786440 | tf_op jit(solution)/shard_map/ppermute | solution.py:282
  60.2 17.1 %copy-start = (s32[4,2]{0,1:T(2,128)S(1)}, s32[4,2]{0,1:T(2,128)}, u32[]{:S(2)}) copy-start(s32[4,2]{0,1:T(2,128)} %param.5) | copy-start | bytes 100
  63.5 13.8 %collective-permute-start.5 = (bf16[2,512,128]{2,1,0:T(8,128)(2,1)}, bf16[2,512,128]{2,1,0:T(8,128)(2,1)S(1)}, u32[]{:S(2)}, u32[]{:S(2)}) collective-permute-start(bf16[2,512,128]{2,1,0:T(8,128)(2,1)} %collective-permute-done.3.rest_4_), channel_id=1, source_target_pairs={{0,224},{32,0},{64,32},{96,64},{128,96},{160,128},{192,160},{224,1... | collective-permute-start | bytes 786440 | tf_op jit(solution)/shard_map/ppermute | solution.py:282
  66.6 10.7 %collective-permute-start.4 = (bf16[4,4,512,128]{3,2,1,0:T(8,128)(2,1)S(1)}, bf16[4,4,512,128]{3,2,1,0:T(8,128)(2,1)S(1)}, u32[]{:S(2)}, u32[]{:S(2)}) collective-permute-start(bf16[4,4,512,128]{3,2,1,0:T(8,128)(2,1)S(1)} %all-to-all-done.mine), channel_id=1, source_target_pairs={{0,1},{1,0},{2,3},{3,2},{4,5},{5,4},{6,7},{7,6},{8,9},{9,8},{10,11... | collective-permute-start | bytes 6291464 | tf_op jit(solution)/shard_map/ppermute | solution.py:282
